TPU v7x, 32 devices: a whole 2x2x4 slice. The times are simulated.
32 devices in a mesh: dp: 2 (over core), row: 4 (over y, x), col: 4 (over z).
Axes of the slice: x: 2, y: 2, z: 4, core: 2. Of those that a mesh axis runs over, the one named last changes fastest.
Arguments:
- tokens: bfloat16 [2, 64, 64, 768], P('dp', 'row', 'col'), may hold values from -8 to 8
- ln1_gain: bfloat16 [768], replicated, may hold values from 0.5 to 1.5
- ln1_bias: bfloat16 [768], replicated, may hold values from -1 to 1
- qkv_weight: bfloat16 [768, 2304], P('dp', ('row', 'col')), may hold values from -1 to 1
- query_bias: bfloat16 [768], replicated, may hold values from -1 to 1
- value_bias: bfloat16 [768], replicated, may hold values from -1 to 1
- rel_rows: bfloat16 [27, 64], replicated, may hold values from -0.75 to 0.75
- rel_cols: bfloat16 [27, 64], replicated, may hold values from -0.75 to 0.75
- proj_weight: bfloat16 [768, 768], P('dp', ('row', 'col')), may hold values from -0.875 to 0.875
- proj_bias: bfloat16 [768], replicated, may hold values from -1 to 1
- ln2_gain: bfloat16 [768], replicated, may hold values from 0.5 to 1.5
- ln2_bias: bfloat16 [768], replicated, may hold values from -1 to 1
- fc1_weight: bfloat16 [768, 3072], P('dp', ('row', 'col')), may hold values from -1 to 1
- fc1_bias: bfloat16 [3072], replicated, may hold values from -1 to 1
- fc2_weight: bfloat16 [3072, 768], P('dp', ('row', 'col')), may hold values from -0.109375 to 0.109375
- fc2_bias: bfloat16 [768], replicated, may hold values from -1 to 1
- cotangent: bfloat16 [2, 64, 64, 768], P('dp', 'row', 'col'), may hold values from -6 to 6
Outputs:
- output: bfloat16 [2, 64, 64, 768], P('dp', 'row', 'col')
- input_grad: bfloat16 [2, 64, 64, 768], P('dp', 'row', 'col')
- grad_ln1_gain: float32 [768], replicated
- grad_ln1_bias: float32 [768], replicated
- grad_qkv_weight: float32 [768, 2304], P('dp', ('row', 'col'))
- grad_query_bias: float32 [768], replicated
- grad_value_bias: float32 [768], replicated
- grad_rel_rows: float32 [27, 64], replicated
- grad_rel_cols: float32 [27, 64], replicated
- grad_proj_weight: float32 [768, 768], P('dp', ('row', 'col'))
- grad_proj_bias: float32 [768], replicated
- grad_ln2_gain: float32 [768], replicated
- grad_ln2_bias: float32 [768], replicated
- grad_fc1_weight: float32 [768, 3072], P('dp', ('row', 'col'))
- grad_fc1_bias: float32 [3072], replicated
- grad_fc2_weight: float32 [3072, 768], P('dp', ('row', 'col'))
- grad_fc2_bias: float32 [768], replicated
- statistics: float32 [2, 5], P('dp')
All inputs are finite; a program needn't handle non-finite values.
Results may differ from a plain program's by a relative error of at most 0.019.
Values may be sent and summed in bfloat16 or wider, within the bound.
A program may use at most 192 MiB of HBM per device.

v0:
```python
import jax
import jax.numpy as jnp
from jax import lax
from jax.sharding import PartitionSpec as P

HEADS = 12
HEAD = 64
WIN = 14


NORM_EPSILON = 1e-06
TOP_PRECISION = lax.Precision.HIGHEST


def extended(block, sides, width):
    for axis, dim in sides:
        count = lax.axis_size(axis)
        forward = [(i, i + 1) for i in range(count - 1)]
        backward = [(target, source) for source, target in forward]
        low = lax.ppermute(
            lax.slice_in_dim(block, block.shape[dim] - width, None, axis=dim), axis, forward
        )
        high = lax.ppermute(lax.slice_in_dim(block, 0, width, axis=dim), axis, backward)
        block = jnp.concatenate([low, block, high], axis=dim)
    return block


def plan_axis(tile_len, tile_count):
    window_count = (tile_len * tile_count + WIN - 1) // WIN
    touched = []
    for t in range(tile_count):
        touched.append(
            [
                WIN * j - tile_len * t
                for j in range(window_count)
                if WIN * j < tile_len * (t + 1) and WIN * j + WIN > tile_len * t
            ]
        )
    slot_count = max((len(p) for p in touched))
    reach = max((max(-s, s + WIN - tile_len) for p in touched for s in p))
    slot_starts = [[p[a] for p in touched] for a in range(slot_count)]
    slot_valid = [[1.0 for p in touched] for a in range(slot_count)]
    extra_cells = window_count * WIN - tile_len * tile_count
    own_ends = [tile_len + (extra_cells if t == tile_count - 1 else 0) for t in range(tile_count)]
    return (slot_starts, slot_valid, reach, own_ends)


def select_entry(entries, index, kind):
    table = jnp.asarray(entries, kind)
    return jnp.sum(
        jnp.where(jnp.arange(len(entries), dtype=jnp.int32) == index, table, jnp.zeros((), kind))
    )


def norm_forward(values, gain_vec, bias_vec):
    center = values - jnp.mean(values, -1, keepdims=True)
    inverse_std = lax.rsqrt(jnp.mean(center * center, -1, keepdims=True) + NORM_EPSILON)
    normal_x = center * inverse_std
    return (normal_x * gain_vec + bias_vec, normal_x, inverse_std)


def norm_backward(grad_in, normal_x, inverse_std, gain_vec):
    scaled = grad_in * gain_vec
    grad_values = inverse_std * (
        scaled
        - jnp.mean(scaled, -1, keepdims=True)
        - normal_x * jnp.mean(scaled * normal_x, -1, keepdims=True)
    )
    flat_axes = tuple(range(grad_in.ndim - 1))
    return (grad_values, jnp.sum(grad_in * normal_x, flat_axes), jnp.sum(grad_in, flat_axes))


def outer_sum(left, right):
    return lax.dot_general(
        left, right, (((0,), (0,)), ((), ())), preferred_element_type=jnp.float32
    )


def times_transposed(left, right):
    return lax.dot_general(
        left, right, (((1,), (1,)), ((), ())), preferred_element_type=jnp.float32
    )


def relative_onehot():
    offsets = jnp.arange(WIN)[:, None] - jnp.arange(WIN)[None, :] + (WIN - 1)
    return (offsets[:, :, None] == jnp.arange(2 * WIN - 1)[None, None, :]).astype(jnp.float32)


def own_line(start, rim_width, end_rel):
    positions = start + jnp.arange(WIN, dtype=jnp.int32)
    return ((positions >= rim_width) & (positions < rim_width + end_rel)).astype(jnp.float32)


def cut_windows(padded_field, row_starts, col_starts):
    batch_size, model_width = (padded_field.shape[0], padded_field.shape[3])
    zero_index = jnp.zeros((), jnp.int32)
    pieces = [
        lax.dynamic_slice(
            padded_field, (zero_index, r, c, zero_index), (batch_size, WIN, WIN, model_width)
        )
        for r in row_starts
        for c in col_starts
    ]
    return jnp.stack(pieces, 0).reshape(len(pieces) * batch_size, WIN * WIN, model_width)


def place_windows(window_rows, row_starts, col_starts, like_field):
    batch_size, model_width = (like_field.shape[0], like_field.shape[3])
    grouped = window_rows.reshape(-1, batch_size, WIN, WIN, model_width)
    padded_field = jnp.zeros_like(like_field)
    zero_index = jnp.zeros((), jnp.int32)
    slot_id = 0
    for r in row_starts:
        for c in col_starts:
            corner = (zero_index, r, c, zero_index)
            current = lax.dynamic_slice(padded_field, corner, (batch_size, WIN, WIN, model_width))
            padded_field = lax.dynamic_update_slice(
                padded_field, current + grouped[slot_id], corner
            )
            slot_id += 1
    return padded_field


def window_scores(queries, keys_w, table_rows, table_cols):
    head_count, head_size = (queries.shape[1], queries.shape[2])
    grid_q = queries.astype(jnp.float32).reshape(WIN, WIN, head_count, head_size)
    rows_term = jnp.einsum("yxhc,ykc->hyxk", grid_q, table_rows, precision=TOP_PRECISION)
    cols_term = jnp.einsum("yxhc,xlc->hyxl", grid_q, table_cols, precision=TOP_PRECISION)
    base = jnp.einsum(
        "ihc,jhc->hij", queries, keys_w, preferred_element_type=jnp.float32
    ) * head_size ** (-0.5)
    joined = (
        base.reshape(head_count, WIN, WIN, WIN, WIN)
        + rows_term[:, :, :, :, None]
        + cols_term[:, :, :, None, :]
    )
    return (joined.reshape(head_count, WIN * WIN, WIN * WIN), grid_q)


def attend(inputs, table_rows, table_cols):
    queries, keys_w, values = inputs
    scores, grid_q = window_scores(queries, keys_w, table_rows, table_cols)
    row_max = jnp.max(scores, -1, keepdims=True)
    exps_raw = jnp.exp(scores - row_max)
    row_total = jnp.sum(exps_raw, -1, keepdims=True)
    softmax_out = exps_raw / row_total
    log_total = (row_max + jnp.log(row_total))[:, :, 0]
    mixed_out = jnp.einsum(
        "hij,jhc->ihc", softmax_out.astype(jnp.bfloat16), values, preferred_element_type=jnp.float32
    )
    return (mixed_out.astype(jnp.bfloat16), log_total)


def attend_back(carried, inputs, table_rows, table_cols):
    queries, keys_w, values, log_total, grad_mixed, own_query = inputs
    head_count, head_size = (queries.shape[1], queries.shape[2])
    score_scale = head_size ** (-0.5)
    scores, grid_q = window_scores(queries, keys_w, table_rows, table_cols)
    softmax_out = jnp.exp(scores - log_total[:, :, None])
    softmax_low = softmax_out.astype(jnp.bfloat16)
    grad_values = jnp.einsum(
        "hij,ihc->jhc", softmax_low, grad_mixed, preferred_element_type=jnp.float32
    )
    grad_probs = jnp.einsum("ihc,jhc->hij", grad_mixed, values, preferred_element_type=jnp.float32)
    inner_total = jnp.sum(softmax_out * grad_probs, -1, keepdims=True)
    grad_scores = (softmax_out * (grad_probs - inner_total)).astype(jnp.bfloat16)
    grad_five = grad_scores.reshape(head_count, WIN, WIN, WIN, WIN)
    rows_sum = jnp.sum(grad_five, axis=4, dtype=jnp.float32)
    cols_sum = jnp.sum(grad_five, axis=3, dtype=jnp.float32)
    extra_rows = jnp.einsum("hyxk,ykc->yxhc", rows_sum, table_rows, precision=TOP_PRECISION)
    extra_cols = jnp.einsum("hyxl,xlc->yxhc", cols_sum, table_cols, precision=TOP_PRECISION)
    grad_queries = (
        jnp.einsum("hij,jhc->ihc", grad_scores, keys_w, preferred_element_type=jnp.float32)
        * score_scale
    )
    grad_queries = grad_queries + (extra_rows + extra_cols).reshape(
        WIN * WIN, head_count, head_size
    )
    grad_keys = (
        jnp.einsum("hij,ihc->jhc", grad_scores, queries, preferred_element_type=jnp.float32)
        * score_scale
    )
    query_mask = own_query.reshape(WIN, WIN)[None, :, :, None]
    table_grad_rows = carried[0] + jnp.einsum(
        "hyxk,yxhc->ykc", rows_sum * query_mask, grid_q, precision=TOP_PRECISION
    )
    table_grad_cols = carried[1] + jnp.einsum(
        "hyxl,yxhc->xlc", cols_sum * query_mask, grid_q, precision=TOP_PRECISION
    )
    flat_width = head_count * head_size
    joined = jnp.concatenate(
        [
            grad_queries.astype(jnp.bfloat16).reshape(WIN * WIN, flat_width),
            grad_keys.astype(jnp.bfloat16).reshape(WIN * WIN, flat_width),
            grad_values.astype(jnp.bfloat16).reshape(WIN * WIN, flat_width),
        ],
        -1,
    )
    return ((table_grad_rows, table_grad_cols), joined)


def reduce_tiles(parts):
    return (
        lax.psum_scatter(
            parts[0].astype(jnp.bfloat16), ("row", "col"), scatter_dimension=1, tiled=True
        ).astype(jnp.float32),
        lax.psum_scatter(
            parts[1].astype(jnp.bfloat16), ("row", "col"), scatter_dimension=1, tiled=True
        ).astype(jnp.float32),
        lax.psum_scatter(
            parts[2].astype(jnp.bfloat16), ("row", "col"), scatter_dimension=1, tiled=True
        ).astype(jnp.float32),
        lax.psum_scatter(
            parts[3].astype(jnp.bfloat16), ("row", "col"), scatter_dimension=1, tiled=True
        ).astype(jnp.float32),
    )


def reduce_images(parts):
    return (
        lax.psum_scatter(
            parts[0].astype(jnp.bfloat16), "dp", scatter_dimension=0, tiled=True
        ).astype(jnp.float32),
        lax.psum_scatter(
            parts[1].astype(jnp.bfloat16), "dp", scatter_dimension=0, tiled=True
        ).astype(jnp.float32),
        lax.psum_scatter(
            parts[2].astype(jnp.bfloat16), "dp", scatter_dimension=0, tiled=True
        ).astype(jnp.float32),
        lax.psum_scatter(
            parts[3].astype(jnp.bfloat16), "dp", scatter_dimension=0, tiled=True
        ).astype(jnp.float32),
    )


def on_device(
    tokens,
    ln1_gain,
    ln1_bias,
    qkv_weight,
    query_bias,
    value_bias,
    rel_rows,
    rel_cols,
    proj_weight,
    proj_bias,
    ln2_gain,
    ln2_bias,
    fc1_weight,
    fc1_bias,
    fc2_weight,
    fc2_bias,
    cotangent,
):
    batch_size, tile_rows, tile_cols, model_width = tokens.shape
    head_count = HEADS
    head_size = HEAD
    window_tokens = WIN * WIN
    cols_full = (
        lax.all_gather(qkv_weight, ("row", "col"), axis=1, tiled=True),
        lax.all_gather(proj_weight, ("row", "col"), axis=1, tiled=True),
        lax.all_gather(fc1_weight, ("row", "col"), axis=1, tiled=True),
        lax.all_gather(fc2_weight, ("row", "col"), axis=1, tiled=True),
    )
    w_qkv, w_proj, w_up, w_down = (
        lax.all_gather(cols_full[0], "dp", axis=0, tiled=True),
        lax.all_gather(cols_full[1], "dp", axis=0, tiled=True),
        lax.all_gather(cols_full[2], "dp", axis=0, tiled=True),
        lax.all_gather(cols_full[3], "dp", axis=0, tiled=True),
    )
    gain_one = ln1_gain.astype(jnp.float32)
    bias_one = ln1_bias.astype(jnp.float32)
    gain_two = ln2_gain.astype(jnp.float32)
    bias_two = ln2_bias.astype(jnp.float32)
    query_add = query_bias.astype(jnp.float32)
    value_add = value_bias.astype(jnp.float32)
    proj_add = proj_bias.astype(jnp.float32)
    up_add = fc1_bias.astype(jnp.float32)
    down_add = fc2_bias.astype(jnp.float32)
    onehot_table = relative_onehot()
    table_rows = jnp.einsum(
        "ikr,rc->ikc", onehot_table, rel_rows.astype(jnp.float32), precision=TOP_PRECISION
    )
    table_cols = jnp.einsum(
        "ikr,rc->ikc", onehot_table, rel_cols.astype(jnp.float32), precision=TOP_PRECISION
    )
    row_plan = plan_axis(tile_rows, lax.axis_size("row"))
    col_plan = plan_axis(tile_cols, lax.axis_size("col"))
    rim_width = max(row_plan[2], col_plan[2], 1)
    row_index = lax.axis_index("row")
    col_index = lax.axis_index("col")
    row_starts = [select_entry(s, row_index, jnp.int32) + rim_width for s in row_plan[0]]
    col_starts = [select_entry(s, col_index, jnp.int32) + rim_width for s in col_plan[0]]
    row_valid = [select_entry(v, row_index, jnp.float32) for v in row_plan[1]]
    col_valid = [select_entry(v, col_index, jnp.float32) for v in col_plan[1]]
    row_end = select_entry(row_plan[3], row_index, jnp.int32)
    col_end = select_entry(col_plan[3], col_index, jnp.int32)
    slot_mask = jnp.stack([a * b for a in row_valid for b in col_valid])
    window_mask = jnp.repeat(slot_mask, batch_size).astype(jnp.bfloat16)[:, None, None]
    own_slots = []
    for a in range(len(row_starts)):
        for b in range(len(col_starts)):
            line_rows = own_line(row_starts[a], rim_width, row_end)
            line_cols = own_line(col_starts[b], rim_width, col_end)
            own_slots.append(
                (row_valid[a] * col_valid[b] * line_rows[:, None] * line_cols[None, :]).reshape(
                    window_tokens
                )
            )
    own_token = jnp.repeat(jnp.stack(own_slots, 0), batch_size, axis=0)
    own_low = own_token.reshape(-1).astype(jnp.bfloat16)[:, None]
    tokens_f = tokens.astype(jnp.float32)
    normed, normal_one, inverse_one = norm_forward(tokens_f, gain_one, bias_one)
    normed_low = normed.astype(jnp.bfloat16)
    padded_field = extended(normed_low, (("row", 1), ("col", 2)), rim_width)
    windows = cut_windows(padded_field, row_starts, col_starts)
    window_count = windows.shape[0]
    window_flat = windows.reshape(-1, model_width)
    packed = jnp.dot(window_flat, w_qkv, preferred_element_type=jnp.float32)
    queries = (
        (packed[:, :model_width] + query_add)
        .astype(jnp.bfloat16)
        .reshape(window_count, window_tokens, head_count, head_size)
    )
    keys_w = (
        packed[:, model_width : 2 * model_width]
        .astype(jnp.bfloat16)
        .reshape(window_count, window_tokens, head_count, head_size)
    )
    values = (
        (packed[:, 2 * model_width :] + value_add)
        .astype(jnp.bfloat16)
        .reshape(window_count, window_tokens, head_count, head_size)
    )
    mixed_out, log_total = lax.map(
        lambda inputs: attend(inputs, table_rows, table_cols), (queries, keys_w, values)
    )
    mixed_flat = mixed_out.reshape(-1, model_width)
    projected = (jnp.dot(mixed_flat, w_proj, preferred_element_type=jnp.float32) + proj_add).astype(
        jnp.bfloat16
    )
    projected = projected.reshape(window_count, window_tokens, model_width) * window_mask
    returned = place_windows(projected, row_starts, col_starts, padded_field)
    attended = returned[:, rim_width : rim_width + tile_rows, rim_width : rim_width + tile_cols]
    attended_f = attended.astype(jnp.float32)
    middle = tokens_f + attended_f
    normed_two, normal_two, inverse_two = norm_forward(middle, gain_two, bias_two)
    normed_two_low = normed_two.astype(jnp.bfloat16).reshape(-1, model_width)
    upper = jnp.dot(normed_two_low, w_up, preferred_element_type=jnp.float32) + up_add
    activated = jax.nn.gelu(upper, approximate=False).astype(jnp.bfloat16)
    branch = (jnp.dot(activated, w_down, preferred_element_type=jnp.float32) + down_add).reshape(
        tokens.shape
    )
    result_f = middle + branch
    output = result_f.astype(jnp.bfloat16)
    squares = jnp.stack(
        [jnp.sum(v * v, (1, 2, 3)) for v in (tokens_f, middle, result_f, attended_f, branch)], 1
    )
    square_totals = lax.psum(squares, ("row", "col"))
    entry_count = tile_rows * tile_cols * lax.axis_size("row") * lax.axis_size("col") * model_width
    statistics = jnp.sqrt(square_totals / entry_count)
    grad_branch = cotangent.reshape(-1, model_width)
    grad_down_w = outer_sum(activated, grad_branch)
    grad_down_bias = jnp.sum(grad_branch, 0, dtype=jnp.float32)
    grad_act = times_transposed(grad_branch, w_down)
    normal_cdf = 0.5 * (1.0 + lax.erf(upper * 0.7071067811865476))
    normal_pdf = jnp.exp(-0.5 * upper * upper) * 0.3989422804014327
    grad_upper = (grad_act * (normal_cdf + upper * normal_pdf)).astype(jnp.bfloat16)
    grad_up_w = outer_sum(normed_two_low, grad_upper)
    grad_up_bias = jnp.sum(grad_upper, 0, dtype=jnp.float32)
    grad_normed_two = times_transposed(grad_upper, w_up).reshape(tokens.shape)
    grad_middle_ln, grad_gain_two, grad_bias_two = norm_backward(
        grad_normed_two, normal_two, inverse_two, gain_two
    )
    grad_middle = cotangent.astype(jnp.float32) + grad_middle_ln
    grad_attended = grad_middle.astype(jnp.bfloat16)
    grad_field = extended(grad_attended, (("row", 1), ("col", 2)), rim_width)
    grad_windows = cut_windows(grad_field, row_starts, col_starts)
    grad_window_flat = grad_windows.reshape(-1, model_width)
    grad_window_own = grad_window_flat * own_low
    grad_proj_w = outer_sum(mixed_flat, grad_window_own)
    grad_proj_bias = jnp.sum(grad_window_own, 0, dtype=jnp.float32)
    grad_mixed = (
        times_transposed(grad_window_flat, w_proj)
        .astype(jnp.bfloat16)
        .reshape(window_count, window_tokens, head_count, head_size)
    )
    table_zero = jnp.zeros((WIN, WIN, head_size), jnp.float32)
    table_grads, grad_packed = lax.scan(
        lambda carried, inputs: attend_back(carried, inputs, table_rows, table_cols),
        (table_zero, table_zero),
        (queries, keys_w, values, log_total, grad_mixed, own_token),
    )
    grad_packed_flat = grad_packed.reshape(-1, 3 * model_width)
    grad_packed_own = grad_packed_flat * own_low
    grad_qkv_w = outer_sum(window_flat, grad_packed_own)
    grad_query_add = jnp.sum(grad_packed_own[:, :model_width], 0, dtype=jnp.float32)
    grad_value_add = jnp.sum(grad_packed_own[:, 2 * model_width :], 0, dtype=jnp.float32)
    grad_window_normed = (
        times_transposed(grad_packed_flat, w_qkv)
        .astype(jnp.bfloat16)
        .reshape(window_count, window_tokens, model_width)
        * window_mask
    )
    grad_normed_field = place_windows(grad_window_normed, row_starts, col_starts, padded_field)
    grad_normed = grad_normed_field[
        :, rim_width : rim_width + tile_rows, rim_width : rim_width + tile_cols
    ]
    grad_tokens_ln, grad_gain_one, grad_bias_one = norm_backward(
        grad_normed.astype(jnp.float32), normal_one, inverse_one, gain_one
    )
    input_grad = (grad_middle + grad_tokens_ln).astype(jnp.bfloat16)
    grad_table_rows = jnp.einsum(
        "ykc,ykr->rc", table_grads[0], onehot_table, precision=TOP_PRECISION
    )
    grad_table_cols = jnp.einsum(
        "ykc,ykr->rc", table_grads[1], onehot_table, precision=TOP_PRECISION
    )
    matrices = (grad_qkv_w, grad_proj_w, grad_up_w, grad_down_w)
    shards = reduce_images(reduce_tiles(matrices))
    small = lax.psum(
        (
            grad_gain_one,
            grad_bias_one,
            grad_query_add,
            grad_value_add,
            grad_table_rows,
            grad_table_cols,
            grad_proj_bias,
            grad_gain_two,
            grad_bias_two,
            grad_up_bias,
            grad_down_bias,
        ),
        ("dp", "row", "col"),
    )
    return (
        output,
        input_grad,
        small[0],
        small[1],
        shards[0],
        small[2],
        small[3],
        small[4],
        small[5],
        shards[1],
        small[6],
        small[7],
        small[8],
        shards[2],
        small[9],
        shards[3],
        small[10],
        statistics,
    )


def solution(mesh):
    placed = (
        P("dp", "row", "col", None),
        P(),
        P(),
        P("dp", ("row", "col")),
        P(),
        P(),
        P(),
        P(),
        P("dp", ("row", "col")),
        P(),
        P(),
        P(),
        P("dp", ("row", "col")),
        P(),
        P("dp", ("row", "col")),
        P(),
        P("dp", "row", "col", None),
    )
    return jax.shard_map(
        on_device,
        mesh=mesh,
        in_specs=placed,
        out_specs=(
            P("dp", "row", "col", None),
            P("dp", "row", "col", None),
            P(),
            P(),
            P("dp", ("row", "col")),
            P(),
            P(),
            P(),
            P(),
            P("dp", ("row", "col")),
            P(),
            P(),
            P(),
            P("dp", ("row", "col")),
            P(),
            P("dp", ("row", "col")),
            P(),
            P("dp", None),
        ),
        check_vma=False,
    )
```

profile of v0, /device:TPU:0, one launch (start us, length us, event | category | flops | bytes accessed | tf_op | source)
XLA Modules:
  0.0 1637.4 jit_solution(213898159662820051)
XLA Ops:
  9.5 63.0 %all-gather.8.cloned.1.call-done = bf16[384,2304]{0,1:T(8,128)(2,1)} async-done(((bf16[384,144]{0,1:T(8,128)(2,1)}), bf16[384,2304]{0,1:T(8,128)(2,1)}) %all-gather.8.cloned.1.call-update) | async-done | bytes 1769488 | tf_op jit(solution)/shard_map/all_gather | solution.py:261
  72.6 50.2 %all_gather.26 = bf16[384,768]{0,1:T(8,128)(2,1)} all-gather(bf16[384,48]{0,1:T(8,128)(2,1)} %param.39), channel_id=1, replica_groups=mesh['dp'=2,'row'=4,'col'=4] {'row','col'}, dimensions={1}, use_global_device_ids=true | all-gather | bytes 626688 | tf_op jit(solution)/shard_map/all_gather | solution.py:262
  122.9 15.0 all-gather.14.cloned.1.call-done
  163.6 18.6 %collective-permute-done.2 = bf16[1,40,12,768]{3,1,2,0:T(8,128)(2,1)S(1)} collective-permute-done((bf16[1,40,12,768]{3,1,2,0:T(8,128)(2,1)S(1)}, bf16[1,40,12,768]{3,1,2,0:T(8,128)(2,1)S(1)}, u32[]{:S(2)}, u32[]{:S(2)}) %collective-permute-start.2) | collective-permute-done | bytes 737312 | tf_op jit(solution)/shard_map/ppermute | solution.py:20
  189.3 14.7 all-gather.18.cloned.1.call-done
  248.3 242.0 %while.27 = (s32[]{:T(128)}, bf16[4,196,12,64]{1,3,2,0:T(8,128)(2,1)}, f32[4,12,196]{2,1,0:T(8,128)}, bf16[4,196,12,64]{1,3,2,0:T(8,128)(2,1)}, bf16[4,196,12,64...) while((s32[]{:T(128)}, ...), condition=%wide.region_9.10_spmd, body=%wide.region_6.0_spmd.sunk | while | flops 172888464 | bytes 25736608 | solution.py:336
  586.2 13.0 collective-permute-done.6
  625.8 473.8 %while.28 = (s32[]{:T(128)}, f32[14,14,64]{2,1,0:T(8,128)S(1)}, f32[14,14,64]{2,1,0:T(8,128)}, bf16[4,196,2304]{1,2,0:T(8,128)(2,1)}, bf16[4,196,12,64]{3,1,2,0:...) while((s32[]{:T(128)}, f32[14,14,64]{2,1,0:T(8,128)S(1)}, ...), condition=%wide.region_24.25_spmd.clone, body=%wide.region_20.24_spmd.clone.sunk | while | flops 456110016 | bytes 68291904 | solution.py:390
  641.0 12.8 add.563
  666.4 12.7 add.565
  686.1 12.7 reshape.735
  757.4 12.7 add.563
  782.8 12.7 add.565
  802.4 12.7 reshape.735
  873.6 12.7 add.563
  898.9 12.7 add.565
  918.5 12.7 reshape.735
  989.8 12.7 add.563
  1034.7 12.7 reshape.735
  1175.2 81.2 %reduce-scatter.15.cloned.1.call-done = bf16[768,144]{0,1:T(8,128)(2,1)} async-done(((bf16[768,2304]{0,1:T(8,128)(2,1)}), bf16[768,144]{0,1:T(8,128)(2,1)}) %reduce-scatter.15.cloned.1.call-update) | async-done | bytes 221200 | tf_op jit(solution)/shard_map/reduce_scatter | solution.py:205
  1265.9 132.1 %reduce-scatter.19.cloned.1.call-done = bf16[768,192]{0,1:T(8,128)(2,1)} async-done(((bf16[768,3072]{0,1:T(8,128)(2,1)}), bf16[768,192]{0,1:T(8,128)(2,1)}) %reduce-scatter.19.cloned.1.call-update) | async-done | bytes 294928 | tf_op jit(solution)/shard_map/reduce_scatter | solution.py:211
  1406.0 134.7 %reduce-scatter.21.cloned.1.call-done = bf16[3072,48]{0,1:T(8,128)(2,1)} async-done(((bf16[3072,768]{0,1:T(8,128)(2,1)}), bf16[3072,48]{0,1:T(8,128)(2,1)}) %reduce-scatter.21.cloned.1.call-update) | async-done | bytes 294928 | tf_op jit(solution)/shard_map/reduce_scatter | solution.py:214
  1541.1 40.1 %psum.95 = f32[1,5]{1,0:T(1,128)S(1)} all-reduce(f32[1,5]{1,0:T(1,128)S(1)} %stack.90), channel_id=1, replica_groups=mesh['dp'=2,'row'=4,'col'=4] {'row','col'}, use_global_device_ids=true, to_apply=%region_60.61 | all-reduce | flops 5 | bytes 40 | tf_op jit(solution)/shard_map/psum | solution.py:360
  1584.3 39.0 %all-reduce = (f32[768]{0:T(1024)}, f32[768]{0:T(1024)}, f32[768]{0:T(1024)}, f32[768]{0:T(1024)}, f32[27,64]{1,0:T(8,128)}, /*index=5*/f32[27,64]{1,0:T(8,128)}...) all-reduce(f32[768]{0:T(1024)S(1)} %get-tuple-element.273, ...), channel_id=1, replica_groups=mesh['dp'=2,'row'=4,'col'=4] {'dp','row','col'}, use_global_device_ids=true, to_apply=%region_28.29 | all-reduce | flops 12672 | bytes 101376 | tf_op jit(solution)/shard_map/psum | solution.py:422
  (602 shorter events, 863.3 us)
Async XLA Ops:
  7.2 65.3 %all-gather.8.cloned.1.call-start = ((), (), s32[]{:S(2)}) async-start(), calls=%async_computation.8 | async-start | bytes 1880064 | tf_op jit(solution)/shard_map/all_gather | solution.py:261
  7.9 129.9 %all-gather.14.cloned.1.call-start = ((), (), s32[]{:S(2)}) async-start(), calls=%async_computation.11 | async-start | bytes 2506752 | tf_op jit(solution)/shard_map/all_gather | solution.py:263
  8.7 195.3 %all-gather.18.cloned.1.call-start = ((), (), s32[]{:S(2)}) async-start(), calls=%async_computation.13 | async-start | bytes 2506752 | tf_op jit(solution)/shard_map/all_gather | solution.py:264
  9.4 207.4 %all-gather.10.cloned.1.call-start = ((), (), s32[]{:S(2)}) async-start(), calls=%async_computation.9 | async-start | bytes 5308416 | tf_op jit(solution)/shard_map/all_gather | solution.py:267
  72.5 421.9 %all-gather.12.cloned.1.call-start = ((), (), s32[]{:S(2)}) async-start(), calls=%async_computation.10 | async-start | bytes 1769472 | tf_op jit(solution)/shard_map/all_gather | solution.py:268
  122.8 409.0 %all-gather.16.cloned.1.call-start = ((), (), s32[]{:S(2)}) async-start(), calls=%async_computation.12 | async-start | bytes 7077888 | tf_op jit(solution)/shard_map/all_gather | solution.py:269
  137.9 405.1 %all-gather.20.cloned.1.call-start = ((), (), s32[]{:S(2)}) async-start(), calls=%async_computation.14 | async-start | bytes 7077888 | tf_op jit(solution)/shard_map/all_gather | solution.py:270
  138.8 17.6 %collective-permute-start = (bf16[1,12,16,768]{3,2,1,0:T(8,128)(2,1)S(1)}, bf16[1,12,16,768]{3,2,1,0:T(8,128)(2,1)S(1)}, u32[]{:S(2)}, u32[]{:S(2)}) collective-permute-start(bf16[1,12,16,768]{3,2,1,0:T(8,128)(2,1)S(1)} %get-tuple-element.376), channel_id=1, source_target_pairs={{0,4},{4,8},{8,12},{1,5},{5,9},{9,13},{2,6},{6,10},{10,14},{3,7},{... | collective-permute-start | bytes 884744 | tf_op jit(solution)/shard_map/ppermute | solution.py:20
  142.2 14.9 collective-permute-start.1
  157.8 24.3 %collective-permute-start.2 = (bf16[1,40,12,768]{3,1,2,0:T(8,128)(2,1)S(1)}, bf16[1,40,12,768]{3,1,2,0:T(8,128)(2,1)S(1)}, u32[]{:S(2)}, u32[]{:S(2)}) collective-permute-start(bf16[1,40,12,768]{3,1,2,0:T(8,128)(2,1)S(1)} %copy.192), channel_id=1, source_target_pairs={{0,1},{1,2},{2,3},{4,5},{5,6},{6,7},{8,9},{9,10},{10,11},{12,13},{... | collective-permute-start | bytes 2211848 | tf_op jit(solution)/shard_map/ppermute | solution.py:20
  161.9 24.7 %collective-permute-start.3 = (bf16[1,40,12,768]{3,1,2,0:T(8,128)(2,1)S(1)}, bf16[1,40,12,768]{3,1,2,0:T(8,128)(2,1)S(1)}, u32[]{:S(2)}, u32[]{:S(2)}) collective-permute-start(bf16[1,40,12,768]{3,1,2,0:T(8,128)(2,1)S(1)} %copy.193), channel_id=1, source_target_pairs={{1,0},{2,1},{3,2},{5,4},{6,5},{7,6},{9,8},{10,9},{11,10},{13,12},{... | collective-permute-start | bytes 2211848 | tf_op jit(solution)/shard_map/ppermute | solution.py:23
  204.0 963.5 %reduce-scatter.17.cloned.1.call-start = ((), (), s32[]{:S(2)}) async-start(), calls=%async_computation.16 | async-start | bytes 1253376 | tf_op jit(solution)/shard_map/reduce_scatter | solution.py:208
  558.2 10.8 collective-permute-start.4
  562.3 15.4 collective-permute-start.5
  580.1 19.1 %collective-permute-start.6 = (bf16[1,40,12,768]{3,1,2,0:T(8,128)(2,1)}, bf16[1,40,12,768]{3,1,2,0:T(8,128)(2,1)S(1)}, u32[]{:S(2)}, u32[]{:S(2)}) collective-permute-start(bf16[1,40,12,768]{3,1,2,0:T(8,128)(2,1)} %copy.205), channel_id=1, source_target_pairs={{0,1},{1,2},{2,3},{4,5},{5,6},{6,7},{8,9},{9,10},{10,11},{12,13},{... | collective-permute-start | bytes 2211848 | tf_op jit(solution)/shard_map/ppermute | solution.py:20
  583.8 19.6 %collective-permute-start.7 = (bf16[1,40,12,768]{3,1,2,0:T(8,128)(2,1)S(1)}, bf16[1,40,12,768]{3,1,2,0:T(8,128)(2,1)S(1)}, u32[]{:S(2)}, u32[]{:S(2)}) collective-permute-start(bf16[1,40,12,768]{3,1,2,0:T(8,128)(2,1)S(1)} %copy.206), channel_id=1, source_target_pairs={{1,0},{2,1},{3,2},{5,4},{6,5},{7,6},{9,8},{10,9},{11,10},{13,12},{... | collective-permute-start | bytes 2211848 | tf_op jit(solution)/shard_map/ppermute | solution.py:23
  625.8 630.6 %reduce-scatter.15.cloned.1.call-start = ((), (), s32[]{:S(2)}) async-start(), calls=%async_computation.15 | async-start | bytes 3760128 | tf_op jit(solution)/shard_map/reduce_scatter | solution.py:205
  625.8 473.8 %copy-start.61 = (bf16[4,196]{1,0:T(4,128)(2,1)S(1)}, bf16[4,196]{1,0:T(4,128)(2,1)}, u32[]{:S(2)}) copy-start(bf16[4,196]{1,0:T(4,128)(2,1)} %get-tuple-element.341) | copy-start | bytes 4708
  1123.1 274.9 %reduce-scatter.19.cloned.1.call-start = ((), (), s32[]{:S(2)}) async-start(), calls=%async_computation.17 | async-start | bytes 5013504 | tf_op jit(solution)/shard_map/reduce_scatter | solution.py:211
  1128.3 412.4 %reduce-scatter.21.cloned.1.call-start = ((), (), s32[]{:S(2)}) async-start(), calls=%async_computation.18 | async-start | bytes 5013504 | tf_op jit(solution)/shard_map/reduce_scatter | solution.py:214
  1133.4 490.4 %reduce-scatter.27.cloned.1.call-start = ((), (), s32[]{:S(2)}) async-start(), calls=%async_computation.21 | async-start | bytes 294912
  1169.3 456.2 %reduce-scatter.25.cloned.1.call-start = ((), (), s32[]{:S(2)}) async-start(), calls=%async_computation.20 | async-start | bytes 589824
  1258.2 369.0 %reduce-scatter.29.cloned.1.call-start = ((), (), s32[]{:S(2)}) async-start(), calls=%async_computation.22 | async-start | bytes 589824
  1399.9 229.1 %reduce-scatter.23.cloned.1.call-start = ((), (), s32[]{:S(2)}) async-start(), calls=%async_computation.19 | async-start | bytes 442368 | tf_op jit(solution)/shard_map/reduce_scatter | solution.py:231
  (113 other events, 4624.4 us)
Sparse Core Ops, SparseCore 0:
  10.8 61.6 all-gather.7
  75.2 62.5 all-gather.13
  140.6 63.3 all-gather.17
  205.4 11.3 all-gather.9
  218.3 10.3 all-gather.11
  230.1 15.4 all-gather.15
  247.1 15.6 all-gather.19
  625.9 123.4 reduce-scatter.16
  1123.3 133.0 reduce-scatter.14
  1261.3 136.6 reduce-scatter.18
  1404.0 136.6 reduce-scatter.20
  1543.4 6.6 reduce-scatter.26
  1552.3 8.9 reduce-scatter.24
  1563.5 8.9 reduce-scatter.28
  1574.6 8.8 reduce-scatter.22
where the time goes:
time: 1650 us; the launch traced here: 1640 us
  local copies, waits for them, and re-layouts  659 us (40%)
  waiting for transfers between devices  510 us (31%)
  matrix products  171 us (10%)
  blocking collectives  129 us (8%)
  other arithmetic  114 us (7%)
  between operations  23.2 us (1%)
  starting transfers between devices  21.2 us (1%)
    add x32, local copies, waits for them, and re-layouts, window_scores(): base.reshape(head_count, WIN, WIN, WIN, WIN) + rows_term[:, :, :, :, None]  357 us
    reduce_scatter x1, waiting for transfers between devices, reduce_tiles(): lax.psum_scatter(parts[3].astype(jnp.bfloat16), ('row', 'col'), scatter_d...  135 us
    reduce_scatter x1, waiting for transfers between devices, reduce_tiles(): lax.psum_scatter(parts[2].astype(jnp.bfloat16), ('row', 'col'), scatter_d...  132 us
    reduce_scatter x1, waiting for transfers between devices, reduce_tiles(): lax.psum_scatter(parts[0].astype(jnp.bfloat16), ('row', 'col'), scatter_d...  81.2 us
    all_gather x1, waiting for transfers between devices, on_device(): lax.all_gather(qkv_weight, ('row', 'col'), axis=1, tiled=True)  63 us
    convert_element_type x4, local copies, waits for them, and re-layouts, attend_back(): rows_sum = jnp.sum(grad_five, axis=4, dtype=jnp.float32)  50.7 us
    all_gather x1, blocking collectives, on_device(): lax.all_gather(proj_weight, ('row', 'col'), axis=1, tiled=True)  50.2 us
    psum x1, blocking collectives, on_device(): square_totals = lax.psum(squares, ('row', 'col'))  40.1 us
  transfers between devices with their start and end apart: 23, of which 14 were waited for; matrix products, arithmetic and copies ran while one was open for 55% of the time, Pallas kernels for 0%

commit v1 on v0

v1 whole, which is shorter than its diff:
```python
import functools

import jax
import jax.numpy as jnp
import numpy as np
from jax import lax
from jax.experimental import pallas as pl
from jax.experimental.pallas import tpu as pltpu
from jax.sharding import PartitionSpec as P

HEADS = 12
HEAD = 64
WIN = 14
EPS = 1e-06
MESH = pl.DeviceIdType.MESH
F32 = jnp.float32
BF = jnp.bfloat16

D = HEADS * HEAD
TILE = 16
TOK = TILE * TILE
HI, LO = 12, 6
SLOT = 256
QROWS = WIN * 16
PAIRS = HEADS // 2
FIELD = 1184
SENDS = 640
MIB = 2**20

LINKS = {
    (-1, 0): (True, 0, 192, 352),
    (1, 0): (True, 160, 96, 256),
    (0, -1): (False, 0, 192, 640),
    (0, 1): (False, 192, 96, 544),
    (-1, -1): (False, 288, 144, 1040),
    (-1, 1): (False, 432, 80, 960),
    (1, -1): (False, 512, 80, 880),
    (1, 1): (False, 592, 48, 832),
}


def nt(a, b):
    return lax.dot_general(a, b, (((1,), (1,)), ((), ())), preferred_element_type=F32)


def nn(a, b):
    return lax.dot_general(a, b, (((1,), (0,)), ((), ())), preferred_element_type=F32)


def tn(a, b):
    return lax.dot_general(a, b, (((0,), (0,)), ((), ())), preferred_element_type=F32)


def pick_rows():
    table = np.zeros((SENDS, TOK), np.float32)
    spans = {
        0: (range(16), range(12)),
        192: (range(16), range(10, 16)),
        288: (range(12), range(12)),
        432: (range(12), range(10, 16)),
        512: (range(10, 16), range(12)),
        592: (range(10, 16), range(10, 16)),
    }
    for base, (ys, xs) in spans.items():
        for i, (y, x) in enumerate((y, x) for y in ys for x in xs):
            table[base + i, y * TILE + x] = 1.0
    return table


def table_places(back):
    place = np.zeros((256, 64), np.float32)
    for head in range(2):
        for r in range(2 * WIN - 1):
            for copy in range(2):
                row_lane = (64 + 28 * copy + r + 64 * head) % 128
                col_lane = (28 * copy + r + 64 * head) % 128
                place[128 * head + row_lane, 26 - r] = 1.0
                place[128 * head + col_lane, 32 + (r if back else 26 - r)] = 1.0
    return place


def key_marks(back):
    marks = np.zeros((2, SLOT, 128), np.float32)
    for head in range(2):
        for j in range(SLOT):
            k, l = divmod(j, 16)
            if k < WIN and l < WIN:
                for copy in range(2):
                    marks[head, j, (64 + 28 * copy + k + 64 * head) % 128] = 1.0
                    marks[head, j, (78 + 28 * copy + (13 - l if back else l) + 64 * head) % 128] = 1.0
            else:
                marks[head, j, (120 + 64 * head) % 128] = -1e30
    return marks


def lane_kinds(rows):
    lane = lax.broadcasted_iota(jnp.int32, (rows, 128), 1)
    kinds = []
    for head in range(2):
        at = (lane + 64 * head) % 128 if head else lane
        own = at < 64
        first = (at >= 64) & (at < 92)
        second = (at >= 92) & (at < 120)
        is_row = ((at >= 64) & (at < 78)) | ((at >= 92) & (at < 106))
        kinds.append((own, first, second, is_row, at == 120))
    return kinds


def slot_axis(first, count, tile_at, tiles):
    rel = first + count - TILE * tile_at
    valid = (count < WIN) & (first + count < TILE * tiles)
    return rel, valid


def window_index(a, b, row, col, n_row, n_col):
    place = lax.broadcasted_iota(jnp.int32, (SLOT, 1), 0)
    y = place // 16
    x = place - 16 * y
    ry, ok_y = slot_axis(((TILE * row) // WIN + a) * WIN, y, row, n_row)
    rx, ok_x = slot_axis(((TILE * col) // WIN + b) * WIN, x, col, n_col)
    up, down = ry < 0, ry >= TILE
    left, right = rx < 0, rx >= TILE
    base_mid = jnp.where(up, 256, jnp.where(down, 352, 0))
    base_left = jnp.where(up, 832, jnp.where(down, 960, 544))
    base_right = jnp.where(up, 880, jnp.where(down, 1040, 640))
    base = jnp.where(left, base_left, jnp.where(right, base_right, base_mid))
    width = jnp.where(left, LO, jnp.where(right, HI, TILE))
    py = jnp.where(up, ry + LO, jnp.where(down, ry - TILE, ry))
    px = jnp.where(left, rx + LO, jnp.where(right, rx - TILE, rx))
    return jnp.where(ok_y & ok_x, base + py * width + px, -1)


def own_slot(row, col):
    place = lax.broadcasted_iota(jnp.int32, (TOK, 1), 0)
    ty = place // TILE
    tx = place - TILE * ty
    out = 0
    parts = []
    for t, at in ((ty, row), (tx, col)):
        y = TILE * at + t - ((TILE * at) // WIN) * WIN
        late = (y >= WIN).astype(jnp.int32)
        parts.append((late, y - WIN * late))
    (a, y), (b, x) = parts
    return (2 * a + b) * SLOT + 16 * y + x


def own_mask(row, col, n_row, n_col):
    place = lax.broadcasted_iota(jnp.int32, (1, 4 * SLOT), 1)
    slot = place // SLOT
    rest = place - slot * SLOT
    y = rest // 16
    x = rest - 16 * y
    a = slot // 2
    b = slot - 2 * a
    good = None
    for t, which, at, n in ((y, a, row, n_row), (x, b, col, n_col)):
        rel = ((TILE * at) // WIN + which) * WIN + t - TILE * at
        end = jnp.where(at == n - 1, 4096, TILE)
        ok = (t < WIN) & (rel >= 0) & (rel < end)
        good = ok if good is None else good & ok
    return good


def one_hot(index, size):
    lane = lax.broadcasted_iota(jnp.int32, (index.shape[0], size), 1)
    return jnp.where(lane == index, 1.0, 0.0).astype(BF)


def norm(v, gain, bias):
    mean = jnp.mean(v, -1, keepdims=True)
    center = v - mean
    inverse = lax.rsqrt(jnp.mean(center * center, -1, keepdims=True) + EPS)
    xhat = center * inverse
    return xhat * gain + bias, xhat, inverse


def norm_back(grad, xhat, inverse, gain):
    d = grad * gain
    return inverse * (
        d - jnp.mean(d, -1, keepdims=True) - xhat * jnp.mean(d * xhat, -1, keepdims=True)
    )


def grid_place():
    return lax.axis_index("dp"), lax.axis_index("row"), lax.axis_index("col")


def exists(step, row, col, n_row, n_col):
    r, c = row + step[0], col + step[1]
    return (r >= 0) & (r < n_row) & (c >= 0) & (c < n_col)


def greet(n_row, n_col, corners, lines):
    dp, row, col = grid_place()
    barrier = pltpu.get_barrier_semaphore()
    count = 0
    if lines:
        for d in (1, 2, 3):
            pl.semaphore_signal(
                barrier, inc=1, device_id=(dp, row, lax.rem(col + d, n_col)), device_id_type=MESH
            )
            pl.semaphore_signal(
                barrier, inc=1, device_id=(dp, lax.rem(row + d, n_row), col), device_id_type=MESH
            )
        pl.semaphore_signal(barrier, inc=1, device_id=(1 - dp, row, col), device_id_type=MESH)
        count += 7
    if corners:
        for step in LINKS:
            if lines and 0 in step:
                continue
            there = exists(step, row, col, n_row, n_col)

            @pl.when(there)
            def _():
                pl.semaphore_signal(
                    barrier,
                    inc=1,
                    device_id=(dp, row + step[0], col + step[1]),
                    device_id_type=MESH,
                )

            count = count + jnp.where(there, 1, 0)
    pl.semaphore_wait(barrier, count)


def halo_copies(field, picked, send, recv, n_row, n_col):
    dp, row, col = grid_place()
    out = []
    for i, (step, (own, first, rows, there)) in enumerate(LINKS.items()):
        src = (field if own else picked).at[pl.ds(first, rows)]
        out.append(
            (
                exists(step, row, col, n_row, n_col),
                pltpu.make_async_remote_copy(
                    src,
                    field.at[pl.ds(there, rows)],
                    send.at[i],
                    recv.at[i],
                    device_id=(dp, row + step[0], col + step[1]),
                    device_id_type=MESH,
                ),
                exists((-step[0], -step[1]), row, col, n_row, n_col),
            )
        )
    return out


def halo_start(field, picked, pick_ref, send, recv, n_row, n_col):
    picked[...] = nn(pick_ref[...], field[pl.ds(0, TOK), :]).astype(BF)
    for there, copy, _ in halo_copies(field, picked, send, recv, n_row, n_col):
        pl.when(there)(copy.start)


def halo_wait(field, picked, send, recv, n_row, n_col):
    for there, copy, comes in halo_copies(field, picked, send, recv, n_row, n_col):
        pl.when(there)(copy.wait_send)
        pl.when(comes)(copy.wait_recv)


def halo_xla(own, n_row, n_col):
    grid = own.reshape(TILE, TILE, -1)
    cut = {
        (-1, 0): grid[:12],
        (1, 0): grid[10:],
        (0, -1): grid[:, :12],
        (0, 1): grid[:, 10:],
        (-1, -1): grid[:12, :12],
        (-1, 1): grid[:12, 10:],
        (1, -1): grid[10:, :12],
        (1, 1): grid[10:, 10:],
    }
    pieces = {0: own}
    for step, block in cut.items():
        pairs = [
            (r * n_col + c, (r + step[0]) * n_col + c + step[1])
            for r in range(n_row)
            for c in range(n_col)
            if 0 <= r + step[0] < n_row and 0 <= c + step[1] < n_col
        ]
        flat = block.reshape(-1, own.shape[1])
        got = lax.ppermute(flat, ("row", "col"), pairs)
        rows, there = LINKS[step][2:]
        pieces[there] = jnp.pad(got, ((0, rows - got.shape[0]), (0, 0)))
    return jnp.concatenate([pieces[k] for k in sorted(pieces)], 0)


def blocks_of(shapes):
    return [(n // 16, k // 2) for n, k in shapes]


class Gather:
    def __init__(self, full, block, half, send, recv):
        dp, row, col = grid_place()
        self.full, self.b, self.h = full, block, half
        self.send, self.recv = send, recv
        self.dp, self.row, self.col = dp, row, col
        self.lanes = pl.ds(pl.multiple_of(dp * half, 128), half)
        self.other = pl.ds(pl.multiple_of((1 - dp) * half, 128), half)

    def region(self, first, rows, lanes):
        return self.full.at[pl.ds(pl.multiple_of(first, 16), rows), lanes]

    def group(self, flip, part=None):
        first = jnp.bitwise_xor(self.row, flip) * 4 * self.b
        if part is None:
            return first, 4 * self.b
        return first + part * 2 * self.b, 2 * self.b

    def copy(self, i, at, land, target):
        core = target == "core"
        if core:
            device = (1 - self.dp, self.row, self.col)
        elif isinstance(target, tuple):
            device = (self.dp, self.row, lax.rem(self.col + target[0], 4))
        else:
            device = (self.dp, jnp.bitwise_xor(self.row, target), self.col)

        def make(where):
            return pltpu.make_async_remote_copy(
                where, where, self.send.at[i], self.recv.at[i], device_id=device, device_id_type=MESH
            )

        return (
            lambda: make(self.region(*at, self.lanes)),
            lambda: make(self.region(*land, self.other if core else self.lanes)),
        )

    def stage(self, k):
        own = (self.row * 4 + self.col) * self.b
        out = []
        if k == 0:
            for d in (1, 2, 3):
                frm = (self.row * 4 + lax.rem(self.col + 4 - d, 4)) * self.b
                out.append(self.copy(d - 1, (own, self.b), (frm, self.b), (d,)))
        elif k == 1:
            for i, flip in ((3, 1), (4, 2)):
                out.append(self.copy(i, self.group(0), self.group(flip), flip))
            out.append(self.copy(7, self.group(0), self.group(0), "core"))
        elif k == 2:
            out.append(self.copy(5, self.group(2, 0), self.group(3, 0), 1))
            out.append(self.copy(6, self.group(1, 1), self.group(3, 1), 2))
            out.append(self.copy(8, self.group(1), self.group(1), "core"))
            out.append(self.copy(9, self.group(2), self.group(2), "core"))
        else:
            out.append(self.copy(10, self.group(3), self.group(3), "core"))
        return out

    def start(self, k):
        for out, _ in self.stage(k):
            out().start()

    def arrive(self, k):
        for (_, come), link in zip(self.stage(k), self.links(k)):
            if link:
                come().wait_recv()

    def links(self, k):
        return {0: (1, 1, 1), 1: (1, 1, 0), 2: (1, 1, 0, 0), 3: (0,)}[k]

    def finish(self):
        for k in range(4):
            for (out, come), link in zip(self.stage(k), self.links(k)):
                if not link:
                    come().wait_recv()
                out().wait_send()


GATHER_SEMS = 11


def gather_kernel(
    n_row, n_col, shapes,
    tokens, vecs, pick, w0, w1, w2, w3,
    field, f0, f1, f2, f3,
    picked, s0, s1, s2, s3, halo_send, halo_recv, local_sem, *sems,
):
    dp, row, col = grid_place()
    field[pl.ds(TOK, FIELD - TOK), :] = jnp.zeros((FIELD - TOK, D), BF)
    greet(n_row, n_col, True, True)
    ways = []
    for i, (shard, stage, full, (b, h)) in enumerate(
        zip((w0, w1, w2, w3), (s0, s1, s2, s3), (f0, f1, f2, f3), blocks_of(shapes))
    ):
        stage[...] = shard[...].T
        way = Gather(full, b, h, sems[2 * i], sems[2 * i + 1])
        mine = pltpu.make_async_copy(
            stage, way.region((row * 4 + col) * b, b, way.lanes), local_sem.at[i]
        )
        mine.start()
        ways.append((way, mine))
    normed, _, _ = norm(tokens[...].astype(F32), vecs[0:1, :], vecs[1:2, :])
    field[pl.ds(0, TOK), :] = normed.astype(BF)
    halo_start(field, picked, pick, halo_send, halo_recv, n_row, n_col)
    for way, mine in ways:
        mine.wait()
        way.start(0)
    for k in range(3):
        for way, _ in ways:
            way.arrive(k)
            way.start(k + 1)
    halo_wait(field, picked, halo_send, halo_recv, n_row, n_col)
    for way, _ in ways:
        way.finish()


def vmem():
    return pl.BlockSpec(memory_space=pltpu.VMEM)


def hbm():
    return pl.BlockSpec(memory_space=pl.ANY)


def gather_call(n_row, n_col, shapes, tokens, vecs, pick, shards):
    blocks = blocks_of(shapes)
    sems = []
    for _ in range(4):
        sems += [pltpu.SemaphoreType.DMA((GATHER_SEMS,)), pltpu.SemaphoreType.DMA((GATHER_SEMS,))]
    return pl.pallas_call(
        functools.partial(gather_kernel, n_row, n_col, shapes),
        name="gather",
        out_shape=[jax.ShapeDtypeStruct((FIELD, D), BF)]
        + [jax.ShapeDtypeStruct(s, BF) for s in shapes],
        in_specs=[vmem()] * 7,
        out_specs=[vmem()] + [hbm()] * 4,
        scratch_shapes=[pltpu.VMEM((SENDS, D), BF)]
        + [pltpu.VMEM(b, BF) for b in blocks]
        + [
            pltpu.SemaphoreType.DMA((8,)),
            pltpu.SemaphoreType.DMA((8,)),
            pltpu.SemaphoreType.DMA((4,)),
        ]
        + sems,
        compiler_params=pltpu.CompilerParams(
            collective_id=0, has_side_effects=True, vmem_limit_bytes=40 * MIB
        ),
    )(tokens, vecs, pick, *shards)


def halo_kernel(n_row, n_col, own, pick, field, picked, send, recv):
    field[pl.ds(TOK, FIELD - TOK), :] = jnp.zeros((FIELD - TOK, D), BF)
    field[pl.ds(0, TOK), :] = own[...]
    greet(n_row, n_col, True, False)
    halo_start(field, picked, pick, send, recv, n_row, n_col)
    halo_wait(field, picked, send, recv, n_row, n_col)


def halo_call(n_row, n_col, own, pick):
    return pl.pallas_call(
        functools.partial(halo_kernel, n_row, n_col),
        name="halo",
        out_shape=jax.ShapeDtypeStruct((FIELD, D), BF),
        in_specs=[vmem()] * 2,
        out_specs=vmem(),
        scratch_shapes=[
            pltpu.VMEM((SENDS, D), BF),
            pltpu.SemaphoreType.DMA((8,)),
            pltpu.SemaphoreType.DMA((8,)),
        ],
        compiler_params=pltpu.CompilerParams(
            collective_id=1, has_side_effects=True, vmem_limit_bytes=40 * MIB
        ),
    )(own, pick)


class Reduce:
    def __init__(self, grad, total, come, block, half, send, recv):
        self.dp, self.row, self.col = grid_place()
        self.grad, self.total, self.come = grad, total, come
        self.b, self.h, self.send, self.recv = block, half, send, recv
        self.lanes = pl.ds(pl.multiple_of(self.dp * half, 128), half)
        self.other = pl.ds(pl.multiple_of((1 - self.dp) * half, 128), half)

    def at(self, flip):
        return pl.multiple_of(jnp.bitwise_xor(self.row, flip) * 4 * self.b, 16)

    def copies(self, k):
        b, come = self.b, self.come
        if k == 0:
            plan = [
                (self.grad.at[:, self.other], come.at[pl.ds(0, 16 * b)], (1 - self.dp, self.row, self.col))
            ]
        elif k == 1:
            x = (self.dp, jnp.bitwise_xor(self.row, 1), self.col)
            y = (self.dp, jnp.bitwise_xor(self.row, 2), self.col)
            far = self.at(3)
            plan = [
                (self.total.at[pl.ds(far, 2 * b)], come.at[pl.ds(16 * b, 2 * b)], x),
                (
                    self.total.at[pl.ds(pl.multiple_of(far + 2 * b, 16), 2 * b)],
                    come.at[pl.ds(18 * b, 2 * b)],
                    y,
                ),
            ]
        elif k == 2:
            plan = [
                (
                    self.total.at[pl.ds(self.at(flip), 4 * b)],
                    come.at[pl.ds(20 * b + 4 * b * (flip - 1), 4 * b)],
                    (self.dp, jnp.bitwise_xor(self.row, flip), self.col),
                )
                for flip in (1, 2)
            ]
        else:
            plan = []
            for d in (1, 2, 3):
                to = lax.rem(self.col + d, 4)
                plan.append(
                    (
                        self.total.at[pl.ds(pl.multiple_of(self.at(0) + to * b, 16), b)],
                        come.at[pl.ds((27 + d) * b, b)],
                        (self.dp, self.row, to),
                    )
                )
        base = {0: 0, 1: 1, 2: 3, 3: 5}[k]
        return [
            pltpu.make_async_remote_copy(
                src, dst, self.send.at[base + i], self.recv.at[base + i], device_id=dev, device_id_type=MESH
            )
            for i, (src, dst, dev) in enumerate(plan)
        ]

    def start(self, k):
        for copy in self.copies(k):
            copy.start()

    def arrive(self, k):
        for copy in self.copies(k):
            copy.wait_recv()

    def sent(self, k):
        for copy in self.copies(k):
            copy.wait_send()

    def add(self, k):
        b, h = self.b, self.h
        total, come = self.total, self.come
        step = 48 if h <= 384 else 16

        def loop(rows, into, froms):
            def body(i, _):
                at = pl.ds(pl.multiple_of(into + i * step, 16), step)
                value = total[at, :].astype(F32)
                for f in froms:
                    value = value + come[pl.ds(pl.multiple_of(f + i * step, 16), step), :].astype(F32)
                total[at, :] = value.astype(BF)
                return 0

            lax.fori_loop(0, rows // step, body, 0)

        if k == 0:

            def body(i, _):
                at = pl.ds(pl.multiple_of(i * step, 16), step)
                value = self.grad[at, self.lanes].astype(F32) + come[at, :].astype(F32)
                total[at, :] = value.astype(BF)
                return 0

            lax.fori_loop(0, 16 * b // step, body, 0)
        elif k == 1:
            loop(2 * b, self.at(2), (16 * b,))
            loop(2 * b, self.at(1) + 2 * b, (18 * b,))
        elif k == 2:
            loop(4 * b, self.at(0), (20 * b, 24 * b))

    def result(self):
        b = self.b
        mine = pl.ds(pl.multiple_of(self.at(0) + self.col * b, 16), b)
        value = self.total[mine, :].astype(F32)
        for d in (1, 2, 3):
            value = value + self.come[pl.ds((27 + d) * b, b), :].astype(F32)
        return value.T


REDUCE_SEMS = 8


def reduce_kernel(
    n_row, n_col, shapes,
    small, g0, g1, g2, g3,
    o0, o1, o2, o3, small_out,
    t0, c0, t1, c1, t2, c2, t3, c3, small_in, small_sem, *sems,
):
    dp, row, col = grid_place()
    greet(n_row, n_col, False, True)
    ways = []
    for i, (g, t, c, (b, h)) in enumerate(
        zip((g0, g1, g2, g3), (t0, t1, t2, t3), (c0, c1, c2, c3), blocks_of(shapes))
    ):
        ways.append(Reduce(g, t, c, b, h, sems[2 * i], sems[2 * i + 1]))
    for way in ways:
        way.start(0)
    small_out[...] = small[...]
    partners = [
        (dp, jnp.bitwise_xor(row, 1), col),
        (dp, jnp.bitwise_xor(row, 2), col),
        (dp, row, jnp.bitwise_xor(col, 1)),
        (dp, row, jnp.bitwise_xor(col, 2)),
        (1 - dp, row, col),
    ]

    def small_copy(s):
        return pltpu.make_async_remote_copy(
            small_out, small_in.at[s], small_sem.at[0, s], small_sem.at[1, s], device_id=partners[s], device_id_type=MESH
        )

    def small_step(s):
        small_copy(s).wait()
        value = small_in[s]
        if s == 4:
            line = lax.broadcasted_iota(jnp.int32, value.shape, 0)
            value = jnp.where(line == 12, 0.0, value)
        small_out[...] = small_out[...] + value
        if s < 4:
            small_copy(s + 1).start()

    small_copy(0).start()
    for way in ways:
        way.arrive(0)
        way.add(0)
        way.start(1)
    small_step(0)
    for way in ways:
        way.arrive(1)
        way.add(1)
        way.start(2)
    small_step(1)
    for n, way in enumerate(ways):
        way.arrive(2)
        way.add(2)
        way.start(3)
        if n == 0:
            small_step(2)
        if n == 1:
            small_step(3)
    small_step(4)
    for way, out in zip(ways, (o0, o1, o2, o3)):
        way.arrive(3)
        out[...] = way.result()
        for k in range(4):
            way.sent(k)


def reduce_call(n_row, n_col, shapes, small, grads):
    blocks = blocks_of(shapes)
    scratch, sems = [], []
    for (n, k), (b, h) in zip(shapes, blocks):
        scratch += [pltpu.VMEM((n, h), BF), pltpu.VMEM((31 * b, h), BF)]
        sems += [pltpu.SemaphoreType.DMA((REDUCE_SEMS,)), pltpu.SemaphoreType.DMA((REDUCE_SEMS,))]
    return pl.pallas_call(
        functools.partial(reduce_kernel, n_row, n_col, shapes),
        name="reduce",
        out_shape=[jax.ShapeDtypeStruct((h, b), F32) for b, h in blocks]
        + [jax.ShapeDtypeStruct(small.shape, F32)],
        in_specs=[vmem()] * 5,
        out_specs=[vmem()] * 5,
        scratch_shapes=scratch
        + [pltpu.VMEM((5,) + small.shape, F32), pltpu.SemaphoreType.DMA((2, 5))]
        + sems,
        compiler_params=pltpu.CompilerParams(
            collective_id=2, has_side_effects=True, vmem_limit_bytes=60 * MIB
        ),
    )(small, *grads)


def table_kernel_value(places, table):
    value = nn(places, table)
    line = lax.broadcasted_iota(jnp.int32, value.shape, 0)
    lane = lax.broadcasted_iota(jnp.int32, value.shape, 1)
    return jnp.where((line < 128) == (lane < 64), value, 0.0).astype(BF)


def spread(a, back):
    rows, cols = [], []
    for y in range(WIN):
        part = a[16 * y : 16 * y + 16, :]
        if back:
            rows.append(pltpu.roll(part, 13 - y, 1))
        else:
            rows.append(pltpu.roll(part, (115 + y) % 128, 1))
            cols.append(pltpu.roll(part, 65, 1, stride=1, stride_axis=0))
    return rows, cols


def attend_pair(i, qkv, table, marks, masks, probs, mixed):
    r0 = pl.multiple_of((i // PAIRS) * SLOT, SLOT)
    pair = lax.rem(i, PAIRS)
    l0 = pl.multiple_of(pair * 128, 128)
    q2 = qkv[pl.ds(r0, QROWS), pl.ds(l0, 128)]
    k2 = qkv[pl.ds(r0, SLOT), pl.ds(D + l0, 128)]
    v2 = qkv[pl.ds(r0, SLOT), pl.ds(2 * D + l0, 128)]
    a2 = nt(q2, table[...])
    qf = q2.astype(F32) * HEAD**-0.5
    kinds = lane_kinds(QROWS)
    outs = []
    for head in range(2):
        own, first, second, is_row, one = kinds[head]
        rows, cols = spread(a2[:, 128 * head : 128 * head + 128], False)
        bias = jnp.where(is_row, jnp.concatenate(rows, 0), jnp.concatenate(cols, 0))
        high = bias.astype(BF).astype(F32)
        aug = jnp.where(
            own,
            qf,
            jnp.where(
                first, high, jnp.where(second, bias - high, jnp.where(one, 1.0, 0.0))
            ),
        ).astype(BF)
        keys = k2 * masks[head : head + 1, :] + marks[head]
        scores = nt(aug, keys)
        top = jnp.max(scores, -1, keepdims=True)
        e = jnp.exp(scores - top)
        p = (e * (1.0 / jnp.sum(e, -1, keepdims=True))).astype(BF)
        probs[(i // PAIRS) * HEADS + 2 * pair + head] = p
        outs.append(nn(p, v2))
    out = jnp.where(kinds[0][0], outs[0], outs[1]).astype(BF)
    mixed[pl.ds(r0, QROWS), pl.ds(l0, 128)] = out


def attend_kernel(
    n_row, n_col,
    field, wqkv, wproj, vecs, places, table_in, marks, masks,
    qkv, probs, mixed_own, attended,
    xw, mixed, table,
):
    _, row, col = grid_place()
    table[...] = table_kernel_value(places[...], table_in[...])
    for w in range(4):
        hot = one_hot(window_index(w // 2, w % 2, row, col, n_row, n_col), FIELD)
        xw[pl.ds(w * SLOT, SLOT), :] = nn(hot, field[...]).astype(BF)
    for part, line in ((0, 2), (1, None), (2, 3)):

        def body(n, _):
            at = pl.multiple_of(n * 256, 256)
            value = nt(xw[...], wqkv[pl.ds(part * D + at, 256), :])
            if line is not None:
                value = value + vecs[line : line + 1, pl.ds(at, 256)]
            qkv[:, pl.ds(part * D + at, 256)] = value.astype(BF)
            return 0

        lax.fori_loop(0, 3, body, 0)
    mixed[...] = jnp.zeros_like(mixed)

    def pair(i, _):
        attend_pair(i, qkv, table, marks, masks, probs, mixed)
        return 0

    lax.fori_loop(0, 4 * PAIRS, pair, 0)
    hot = one_hot(own_slot(row, col), 4 * SLOT)
    own = nn(hot, mixed[...]).astype(BF)
    mixed_own[...] = own
    attended[...] = (nt(own, wproj[...]) + vecs[4:5, :]).astype(BF)


def attend_call(n_row, n_col, field, wqkv, wproj, vecs, places, table, marks, masks):
    return pl.pallas_call(
        functools.partial(attend_kernel, n_row, n_col),
        name="attend",
        out_shape=[
            jax.ShapeDtypeStruct((4 * SLOT, 3 * D), BF),
            jax.ShapeDtypeStruct((4 * HEADS, QROWS, SLOT), BF),
            jax.ShapeDtypeStruct((TOK, D), BF),
            jax.ShapeDtypeStruct((TOK, D), BF),
        ],
        in_specs=[vmem()] * 8,
        out_specs=[vmem()] * 4,
        scratch_shapes=[
            pltpu.VMEM((4 * SLOT, D), BF),
            pltpu.VMEM((4 * SLOT, D), BF),
            pltpu.VMEM((256, 128), BF),
        ],
        compiler_params=pltpu.CompilerParams(vmem_limit_bytes=56 * MIB),
    )(field, wqkv, wproj, vecs, places, table, marks, masks)


def mlp_kernel(
    tokens, attended, cot, w1, w2, vecs,
    output, grad_middle, grad_attended, g1, g2, small,
    n2, cot_t, branch, gn2,
):
    gain = vecs[5:6, :]
    tok = tokens[...].astype(F32)
    middle = tok + attended[...].astype(F32)
    normed, xhat, inverse = norm(middle, gain, vecs[6:7, :])
    n2[...] = normed.astype(BF)
    cot_t[...] = cot[...].T
    branch[...] = jnp.zeros_like(branch)
    gn2[...] = jnp.zeros_like(gn2)
    small[...] = jnp.zeros_like(small)

    def body(j, _):
        at = pl.multiple_of(j * 256, 256)
        line = j // 3
        lane = pl.multiple_of(lax.rem(j, 3) * 256, 256)
        w1c = w1[pl.ds(at, 256), :]
        w2c = w2[:, pl.ds(at, 256)]
        u = nt(n2[...], w1c) + vecs[pl.ds(8 + line, 1), pl.ds(lane, 256)]
        cdf = 0.5 * (1.0 + lax.erf(u * 0.7071067811865476))
        act = (u * cdf).astype(BF)
        pdf = jnp.exp(-0.5 * u * u) * 0.3989422804014327
        branch[...] += nt(act, w2c)
        gact = nn(cot[...], w2c)
        gu = (gact * (cdf + u * pdf)).astype(BF)
        gn2[...] += nn(gu, w1c)
        g1[pl.ds(at, 256), :] = tn(gu, n2[...]).astype(BF)
        g2[:, pl.ds(at, 256)] = nn(cot_t[...], act).astype(BF)
        small[pl.ds(8 + line, 1), pl.ds(lane, 256)] = jnp.sum(gu.astype(F32), 0, keepdims=True)
        return 0

    lax.fori_loop(0, w1.shape[0] // 256, body, 0)
    att = attended[...].astype(F32)
    middle = tokens[...].astype(F32) + att
    normed, xhat, inverse = norm(middle, gain, vecs[6:7, :])
    br = branch[...] + vecs[7:8, :]
    result = middle + br
    output[...] = result.astype(BF)
    grad = gn2[...]
    cf = cot[...].astype(F32)
    gm = cf + norm_back(grad, xhat, inverse, gain)
    grad_middle[...] = gm
    grad_attended[...] = gm.astype(BF)
    small[5:6, :] = jnp.sum(grad * xhat, 0, keepdims=True)
    small[6:7, :] = jnp.sum(grad, 0, keepdims=True)
    small[7:8, :] = jnp.sum(cf, 0, keepdims=True)
    lane = lax.broadcasted_iota(jnp.int32, (1, D), 1)
    stats = jnp.zeros((1, D), F32)
    for n, v in enumerate((tokens[...].astype(F32), middle, result, att, br)):
        total = jnp.sum(jnp.sum(v * v, 0, keepdims=True), 1, keepdims=True)
        stats = jnp.where(lane == n, total, stats)
    small[12:13, :] = stats


def mlp_call(tokens, attended, cot, w1, w2, vecs):
    hidden = w1.shape[0]
    return pl.pallas_call(
        mlp_kernel,
        name="mlp",
        out_shape=[
            jax.ShapeDtypeStruct((TOK, D), BF),
            jax.ShapeDtypeStruct((TOK, D), F32),
            jax.ShapeDtypeStruct((TOK, D), BF),
            jax.ShapeDtypeStruct((hidden, D), BF),
            jax.ShapeDtypeStruct((D, hidden), BF),
            jax.ShapeDtypeStruct((16, D), F32),
        ],
        in_specs=[vmem()] * 6,
        out_specs=[vmem()] * 6,
        scratch_shapes=[
            pltpu.VMEM((TOK, D), BF),
            pltpu.VMEM((D, TOK), BF),
            pltpu.VMEM((TOK, D), F32),
            pltpu.VMEM((TOK, D), F32),
        ],
        compiler_params=pltpu.CompilerParams(vmem_limit_bytes=56 * MIB),
    )(tokens, attended, cot, w1, w2, vecs)


def attend_back_pair(i, qkv, gmix, probs, table, marks, masks, own_rows, dqkv, gtab):
    r0 = pl.multiple_of((i // PAIRS) * SLOT, SLOT)
    pair = lax.rem(i, PAIRS)
    l0 = pl.multiple_of(pair * 128, 128)
    scale = HEAD**-0.5
    q2 = qkv[pl.ds(r0, QROWS), pl.ds(l0, 128)]
    k2 = qkv[pl.ds(r0, SLOT), pl.ds(D + l0, 128)]
    v2 = qkv[pl.ds(r0, SLOT), pl.ds(2 * D + l0, 128)]
    g2 = gmix[pl.ds(r0, QROWS), pl.ds(l0, 128)]
    q_own = q2 * own_rows[pl.ds(r0, QROWS), :]
    kinds = lane_kinds(QROWS)
    dq, dk, dv = [], [], []
    for head in range(2):
        own, first, second, is_row, one = kinds[head]
        mask = masks[head : head + 1, :]
        p = probs[(i // PAIRS) * HEADS + 2 * pair + head]
        pf = p.astype(F32)
        dp = nt(g2, v2 * mask)
        ds = (pf * (dp - jnp.sum(pf * dp, -1, keepdims=True))).astype(BF)
        keys = k2 * (mask * jnp.asarray(scale, BF)) + marks[head]
        dqa = nn(ds, keys)
        rows, _ = spread(jnp.where(is_row, dqa, 0.0), True)
        line = jnp.where((first | second) & ~is_row, dqa, 0.0)
        back = jnp.concatenate(rows, 0) + unspread_cols(line)
        at = (lax.broadcasted_iota(jnp.int32, (QROWS, 128), 1) + 64 * head) % 128
        is_high = (at < 28) | ((at >= 64) & (at < 92))
        high = back.astype(BF).astype(F32)
        split = jnp.where(is_high, high, back - high).astype(BF)
        extra = nn(split, table[128 * head : 128 * head + 128, :])
        dq.append(dqa + extra)
        gtab[head] += tn(split, q_own)
        dk.append(tn(ds, q2))
        dv.append(tn(p, g2))
    wide = lane_kinds(SLOT)[0][0]
    dqkv[pl.ds(r0, QROWS), pl.ds(l0, 128)] = jnp.where(kinds[0][0], dq[0], dq[1]).astype(BF)
    dqkv[pl.ds(r0, SLOT), pl.ds(D + l0, 128)] = (jnp.where(wide, dk[0], dk[1]) * scale).astype(BF)
    dqkv[pl.ds(r0, SLOT), pl.ds(2 * D + l0, 128)] = jnp.where(wide, dv[0], dv[1]).astype(BF)


def unspread_cols(line):
    parts = []
    for y in range(WIN):
        parts.append(pltpu.roll(line[16 * y : 16 * y + 16, :], 50, 1, stride=1, stride_axis=0))
    return jnp.concatenate(parts, 0)


def attend_back_kernel(
    n_row, n_col,
    gfield, nfield, tokens, grad_middle, mixed_own, qkv, probs, wqkv, wproj, vecs, places, table_in, marks, masks, small_in,
    input_grad, gqkv, gproj, small,
    gw, gmix, dqkv, dqkv_own, table, own_rows, gtab,
):
    _, row, col = grid_place()
    table[...] = table_kernel_value(places[...], table_in[...])
    small[...] = jnp.zeros_like(small)
    small[0:16, :] = small_in[...]
    gtab[...] = jnp.zeros_like(gtab)
    dqkv[...] = jnp.zeros_like(dqkv)
    for w in range(4):
        index = window_index(w // 2, w % 2, row, col, n_row, n_col)
        hot = one_hot(index, FIELD)
        gw[pl.ds(w * SLOT, SLOT), :] = nn(hot, gfield[...]).astype(BF)
        own_rows[pl.ds(w * SLOT, SLOT), :] = jnp.broadcast_to(
            jnp.where((index >= 0) & (index < TOK), 1.0, 0.0), (SLOT, 128)
        ).astype(BF)
    gown = gfield[pl.ds(0, TOK), :]

    def mix(n, _):
        at = pl.multiple_of(n * 256, 256)
        gmix[:, pl.ds(at, 256)] = nn(gw[...], wproj[:, pl.ds(at, 256)]).astype(BF)
        gproj[pl.ds(at, 256), :] = tn(gfield[pl.ds(0, TOK), pl.ds(at, 256)], mixed_own[...]).astype(BF)
        return 0

    lax.fori_loop(0, 3, mix, 0)
    small[4:5, :] = jnp.sum(gown.astype(F32), 0, keepdims=True)

    def pair(i, _):
        attend_back_pair(i, qkv, gmix, probs, table, marks, masks, own_rows, dqkv, gtab)
        return 0

    lax.fori_loop(0, 4 * PAIRS, pair, 0)
    hot = one_hot(own_slot(row, col), 4 * SLOT)
    own = jnp.broadcast_to(jnp.where(own_mask(row, col, n_row, n_col), 1.0, 0.0), (16, 4 * SLOT)).astype(BF)
    small[2:3, :] = nn(own, dqkv[:, 0:D])[0:1, :]
    small[3:4, :] = nn(own, dqkv[:, 2 * D : 3 * D])[0:1, :]

    def weight(n, _):
        at = pl.multiple_of(n * 256, 256)
        part = nn(hot, dqkv[:, pl.ds(at, 256)]).astype(BF)
        dqkv_own[:, pl.ds(at, 256)] = part
        gqkv[pl.ds(at, 256), :] = tn(part, nfield[pl.ds(0, TOK), :]).astype(BF)
        return 0

    lax.fori_loop(0, 9, weight, 0)
    grad = nn(dqkv_own[...], wqkv[...]).astype(BF).astype(F32)
    gain = vecs[0:1, :]
    _, xhat, inverse = norm(tokens[...].astype(F32), gain, vecs[1:2, :])
    input_grad[...] = (grad_middle[...] + norm_back(grad, xhat, inverse, gain)).astype(BF)
    small[0:1, :] = jnp.sum(grad * xhat, 0, keepdims=True)
    small[1:2, :] = jnp.sum(grad, 0, keepdims=True)
    lane = lax.broadcasted_iota(jnp.int32, (128, 128), 1)
    left = jnp.where(lane < 64, gtab[0], 0.0)
    right = jnp.where(lane >= 64, gtab[1], 0.0)
    spots = places[...].astype(F32)
    tab = lax.dot_general(
        spots,
        jnp.concatenate([left, right], 0),
        (((0,), (0,)), ((), ())),
        precision=lax.Precision.HIGHEST,
        preferred_element_type=F32,
    )
    for t in range(4):
        small[16:32, 128 * t : 128 * t + 128] = tab[16 * t : 16 * t + 16, :]


def attend_back_call(n_row, n_col, *args):
    return pl.pallas_call(
        functools.partial(attend_back_kernel, n_row, n_col),
        name="attend_back",
        out_shape=[
            jax.ShapeDtypeStruct((TOK, D), BF),
            jax.ShapeDtypeStruct((3 * D, D), BF),
            jax.ShapeDtypeStruct((D, D), BF),
            jax.ShapeDtypeStruct((32, D), F32),
        ],
        in_specs=[vmem()] * 15,
        out_specs=[vmem()] * 4,
        scratch_shapes=[
            pltpu.VMEM((4 * SLOT, D), BF),
            pltpu.VMEM((4 * SLOT, D), BF),
            pltpu.VMEM((4 * SLOT, 3 * D), BF),
            pltpu.VMEM((TOK, 3 * D), BF),
            pltpu.VMEM((256, 128), BF),
            pltpu.VMEM((4 * SLOT, 128), BF),
            pltpu.VMEM((2, 128, 128), F32),
        ],
        compiler_params=pltpu.CompilerParams(vmem_limit_bytes=60 * MIB),
    )(*args)


def on_device(
    n_dp, n_row, n_col,
    tokens, ln1_gain, ln1_bias, qkv_weight, query_bias, value_bias, rel_rows, rel_cols,
    proj_weight, proj_bias, ln2_gain, ln2_bias, fc1_weight, fc1_bias, fc2_weight, fc2_bias, cotangent,
):
    direct = (n_dp, n_row, n_col) == (2, 4, 4)
    tok = tokens.reshape(TOK, D)
    cot = cotangent.reshape(TOK, D)
    vecs = jnp.concatenate(
        [
            jnp.stack(
                [ln1_gain, ln1_bias, query_bias, value_bias, proj_bias, ln2_gain, ln2_bias, fc2_bias]
            ),
            fc1_bias.reshape(-1, D),
        ],
        0,
    ).astype(F32)
    vecs = jnp.pad(vecs, ((0, 16 - vecs.shape[0]), (0, 0)))
    table = jnp.concatenate([jnp.pad(rel_rows, ((0, 5), (0, 0))), jnp.pad(rel_cols, ((0, 5), (0, 0)))], 0)
    table = jnp.concatenate([table, table], 1)
    pick = jnp.asarray(pick_rows(), BF)
    places, places_back = (jnp.asarray(table_places(back), BF) for back in (False, True))
    marks, marks_back = (jnp.asarray(key_marks(back), BF) for back in (False, True))
    mask_values = np.zeros((16, 128), np.float32)
    mask_values[0, :64] = 1.0
    mask_values[1, 64:] = 1.0
    masks = jnp.asarray(mask_values, BF)
    shards = (qkv_weight, proj_weight, fc1_weight, fc2_weight)
    shapes = [(s.shape[1] * n_row * n_col, s.shape[0] * n_dp) for s in shards]
    if direct:
        field, wqkv, wproj, w1, w2 = gather_call(n_row, n_col, shapes, tok, vecs, pick, shards)
    else:
        full = []
        for s in shards:
            s = lax.all_gather(s, ("row", "col"), axis=1, tiled=True)
            full.append(lax.all_gather(s, "dp", axis=0, tiled=True).T)
        wqkv, wproj, w1, w2 = full
        normed = norm(tok.astype(F32), vecs[0], vecs[1])[0].astype(BF)
        field = halo_xla(normed, n_row, n_col)
    qkv, probs, mixed_own, attended = attend_call(
        n_row, n_col, field, wqkv, wproj, vecs, places, table, marks, masks
    )
    output, grad_middle, grad_attended, g1, g2, small = mlp_call(tok, attended, cot, w1, w2, vecs)
    if direct:
        gfield = halo_call(n_row, n_col, grad_attended, pick)
    else:
        gfield = halo_xla(grad_attended, n_row, n_col)
    input_grad, gqkv, gproj, small = attend_back_call(
        n_row, n_col,
        gfield, field, tok, grad_middle, mixed_own, qkv, probs, wqkv, wproj, vecs, places_back, table, marks_back, masks, small,
    )
    grads = (gqkv, gproj, g1, g2)
    if direct:
        *sums, small = reduce_call(n_row, n_col, shapes, small, grads)
    else:
        sums = []
        for g in grads:
            g = lax.psum_scatter(g, ("row", "col"), scatter_dimension=0, tiled=True)
            g = lax.psum_scatter(g, "dp", scatter_dimension=1, tiled=True)
            sums.append(g.T.astype(F32))
        local = lax.psum(small, ("row", "col"))
        line = jnp.arange(32)[:, None] == 12
        small = jnp.where(line, local, lax.psum(jnp.where(line, 0.0, local), "dp"))
    count = TOK * n_row * n_col * D
    stats = jnp.sqrt(small[12:13, :5] / count)
    tables = jnp.concatenate([small[16:32, 128 * t : 128 * t + 128] for t in range(4)], 0)
    tables = tables[:, :64] + tables[:, 64:]
    return (
        output.reshape(tokens.shape),
        input_grad.reshape(tokens.shape),
        small[0],
        small[1],
        sums[0],
        small[2],
        small[3],
        tables[0:27],
        tables[32:59],
        sums[1],
        small[4],
        small[5],
        small[6],
        sums[2],
        small[8:12].reshape(-1),
        sums[3],
        small[7],
        stats,
    )


def solution(mesh):
    tile = P("dp", "row", "col", None)
    weight = P("dp", ("row", "col"))
    sizes = [mesh.shape[a] for a in ("dp", "row", "col")]
    ins = [tile] + [P()] * 16
    for i in (3, 8, 12, 14):
        ins[i] = weight
    ins[16] = tile
    outs = [tile, tile] + [P()] * 16
    for i in (4, 9, 13, 15):
        outs[i] = weight
    outs[17] = P("dp", None)
    return jax.shard_map(
        functools.partial(on_device, *sizes),
        mesh=mesh,
        in_specs=tuple(ins),
        out_specs=tuple(outs),
        check_vma=False,
    )
```

time: 1650 us -> 362 us (0.22)
  local copies, waits for them, and re-layouts: 659 us -> 34 us
  waiting for transfers between devices: 510 us -> 0 us
  Pallas kernels: 0 us -> 323 us
  matrix products: 171 us -> 0 us
  blocking collectives: 129 us -> 0 us
  other arithmetic: 114 us -> 1.97 us
  between operations: 23.2 us -> 0.76 us
  starting transfers between devices: 21.2 us -> 0 us
    add x36 -> x0, local copies, waits for them, and re-layouts: 363 us -> none  [the longest x32 357 us: window_scores(): base.reshape(head_count, WIN, WIN, WIN, WIN) + rows_term[:, :, :, :, None]]
    reduce_scatter x5 -> x0, waiting for transfers between devices: 348 us -> none  [the longest x1 135 us: reduce_tiles(): lax.psum_scatter(parts[3].astype(jnp.bfloat16), ('row', 'col'), scatter_d...]
    pallas_call x0 -> x6, Pallas kernels: none -> 323 us  [the longest x1 99.8 us: gather_call(): pl.pallas_call(functools.partial(gather_kernel, n_row, n_col, shapes), na...]
    dot_general x76 -> x0, matrix products: 171 us -> none  [the longest x8 22.7 us: window_scores(): jnp.einsum('ihc,jhc->hij', queries, keys_w, preferred_element_type=jnp.fl...]
    all_gather x7 -> x0, waiting for transfers between devices: 105 us -> none  [the longest x1 63 us: on_device(): lax.all_gather(qkv_weight, ('row', 'col'), axis=1, tiled=True)]
    psum x2 -> x0, blocking collectives: 79.2 us -> none  [the longest x1 40.1 us: on_device(): square_totals = lax.psum(squares, ('row', 'col'))]
    ppermute x8 -> x0, waiting for transfers between devices: 54.6 us -> none  [the longest x4 36.9 us: extended(): lax.ppermute(lax.slice_in_dim(block, block.shape[dim] - width, None, axis...]
    convert_element_type x5 -> x0, local copies, waits for them, and re-layouts: 50.8 us -> none  [the longest x4 50.7 us: attend_back(): rows_sum = jnp.sum(grad_five, axis=4, dtype=jnp.float32)]
  transfers between devices with their start and end apart: 23 -> 0, of which waited for: 14 -> 0; matrix products, arithmetic and copies ran while one was open for 55% -> 0% of each run, Pallas kernels for 0% -> 0%
where the time goes in v1:
time: 362 us; the launch traced here: 360 us
  Pallas kernels  323 us (89%)
  local copies, waits for them, and re-layouts  34 us (9%)
    pallas_call x1, Pallas kernels, gather_call(): pl.pallas_call(functools.partial(gather_kernel, n_row, n_col, shapes), na...  99.8 us
    pallas_call x1, Pallas kernels, reduce_call(): pl.pallas_call(functools.partial(reduce_kernel, n_row, n_col, shapes), na...  93 us
    pallas_call x1, Pallas kernels, attend_back_call(): pl.pallas_call(functools.partial(attend_back_kernel, n_row, n_col), name=...  52.6 us
    pallas_call x1, Pallas kernels, attend_call(): pl.pallas_call(functools.partial(attend_kernel, n_row, n_col), name='atte...  32.9 us
    pallas_call x1, Pallas kernels, mlp_call(): pl.pallas_call(mlp_kernel, name='mlp', out_shape=[jax.ShapeDtypeStruct((T...  24.1 us
    unnamed x28, local copies, waits for them, and re-layouts  21.9 us
    pallas_call x1, Pallas kernels, halo_call(): pl.pallas_call(functools.partial(halo_kernel, n_row, n_col), name='halo',...  21.1 us

profile of v1, /device:TPU:0, one launch (start us, length us, event | category | flops | bytes accessed | tf_op | source)
XLA Modules:
  0.0 360.2 jit_solution(1840586022282900235)
XLA Ops:
  9.0 0.9 copy.42.w1
  9.9 1.0 copy.41.w0
  11.0 1.0 copy.43.w2
  12.0 1.1 copy.44.w3
  13.2 1.0 copy-done.5
  14.2 1.0 copy-done.6
  15.1 99.8 %gather.1 = (bf16[1184,768]{1,0:T(8,128)(2,1)S(1)}, bf16[2304,768]{1,0:T(8,128)(2,1)S(1)}, bf16[768,768]{1,0:T(8,128)(2,1)S(1)}, bf16[3072,768]{1,0:T(8,128)(2,1)S(1)}, bf16[768,3072]{1,0:T(8,128)(2,1)}) custom-call(bf16[256,768]{1,0:T(8,128)(2,1)S(1)} %bitcast.6, f32[16,768]{1,0:T(8,128)S(1)} %pad_convert_fusion.vecs, bf16[640,256]{1,0:T(8,128)(2,1)S(1)} %copy-done.6, ...), custom_call_target="tpu_custom_call" | custom-call | tf_op jit(solution)/shard_map/gather/pallas_call | solution.py:419
  115.0 1.8 copy-done
  116.8 1.2 copy-done.1
  118.0 1.0 copy-done.3
  119.0 2.2 copy-done.4
  121.2 32.9 %attend.1 = (bf16[1024,2304]{1,0:T(8,128)(2,1)}, bf16[48,224,256]{2,1,0:T(8,128)(2,1)}, bf16[256,768]{1,0:T(8,128)(2,1)}, bf16[256,768]{1,0:T(8,128)(2,1)}) custom-call(bf16[1184,768]{1,0:T(8,128)(2,1)} %copy-done.1, bf16[2304,768]{1,0:T(8,128)(2,1)} %copy-done, bf16[768,768]{1,0:T(8,128)(2,1)} %copy-done.3, f32[16,768]{1,0:T(8,128)} %copy-done.8, ...), custom_call_target="tpu_custom_call" | custom-call | tf_op jit(solution)/shard_map/attend/pallas_call | solution.py:755
  154.0 24.1 %mlp.1 = (bf16[256,768]{1,0:T(8,128)(2,1)}, f32[256,768]{1,0:T(8,128)}, bf16[256,768]{1,0:T(8,128)(2,1)}, bf16[3072,768]{1,0:T(8,128)(2,1)}, bf16[768,3072]{1,0:T(8,128)(2,1)}, /*index=5*/f32[16,768]{1,0:T(8,128)}) custom-call(bf16[256,768]{1,0:T(8,128)(2,1)} %bitcast.4, bf16[256,768]{1,0:T(8,128)(2,1)} %get-tuple-element.45.attended, ...), custom_call_target="tpu_custom_call" | custom-call | tf_op jit(solution)/shard_map/mlp/pallas_call | solution.py:834
  178.1 1.0 copy-done.9
  179.1 21.1 %halo.1.gfield = bf16[1184,768]{1,0:T(8,128)(2,1)S(1)} custom-call(bf16[256,768]{1,0:T(8,128)(2,1)S(1)} %copy-done.9, bf16[640,256]{1,0:T(8,128)(2,1)S(1)} %copy-done.7), custom_call_target="tpu_custom_call" | custom-call | tf_op jit(solution)/shard_map/halo/pallas_call | solution.py:449
  200.2 1.2 copy-done.2
  201.5 52.6 %attend_back.1 = (bf16[256,768]{1,0:T(8,128)(2,1)}, bf16[2304,768]{1,0:T(8,128)(2,1)}, bf16[768,768]{1,0:T(8,128)(2,1)}, f32[32,768]{1,0:T(8,128)}) custom-call(bf16[1184,768]{1,0:T(8,128)(2,1)} %copy-done.2, bf16[1184,768]{1,0:T(8,128)(2,1)} %copy-done.1, bf16[256,768]{1,0:T(8,128)(2,1)} %bitcast.5, f32[256,768]{1,0:T(8,128)} %get-tuple-element.50.grad_middle, ...), custom_call_target="tpu_custom_call" | custom-call | tf_op jit(solution)/shard_map/attend_back/pallas_call | solution.py:973
  254.0 93.0 %reduce.17 = (f32[384,144]{1,0:T(8,128)}, f32[384,48]{1,0:T(8,128)}, f32[384,192]{1,0:T(8,128)}, f32[1536,48]{1,0:T(8,128)}, f32[32,768]{1,0:T(8,128)}) custom-call(f32[32,768]{1,0:T(8,128)} %get-tuple-element.56.small, bf16[2304,768]{1,0:T(8,128)(2,1)} %get-tuple-element.57.g0, bf16[768,768]{1,0:T(8,128)(2,1)} %get-tuple-element.58.g1, ...), custom_call_target="tpu_custom_call" | custom-call | tf_op jit(solution)/shard_map/reduce/pallas_call | solution.py:650
  347.0 1.8 copy.45
  348.8 1.2 multiply_sqrt_fusion
  351.4 1.7 slice_reduce_fusion
  354.6 1.7 copy.46
  356.2 1.9 copy.47
  358.1 2.1 copy.48
  (32 shorter events, 11.2 us)
Async XLA Ops:
  9.0 112.2 %copy-start.8 = (f32[16,768]{1,0:T(8,128)}, f32[16,768]{1,0:T(8,128)S(1)}, u32[]{:S(2)}) copy-start(f32[16,768]{1,0:T(8,128)S(1)} %pad_convert_fusion.vecs) | copy-start | bytes 147460
  13.1 1.0 copy-start.5
  14.1 1.0 copy-start.6
  115.0 1.8 copy-start
  116.8 1.2 copy-start.1
  118.0 1.0 copy-start.3
  119.0 2.2 copy-start.4
  154.0 24.1 %copy-start.7 = (bf16[640,256]{1,0:T(8,128)(2,1)S(1)}, bf16[640,256]{1,0:T(8,128)(2,1)}, u32[]{:S(2)}) copy-start(bf16[640,256]{1,0:T(8,128)(2,1)} %constant.20.clone.pick) | copy-start | bytes 983044
  178.1 1.0 copy-start.9
  200.2 1.2 copy-start.2

commit v2 on v0

v2 whole, which is shorter than its diff:
```python
import functools
import types

import jax
import jax.numpy as jnp
import numpy as np
from jax import lax
from jax.experimental import pallas as pl
from jax.experimental.pallas import tpu as pltpu
from jax.sharding import PartitionSpec as P

HEADS = 12
HEAD = 64
WIN = 14
EPS = 1e-06
MESH = pl.DeviceIdType.MESH
AXES = ("row", "col")
F32 = jnp.float32
BF = jnp.bfloat16

D = HEADS * HEAD
TILE = 16
TOK = TILE * TILE
LO = 6
SLOT = 256
PAIRS = HEADS // 2
FIELD = 496
PICKED = 144
MIB = 2**20

LINKS = {
    (1, 0): (True, 160, 96, 256),
    (0, 1): (False, 0, 96, 352),
    (1, 1): (False, 96, 48, 448),
}


def nt(a, b):
    return lax.dot_general(a, b, (((1,), (1,)), ((), ())), preferred_element_type=F32)


def nn(a, b):
    return lax.dot_general(a, b, (((1,), (0,)), ((), ())), preferred_element_type=F32)


def tn(a, b):
    return lax.dot_general(a, b, (((0,), (0,)), ((), ())), preferred_element_type=F32)


def pick_rows():
    table = np.zeros((PICKED, TOK), np.float32)
    for base, first in ((0, 0), (96, TILE - LO)):
        for i in range((TILE - first) * LO):
            y, x = divmod(i, LO)
            table[base + i, (first + y) * TILE + TILE - LO + x] = 1.0
    return table


def table_places(back):
    place = np.zeros((256, 64), np.float32)
    for head in range(2):
        for r in range(2 * WIN - 1):
            for copy in range(2):
                row_lane = (64 + 28 * copy + r + 64 * head) % 128
                col_lane = (28 * copy + r + 64 * head) % 128
                place[128 * head + row_lane, 26 - r] = 1.0
                place[128 * head + col_lane, 32 + (r if back else 26 - r)] = 1.0
    return place


def key_marks(back):
    marks = np.zeros((2, SLOT, 128), np.float32)
    for head in range(2):
        for j in range(SLOT):
            k, l = divmod(j, 16)
            if k < WIN and l < WIN:
                for copy in range(2):
                    marks[head, j, (64 + 28 * copy + k + 64 * head) % 128] = 1.0
                    marks[head, j, (78 + 28 * copy + (13 - l if back else l) + 64 * head) % 128] = 1.0
            else:
                marks[head, j, (120 + 64 * head) % 128] = -1e30
    return marks


def lane_kinds(rows):
    lane = lax.broadcasted_iota(jnp.int32, (rows, 128), 1)
    kinds = []
    for head in range(2):
        at = (lane + 64 * head) % 128 if head else lane
        own = at < 64
        first = (at >= 64) & (at < 92)
        second = (at >= 92) & (at < 120)
        is_row = ((at >= 64) & (at < 78)) | ((at >= 92) & (at < 106))
        kinds.append((own, first, second, is_row, at == 120))
    return kinds


def window_index(w, row, col, n_row, n_col):
    place = lax.broadcasted_iota(jnp.int32, (SLOT, 1), 0)
    y = place // 16
    x = place - 16 * y
    a, b = w // 2, w % 2
    ry = WIN * (row + a) + y - TILE * row
    rx = WIN * (col + b) + x - TILE * col
    good = (y < WIN) & (x < WIN) & (ry < TILE) & (rx < TILE)
    if a:
        good = good & (row == n_row - 1)
    if b:
        good = good & (col == n_col - 1)
    up, left = ry < 0, rx < 0
    base = jnp.where(up, jnp.where(left, 448, 256), jnp.where(left, 352, 0))
    width = jnp.where(left, LO, TILE)
    index = base + jnp.where(up, ry + LO, ry) * width + jnp.where(left, rx + LO, rx)
    return jnp.where(good, index, -1)


def field_slots(row, col, n_row, n_col):
    at = lax.broadcasted_iota(jnp.int32, (FIELD, 1), 0)
    above = (at >= 256) & (at < 352)
    left = (at >= 352) & (at < 448)
    corner = at >= 448
    narrow = left | corner
    rest = jnp.where(corner, at - 448, jnp.where(left, at - 352, jnp.where(above, at - 256, at)))
    sixth = sum((rest >= LO * k).astype(jnp.int32) for k in range(1, TILE))
    ty = jnp.where(narrow, sixth, rest // TILE)
    tx = rest - ty * jnp.where(narrow, LO, TILE)
    ty = jnp.where(above | corner, ty - LO, ty)
    tx = jnp.where(narrow, tx - LO, tx)
    good = at < 484
    where = 0
    for t, place, n, stride, unit in ((ty, row, n_row, 2, 16), (tx, col, n_col, 1, 1)):
        y = TILE * place + t - WIN * place
        late = y >= WIN
        good = good & (y >= 0) & (jnp.logical_not(late) | (place == n - 1))
        where = where + jnp.where(late, stride * SLOT + unit * (y - WIN), unit * y)
    return jnp.where(good, where, -1)


def home_index(row, col, n_row, n_col):
    place = lax.broadcasted_iota(jnp.int32, (TOK, 1), 0)
    ty = place // TILE
    tx = place - TILE * ty
    down = (TILE * row + ty - WIN * row >= WIN) & (row < n_row - 1)
    right = (TILE * col + tx - WIN * col >= WIN) & (col < n_col - 1)
    near = TILE - LO
    return jnp.where(
        down,
        jnp.where(right, 448 + (ty - near) * LO + tx - near, 256 + (ty - near) * TILE + tx),
        jnp.where(right, 352 + ty * LO + tx - near, place),
    )


def one_hot(index, size):
    lane = lax.broadcasted_iota(jnp.int32, (index.shape[0], size), 1)
    return jnp.where(lane == index, 1.0, 0.0).astype(BF)


def norm(v, gain, bias):
    mean = jnp.mean(v, -1, keepdims=True)
    center = v - mean
    inverse = lax.rsqrt(jnp.mean(center * center, -1, keepdims=True) + EPS)
    xhat = center * inverse
    return xhat * gain + bias, xhat, inverse


def norm_back(grad, xhat, inverse, gain):
    d = grad * gain
    return inverse * (
        d - jnp.mean(d, -1, keepdims=True) - xhat * jnp.mean(d * xhat, -1, keepdims=True)
    )


def grid_place():
    return lax.axis_index("dp"), lax.axis_index("row"), lax.axis_index("col")


def exists(step, row, col, n_row, n_col):
    r, c = row + step[0], col + step[1]
    return (r >= 0) & (r < n_row) & (c >= 0) & (c < n_col)


CORNERS = ((1, 1), (-1, -1))


def greet(n_row, n_col):
    dp, row, col = grid_place()
    barrier = pltpu.get_barrier_semaphore()
    others = [(dp, row, lax.rem(col + d, n_col)) for d in (1, 2, 3)]
    others += [(dp, lax.rem(row + d, n_row), col) for d in (1, 2, 3)]
    others.append((1 - dp, row, col))
    for other in others:
        pl.semaphore_signal(barrier, inc=1, device_id=other, device_id_type=MESH)
    count = len(others)
    for step in CORNERS:
        there = exists(step, row, col, n_row, n_col)

        @pl.when(there)
        def _():
            pl.semaphore_signal(
                barrier, inc=1, device_id=(dp, row + step[0], col + step[1]), device_id_type=MESH
            )

        count = count + jnp.where(there, 1, 0)
    pl.semaphore_wait(barrier, count)


class Halo:
    def __init__(self, source, picked, land, back, send, recv, n_row, n_col):
        self.source, self.picked, self.land, self.back = source, picked, land, back
        self.send, self.recv, self.size = send, recv, (n_row, n_col)

    def copies(self):
        dp, row, col = grid_place()
        sign = -1 if self.back else 1
        for i, ((dr, dc), (own, first, rows, there)) in enumerate(LINKS.items()):
            if self.back:
                src = self.source.at[pl.ds(there, rows)]
            else:
                src = (self.source if own else self.picked).at[pl.ds(first, rows)]
            copy = pltpu.make_async_remote_copy(
                src,
                self.land.at[pl.ds(there, rows)],
                self.send.at[i],
                self.recv.at[i],
                device_id=(dp, row + sign * dr, col + sign * dc),
                device_id_type=MESH,
            )
            goes = exists((sign * dr, sign * dc), row, col, *self.size)
            comes = exists((-sign * dr, -sign * dc), row, col, *self.size)
            yield copy, goes, comes

    def start(self):
        for copy, goes, _ in self.copies():
            pl.when(goes)(copy.start)

    def wait(self):
        for copy, goes, comes in self.copies():
            pl.when(goes)(copy.wait_send)
            pl.when(comes)(copy.wait_recv)


def pick_start(halo, pick):
    halo.picked[...] = nn(pick[...], halo.source[pl.ds(0, TOK), :]).astype(BF)
    halo.start()


def halo_xla(blocks, back, n_row, n_col):
    sign = -1 if back else 1
    pieces = [blocks[0]]
    for (dr, dc), block in zip(LINKS, blocks[1:]):
        dr, dc = sign * dr, sign * dc
        pairs = [
            (r * n_col + c, (r + dr) * n_col + c + dc)
            for r in range(n_row)
            for c in range(n_col)
            if 0 <= r + dr < n_row and 0 <= c + dc < n_col
        ]
        pieces.append(lax.ppermute(block, AXES, pairs))
    return jnp.concatenate(pieces, 0)


def lend_xla(own, n_row, n_col):
    grid = own.reshape(TILE, TILE, -1)
    corner = grid[TILE - LO :, TILE - LO :].reshape(LO * LO, -1)
    blocks = [
        own,
        own[TILE * (TILE - LO) :],
        grid[:, TILE - LO :].reshape(TILE * LO, -1),
        jnp.pad(corner, ((0, 48 - LO * LO), (0, 0))),
    ]
    return halo_xla(blocks, False, n_row, n_col)


def return_xla(field, n_row, n_col):
    return halo_xla([field[:256], field[256:352], field[352:448], field[448:]], True, n_row, n_col)


def blocks_of(shapes):
    return [(n // 16, k // 2) for n, k in shapes]


def rows_at(first, count):
    return pl.ds(pl.multiple_of(first, 16), count)


LINE, OWN, OWN_CORE, LINE_CORE, FAR, NEAR_CORE, FAR_CORE, CORE = range(10, 18)


class Gather:
    SEMS = 20

    def __init__(self, full, shard, block, half, send, recv):
        self.dp, self.row, self.col = grid_place()
        self.full, self.shard, self.b = full, shard, block
        self.send, self.recv = send, recv
        self.lanes = pl.ds(pl.multiple_of(self.dp * half, 128), half)
        self.other = pl.ds(pl.multiple_of((1 - self.dp) * half, 128), half)

    def block(self, flip, place):
        return (jnp.bitwise_xor(self.row, flip) * 4 + place) * self.b

    def came(self, d):
        return lax.rem(self.col + 4 - d, 4)

    def copy(self, i, first, count, land, target, shard=False):
        core = target == CORE
        if core:
            device = (1 - self.dp, self.row, self.col)
        elif isinstance(target, tuple):
            device = (self.dp, self.row, lax.rem(self.col + target[0], 4))
        else:
            device = (self.dp, jnp.bitwise_xor(self.row, target), self.col)

        def make(src, dst):
            return pltpu.make_async_remote_copy(
                src, dst, self.send.at[i], self.recv.at[i], device_id=device, device_id_type=MESH
            )

        def out():
            there = self.full.at[rows_at(first, count), self.lanes]
            return make(self.shard if shard else there, there)

        def come():
            here = self.full.at[rows_at(land, count), self.other if core else self.lanes]
            return make(here, here)

        return out, come

    def copies(self, k):
        b = self.b
        own = self.block(0, self.col)
        if k == LINE:
            return [
                self.copy(d - 1, own, b, self.block(0, self.came(d)), (d,), True) for d in (1, 2, 3)
            ]
        if k == OWN:
            return [self.copy(2 + f, own, b, self.block(f, self.col), f, True) for f in (1, 2)]
        if k == OWN_CORE:
            return [self.copy(5, own, b, own, CORE, True)]
        if k < LINE:
            at = self.came(k)
            return [
                self.copy(4 + 2 * k, self.block(0, at), b, self.block(1, at), 1),
                self.copy(5 + 2 * k, self.block(0, at), b, self.block(2, at), 2),
            ]
        if k == LINE_CORE:
            return [
                self.copy(11 + d, self.block(0, self.came(d)), b, self.block(0, self.came(d)), CORE)
                for d in (1, 2, 3)
            ]
        if k == FAR:
            return [
                self.copy(15, self.block(2, 0), 2 * b, self.block(3, 0), 1),
                self.copy(16, self.block(1, 2), 2 * b, self.block(3, 2), 2),
            ]
        if k == NEAR_CORE:
            return [self.copy(16 + f, self.block(f, 0), 4 * b, self.block(f, 0), CORE) for f in (1, 2)]
        return [self.copy(19, self.block(3, 0), 4 * b, self.block(3, 0), CORE)]

    def start(self, *kinds):
        for k in kinds:
            for out, _ in self.copies(k):
                out().start()

    def arrive(self, *kinds):
        for k in kinds:
            for _, come in self.copies(k):
                come().wait_recv()

    def step(self, n):
        if n == 0:
            for d in (1, 2, 3):
                self.copies(LINE)[d - 1][1]().wait_recv()
                self.start(d)
            self.start(LINE_CORE)
        elif n == 1:
            self.arrive(OWN, 1, 2, 3)
            self.start(FAR, NEAR_CORE)
        else:
            self.arrive(FAR)
            self.start(FAR_CORE)

    def whole(self):
        self.arrive(OWN_CORE, LINE_CORE, NEAR_CORE, FAR_CORE)

    def finish(self):
        for k in (LINE, OWN, OWN_CORE, 1, 2, 3, LINE_CORE, FAR, NEAR_CORE, FAR_CORE):
            for out, _ in self.copies(k):
                out().wait_send()


class Reduce:
    SEMS = 30

    def __init__(self, grad, total, base, come, block, half, pieces, parts, send, recv):
        self.dp, self.row, self.col = grid_place()
        self.grad, self.total, self.base, self.come = grad, total, base, come
        self.b, self.h, self.send, self.recv = block, half, send, recv
        self.pieces, self.parts, self.width = pieces, parts, half // parts
        self.other = pl.ds(pl.multiple_of((1 - self.dp) * half, 128), half)

    def at(self, flip, place=0):
        return (jnp.bitwise_xor(self.row, flip) * 4 + place) * self.b

    def lanes(self, part):
        return pl.ds(pl.multiple_of(self.base + part * self.width, 128), self.width)

    def came(self, first, count, part):
        return self.come.at[rows_at(first, count), pl.ds(part * self.width, self.width)]

    def tot(self, first, count, part):
        return self.total.at[rows_at(first, count), self.lanes(part)]

    def sem(self, k, part):
        if k == 0:
            return part
        return self.pieces + 7 * part + {1: 0, 2: 2, 3: 4}[k]

    def copies(self, k, part):
        b = self.b
        if k == 0:
            n = 16 * b // self.pieces
            rows = rows_at(part * n, n)
            plan = [(self.grad.at[rows, self.other], self.come.at[rows], (1 - self.dp, self.row, self.col))]
        elif k == 1:
            plan = [
                (
                    self.tot(self.at(3, 2 * half), 2 * b, part),
                    self.came((16 + 2 * half) * b, 2 * b, part),
                    (self.dp, jnp.bitwise_xor(self.row, 1 + half), self.col),
                )
                for half in (0, 1)
            ]
        elif k == 2:
            plan = [
                (
                    self.tot(self.at(flip), 4 * b, part),
                    self.came((16 + 4 * flip) * b, 4 * b, part),
                    (self.dp, jnp.bitwise_xor(self.row, flip), self.col),
                )
                for flip in (1, 2)
            ]
        else:
            plan = []
            for d in (1, 2, 3):
                to = lax.rem(self.col + d, 4)
                plan.append(
                    (
                        self.tot(self.at(0, to), b, part),
                        self.came((27 + d) * b, b, part),
                        (self.dp, self.row, to),
                    )
                )
        base = self.sem(k, part)
        return [
            pltpu.make_async_remote_copy(
                src, dst, self.send.at[base + i], self.recv.at[base + i], device_id=dev, device_id_type=MESH
            )
            for i, (src, dst, dev) in enumerate(plan)
        ]

    def start(self, k, part=0):
        for copy in self.copies(k, part):
            copy.start()

    def arrive(self, k, part=0):
        for copy in self.copies(k, part):
            copy.wait_recv()

    def sum_rows(self, first, count, froms, part):
        steps = (96, 64, 48, 32, 16) if self.width <= 384 else (32, 16)
        step = next(s for s in steps if count % s == 0)
        lanes = self.lanes(part)
        side = pl.ds(part * self.width, self.width)

        def body(i, _):
            at = rows_at(first + i * step, step)
            value = self.total[at, lanes]
            if len(froms) == 1:
                value = value + self.come[rows_at(froms[0] + i * step, step), side]
            else:
                value = value.astype(F32)
                for f in froms:
                    value = value + self.come[rows_at(f + i * step, step), side].astype(F32)
                value = value.astype(BF)
            self.total[at, lanes] = value
            return 0

        lax.fori_loop(0, count // step, body, 0)

    def add_piece(self, piece):
        n = 16 * self.b // self.pieces
        self.arrive(0, piece)
        for part in range(self.parts):
            self.sum_rows(piece * n, n, (piece * n,), part)

    def step(self, k, part=0):
        b = self.b
        if k == 0:
            for piece in range(self.pieces):
                self.add_piece(piece)
            for part in range(1, self.parts):
                self.start(1, part)
            part = 0
        else:
            self.arrive(k, part)
            if k == 1:
                self.sum_rows(self.at(2), 2 * b, (16 * b,), part)
                self.sum_rows(self.at(1, 2), 2 * b, (18 * b,), part)
            else:
                self.sum_rows(self.at(0), 4 * b, (20 * b, 24 * b), part)
        self.start(k + 1, part)

    def result(self, out, part=0):
        b = self.b
        self.arrive(3, part)
        value = self.total[rows_at(self.at(0, self.col), b), self.lanes(part)].astype(F32)
        side = pl.ds(part * self.width, self.width)
        for d in (1, 2, 3):
            value = value + self.come[pl.ds((27 + d) * b, b), side].astype(F32)
        out[:, side] = value

    def finish(self):
        for piece in range(self.pieces):
            self.copies(0, piece)[0].wait_send()
        for part in range(self.parts):
            for k in (1, 2, 3):
                for copy in self.copies(k, part):
                    copy.wait_send()


def vmem():
    return pl.BlockSpec(memory_space=pltpu.VMEM)


def hbm():
    return pl.BlockSpec(memory_space=pl.ANY)


def dma(*n):
    return pltpu.SemaphoreType.DMA(n)


def named_call(body, ins, outs, scratch, name, **params):
    names = [*ins, *outs, *scratch]

    def kernel(*refs):
        body(types.SimpleNamespace(**dict(zip(names, refs))))

    result = pl.pallas_call(
        kernel,
        name=name,
        out_shape=[shape for shape, _ in outs.values()],
        in_specs=[spec for _, spec in ins.values()],
        out_specs=[spec for _, spec in outs.values()],
        scratch_shapes=list(scratch.values()),
        compiler_params=pltpu.CompilerParams(**params),
    )(*[array for array, _ in ins.values()])
    return types.SimpleNamespace(**dict(zip(outs, result)))


def vector(ref):
    return ref[...].astype(F32).reshape(1, -1)


def joint_table(rel_rows, rel_cols):
    parts = [rel_rows[...], jnp.zeros((5, HEAD), BF), rel_cols[...], jnp.zeros((5, HEAD), BF)]
    table = jnp.concatenate([p.astype(F32) for p in parts], 0)
    return jnp.concatenate([table, table], 1).astype(BF)


def table_kernel_value(places, table):
    value = nn(places, table)
    line = lax.broadcasted_iota(jnp.int32, value.shape, 0)
    lane = lax.broadcasted_iota(jnp.int32, value.shape, 1)
    return jnp.where((line < 128) == (lane < 64), value, 0.0).astype(BF)


def spread(a, back):
    rows, cols = [], []
    for y in range(a.shape[0] // 16):
        part = a[16 * y : 16 * y + 16, :]
        rows.append(pltpu.roll(part, 13 - y if back else (115 + y) % 128, 1))
        cols.append(pltpu.roll(part, 50 if back else 65, 1, stride=1, stride_axis=0))
    return jnp.concatenate(rows, 0), jnp.concatenate(cols, 0)


def pair_place(w, pair):
    return pl.multiple_of(w * SLOT, SLOT), pl.multiple_of(pair * 128, 128)


def attend_pair(w, pair, n, qkv, table, marks, masks, probs, mixed):
    r0, l0 = pair_place(w, pair)
    q2 = qkv[pl.ds(r0, n), pl.ds(l0, 128)]
    k2 = qkv[pl.ds(r0, SLOT), pl.ds(D + l0, 128)]
    v2 = qkv[pl.ds(r0, SLOT), pl.ds(2 * D + l0, 128)]
    a2 = nt(q2, table[...])
    qf = q2.astype(F32) * HEAD**-0.5
    kinds = lane_kinds(n)
    outs = []
    for head in range(2):
        own, first, second, is_row, one = kinds[head]
        rows, cols = spread(a2[:, 128 * head : 128 * head + 128], False)
        bias = jnp.where(is_row, rows, cols)
        high = bias.astype(BF).astype(F32)
        low = jnp.where(second, bias - high, jnp.where(one, 1.0, 0.0))
        aug = jnp.where(own, qf, jnp.where(first, high, low)).astype(BF)
        keys = k2 * masks[head : head + 1, :] + marks[head]
        scores = nt(aug, keys)
        top = jnp.max(scores, -1, keepdims=True)
        e = jnp.exp(scores - top)
        p = (e * (1.0 / jnp.sum(e, -1, keepdims=True))).astype(BF)
        probs[w * HEADS + 2 * pair + head, 0:n, :] = p
        outs.append(nn(p, v2))
    mixed[pl.ds(r0, n), pl.ds(l0, 128)] = jnp.where(kinds[0][0], outs[0], outs[1]).astype(BF)


def attend_back_pair(w, pair, n, qkv, gmix, probs, table, marks, masks, dqkv, gtab):
    r0, l0 = pair_place(w, pair)
    scale = HEAD**-0.5
    q2 = qkv[pl.ds(r0, n), pl.ds(l0, 128)]
    k2 = qkv[pl.ds(r0, SLOT), pl.ds(D + l0, 128)]
    v2 = qkv[pl.ds(r0, SLOT), pl.ds(2 * D + l0, 128)]
    g2 = gmix[pl.ds(r0, n), pl.ds(l0, 128)]
    kinds = lane_kinds(n)
    dq, dk, dv = [], [], []
    for head in range(2):
        own, first, second, is_row, one = kinds[head]
        mask = masks[head : head + 1, :]
        p = probs[w * HEADS + 2 * pair + head, 0:n, :]
        pf = p.astype(F32)
        dp = nt(g2, v2 * mask)
        ds = (pf * (dp - jnp.sum(pf * dp, -1, keepdims=True))).astype(BF)
        keys = k2 * (mask * jnp.asarray(scale, BF)) + marks[head]
        dqa = nn(ds, keys)
        marked = jnp.where(first | second, dqa, 0.0)
        rows, _ = spread(jnp.where(is_row, marked, 0.0), True)
        _, cols = spread(jnp.where(is_row, 0.0, marked), True)
        back = rows + cols
        at = lax.broadcasted_iota(jnp.int32, (n, 128), 1)
        if head:
            at = (at + 64) % 128
        high = back.astype(BF).astype(F32)
        split = jnp.where((at < 28) | ((at >= 64) & (at < 92)), high, back - high).astype(BF)
        extra = nn(split, table[128 * head : 128 * head + 128, :])
        dq.append(dqa + extra)
        gtab[head] += tn(split, q2)
        dk.append(tn(ds, q2))
        dv.append(tn(p, g2))
    wide = lane_kinds(SLOT)[0][0]
    dqkv[pl.ds(r0, n), pl.ds(l0, 128)] = jnp.where(kinds[0][0], dq[0], dq[1]).astype(BF)
    dqkv[pl.ds(r0, SLOT), pl.ds(D + l0, 128)] = (jnp.where(wide, dk[0], dk[1]) * scale).astype(BF)
    dqkv[pl.ds(r0, SLOT), pl.ds(2 * D + l0, 128)] = jnp.where(wide, dv[0], dv[1]).astype(BF)


def over_windows(body, hooks, n_row, n_col):
    _, row, col = grid_place()
    for a, n in ((0, 16 * WIN), (1, 16 * (TILE * n_row - WIN * n_row))):

        def step(i, _):
            b = i // PAIRS
            good = (b == 0) | (col == n_col - 1)
            if a:
                good = good & (row == n_row - 1)

            @pl.when(good)
            def _():
                body(2 * a + b, lax.rem(i, PAIRS), n)

            for when, hook in hooks:
                if when // (2 * PAIRS) == a:
                    pl.when(i == when % (2 * PAIRS))(hook)
            return 0

        lax.fori_loop(0, 2 * PAIRS, step, 0)


def attend_part(r, n_row, n_col, hooks, between):
    _, row, col = grid_place()
    biases = (vector(r.query_bias), None, vector(r.value_bias))
    for part, bias in enumerate(biases):
        for n in range(3):
            at = part * D + 256 * n
            value = nt(r.xw[...], r.wqkv[pl.ds(at, 256), :])
            if bias is not None:
                value = value + bias[:, 256 * n : 256 * n + 256]
            r.qkv[:, pl.ds(at, 256)] = value.astype(BF)
        between(part)

    def body(w, pair, n):
        attend_pair(w, pair, n, r.qkv, r.table, r.marks, r.masks, r.probs, r.mixed)

    over_windows(body, hooks, n_row, n_col)
    hot = one_hot(field_slots(row, col, n_row, n_col), 4 * SLOT)
    r.ret[...] = nn(hot, r.mixed[...]).astype(BF)


def cut_windows(source, land, n_row, n_col, w):
    _, row, col = grid_place()
    hot = one_hot(window_index(w, row, col, n_row, n_col), FIELD)
    land[pl.ds(w * SLOT, SLOT), :] = nn(hot, source[...]).astype(BF)


def mlp_first(r, n_row, n_col, hidden):
    _, row, col = grid_place()
    hot = one_hot(home_index(row, col, n_row, n_col), FIELD)
    r.mixed_own[...] = nn(hot, r.home[...]).astype(BF)
    r.attended[...] = (nt(r.mixed_own[...], r.wproj[...]) + vector(r.proj_bias)).astype(BF)
    middle = r.tokens[...].astype(F32) + r.attended[...].astype(F32)
    r.n2[...] = norm(middle, vector(r.ln2_gain), vector(r.ln2_bias))[0].astype(BF)
    up_bias = vector(r.fc1_bias)
    for line in range(hidden // D):
        r.up_bias[line : line + 1, :] = up_bias[:, line * D : line * D + D]

    def chunk(j, _):
        at = pl.multiple_of(j * 256, 256)
        lane = pl.multiple_of(lax.rem(j, 3) * 256, 256)
        u = nt(r.n2[...], r.w1[pl.ds(at, 256), :]) + r.up_bias[pl.ds(j // 3, 1), pl.ds(lane, 256)]
        cdf = 0.5 * (1.0 + lax.erf(u * 0.7071067811865476))
        r.act[:, pl.ds(at, 256)] = (u * cdf).astype(BF)
        r.slope[:, pl.ds(at, 256)] = cdf + u * (jnp.exp(-0.5 * u * u) * 0.3989422804014327)
        return 0

    lax.fori_loop(0, hidden // 256, chunk, 0)


def mlp_second(r, hidden):
    r.gn2[...] = jnp.zeros_like(r.gn2)
    r.small[...] = jnp.zeros_like(r.small)

    def chunk(j, _):
        at = pl.multiple_of(j * 256, 256)
        lane = pl.multiple_of(lax.rem(j, 3) * 256, 256)
        gu = (nn(r.cot[...], r.w2[:, pl.ds(at, 256)]) * r.slope[:, pl.ds(at, 256)]).astype(BF)
        r.gu[:, pl.ds(at, 256)] = gu
        r.gn2[...] += nn(gu, r.w1[pl.ds(at, 256), :])
        r.small[pl.ds(8 + j // 3, 1), pl.ds(lane, 256)] = jnp.sum(gu.astype(F32), 0, keepdims=True)
        return 0

    lax.fori_loop(0, hidden // 256, chunk, 0)
    gain = vector(r.ln2_gain)
    middle = r.tokens[...].astype(F32) + r.attended[...].astype(F32)
    _, xhat, inverse = norm(middle, gain, vector(r.ln2_bias))
    grad = r.gn2[...]
    cf = r.cot[...].astype(F32)
    gm = cf + norm_back(grad, xhat, inverse, gain)
    r.grad_middle[...] = gm
    low = gm.astype(BF)
    r.gfield[pl.ds(0, TOK), :] = low
    r.small[4:5, :] = jnp.sum(low.astype(F32), 0, keepdims=True)
    r.small[5:6, :] = jnp.sum(grad * xhat, 0, keepdims=True)
    r.small[6:7, :] = jnp.sum(grad, 0, keepdims=True)
    r.small[7:8, :] = jnp.sum(cf, 0, keepdims=True)


def mlp_last(r, hidden):
    r.branch[...] = jnp.zeros_like(r.branch)

    def chunk(j, _):
        at = pl.multiple_of(j * 256, 256)
        r.branch[...] += nt(r.act[:, pl.ds(at, 256)], r.w2[:, pl.ds(at, 256)])
        return 0

    lax.fori_loop(0, hidden // 256, chunk, 0)
    att = r.attended[...].astype(F32)
    tok = r.tokens[...].astype(F32)
    middle = tok + att
    br = r.branch[...] + vector(r.fc2_bias)
    result = middle + br
    r.output[...] = result.astype(BF)
    lane = lax.broadcasted_iota(jnp.int32, (1, D), 1)
    stats = jnp.zeros((1, D), F32)
    for n, v in enumerate((tok, middle, result, att, br)):
        total = jnp.sum(jnp.sum(v * v, 0, keepdims=True), 1, keepdims=True)
        stats = jnp.where(lane == n, total, stats)
    r.small[12:13, :] = stats


UP_PIECES, DOWN_PIECES = 12, 6


def mlp_weights(r, hidden, up_sent, down_sent):
    r.cot_t[...] = r.cot[...].T

    def up(j, _):
        n = hidden // UP_PIECES
        at = pl.multiple_of(j * n, n)
        r.g1[pl.ds(at, n), :] = tn(r.gu[:, pl.ds(at, n)], r.n2[...]).astype(BF)
        up_sent(j)
        return 0

    def down(j, _):
        n = D // DOWN_PIECES
        at = pl.multiple_of(j * n, n)
        r.g2[pl.ds(at, n), :] = nn(r.cot_t[pl.ds(at, n), :], r.act[...]).astype(BF)
        down_sent(j)
        return 0

    lax.fori_loop(0, UP_PIECES, up, 0)
    lax.fori_loop(0, DOWN_PIECES, down, 0)


def proj_weight_grad(r):
    def chunk(n, _):
        at = pl.multiple_of(n * 256, 256)
        r.gproj[pl.ds(at, 256), :] = tn(r.gfield[pl.ds(0, TOK), pl.ds(at, 256)], r.mixed_own[...]).astype(BF)
        return 0

    lax.fori_loop(0, D // 256, chunk, 0)


def prepare(r):
    r.table[...] = table_kernel_value(r.places[...], joint_table(r.rel_rows, r.rel_cols))
    r.mixed[...] = jnp.zeros_like(r.mixed)


def front_body(n_row, n_col, shapes, hidden, r):
    rest = FIELD - TOK
    for ref in (r.field, r.gfield, r.home):
        ref[pl.ds(TOK, rest), :] = jnp.zeros((rest, D), BF)
    greet(n_row, n_col)
    ways = [
        Gather(full, shard, b, h, send, recv)
        for full, shard, (b, h), send, recv in zip(
            (r.wqkv, r.wproj, r.w1, r.w2),
            (r.s0, r.s1, r.s2, r.s3),
            blocks_of(shapes),
            (r.p0, r.p1, r.p2, r.p3),
            (r.r0, r.r1, r.r2, r.r3),
        )
    ]
    qkv_way, proj_way, up_way, down_way = ways
    qkv_way.start(LINE, OWN, OWN_CORE)
    normed, _, _ = norm(r.tokens[...].astype(F32), vector(r.ln1_gain), vector(r.ln1_bias))
    r.field[pl.ds(0, TOK), :] = normed.astype(BF)
    lend = Halo(r.field, r.picked, r.field, False, r.lend_sem.at[0], r.lend_sem.at[1], n_row, n_col)
    give = Halo(r.ret, None, r.home, True, r.give_sem.at[0], r.give_sem.at[1], n_row, n_col)
    glend = Halo(r.gfield, r.gpicked, r.gfield, False, r.glend_sem.at[0], r.glend_sem.at[1], n_row, n_col)
    pick_start(lend, r.pick)
    local = []
    for i, way in enumerate(ways):
        if i:
            way.start(OWN, OWN_CORE)
        own = way.full.at[rows_at(way.block(0, way.col), way.b), way.lanes]
        mine = pltpu.make_async_copy(way.shard, own, r.local_sem.at[i])
        mine.start()
        local.append(mine)
    prepare(r)
    for mine in local:
        mine.wait()
    lend.wait()
    for w in range(4):
        cut_windows(r.field, r.xw, n_row, n_col, w)
    qkv_way.step(0)
    proj_way.start(LINE)
    up_way.start(LINE)
    qkv_way.step(1)
    proj_way.step(0)
    qkv_way.step(2)
    down_way.start(LINE)
    up_way.step(0)
    qkv_way.whole()
    out_copies = [
        pltpu.make_async_copy(src, dst, r.out_sem.at[i])
        for i, (src, dst) in enumerate(
            [
                (r.qkv, r.qkv_out),
                (r.wqkv, r.wqkv_out),
                (r.probs, r.probs_out),
                (r.wproj, r.wproj_out),
                (r.xw, r.xw_out),
                (r.act, r.act_out),
                (r.gu, r.gu_out),
            ]
        )
    ]

    def between(part):
        if part == 0:
            proj_way.step(1)
        elif part == 2:
            out_copies[0].start()
            out_copies[1].start()
            out_copies[4].start()

    hooks = (
        (0, lambda: proj_way.step(2)),
        (1, lambda: down_way.step(0)),
        (3, lambda: up_way.step(1)),
        (11, lambda: up_way.step(2)),
        (14, lambda: down_way.step(1)),
    )
    attend_part(r, n_row, n_col, hooks, between)
    give.start()
    out_copies[2].start()
    r.home[pl.ds(0, TOK), :] = r.ret[pl.ds(0, TOK), :]
    proj_way.whole()
    out_copies[3].start()
    down_way.step(2)
    up_way.whole()
    give.wait()
    mlp_first(r, n_row, n_col, hidden)
    out_copies[5].start()
    down_way.whole()
    mlp_second(r, hidden)
    pick_start(glend, r.pick)
    out_copies[6].start()
    mlp_last(r, hidden)
    glend.wait()
    for way in ways:
        way.finish()
    for copy in out_copies:
        copy.wait()


def split_ins(tensors, *names):
    return {k: (tensors[k], vmem()) for k in names}


def forward_buffers(shapes, hidden):
    v = pltpu.VMEM
    first = dict(
        xw=v((4 * SLOT, D), BF),
        qkv=v((4 * SLOT, 3 * D), BF),
        probs=v((4 * HEADS, 16 * WIN, SLOT), BF),
        mixed=v((4 * SLOT, D), BF),
        table=v((256, 128), BF),
        ret=v((FIELD, D), BF),
    )
    second = dict(
        attended=v((TOK, D), BF),
        act=v((TOK, hidden), BF),
        slope=v((TOK, hidden), F32),
        gu=v((TOK, hidden), BF),
        branch=v((TOK, D), F32),
        gn2=v((TOK, D), F32),
        up_bias=v((hidden // D, D), F32),
    )
    sd = jax.ShapeDtypeStruct
    results = dict(
        n2=(sd((TOK, D), BF), vmem()),
        mixed_own=(sd((TOK, D), BF), vmem()),
        gfield=(sd((FIELD, D), BF), vmem()),
        grad_middle=(sd((TOK, D), F32), vmem()),
        output=(sd((TOK, D), BF), vmem()),
        small=(sd((16, D), F32), vmem()),
    )
    return first, second, results


def as_out(buffer):
    return (jax.ShapeDtypeStruct(buffer.shape, buffer.dtype), vmem())


def front_call(n_row, n_col, shapes, tensors, shards):
    hidden = shapes[2][0]
    sd, v = jax.ShapeDtypeStruct, pltpu.VMEM
    ins = {k: (t, vmem()) for k, t in tensors.items()}
    ins |= {"s" + str(i): (w, vmem()) for i, w in enumerate(shards)}
    first, second, results = forward_buffers(shapes, hidden)
    outs = dict(
        qkv_out=(sd((4 * SLOT, 3 * D), BF), hbm()),
        probs_out=(sd((4 * HEADS, 16 * WIN, SLOT), BF), hbm()),
        wqkv_out=(sd(shapes[0], BF), hbm()),
        wproj_out=(sd(shapes[1], BF), hbm()),
        xw_out=(sd((4 * SLOT, D), BF), hbm()),
        act_out=(sd((TOK, hidden), BF), hbm()),
        gu_out=(sd((TOK, hidden), BF), hbm()),
        **results,
    )
    wqkv, wproj, w1, w2 = [v(s, BF) for s in shapes]
    scratch = dict(
        **first,
        **second,
        wqkv=wqkv,
        wproj=wproj,
        w1=w1,
        w2=w2,
        field=v((FIELD, D), BF),
        home=v((FIELD, D), BF),
        picked=v((PICKED, D), BF),
        gpicked=v((PICKED, D), BF),
        out_sem=dma(7),
        local_sem=dma(4),
        lend_sem=dma(2, 3),
        give_sem=dma(2, 3),
        glend_sem=dma(2, 3),
    )
    for i in range(4):
        scratch |= {"p" + str(i): dma(Gather.SEMS), "r" + str(i): dma(Gather.SEMS)}
    return named_call(
        functools.partial(front_body, n_row, n_col, shapes, hidden), ins, outs, scratch, "front",
        vmem_limit_bytes=63 * MIB, collective_id=0, has_side_effects=True,
    )


def front_plain(n_row, n_col, shapes, tensors, weights, field):
    hidden = shapes[2][0]
    first, second, results = forward_buffers(shapes, hidden)
    wqkv, wproj, w1, w2 = [(w, vmem()) for w in weights]
    ins = split_ins(tensors, "query_bias", "value_bias", "rel_rows", "rel_cols", "masks") | split_ins(tensors, "places", "marks")
    outs = {k: as_out(first.pop(k)) for k in ("qkv", "probs", "ret")}

    def attend_body(r):
        prepare(r)
        for w in range(4):
            cut_windows(r.field, r.xw, n_row, n_col, w)
        attend_part(r, n_row, n_col, (), lambda part: None)

    one = named_call(
        attend_body, ins | dict(field=(field, vmem()), wqkv=wqkv), outs, first, "attend", vmem_limit_bytes=60 * MIB
    )
    home = return_xla(one.ret, n_row, n_col)
    ins = split_ins(tensors, "tokens", "cot", "proj_bias", "ln2_gain", "ln2_bias", "fc1_bias", "fc2_bias")
    outs = results | dict(act=as_out(second.pop("act")), gu=as_out(second.pop("gu")))

    def mlp_body(r):
        r.gfield[...] = jnp.zeros_like(r.gfield)
        mlp_first(r, n_row, n_col, hidden)
        mlp_second(r, hidden)
        mlp_last(r, hidden)

    two = named_call(
        mlp_body, ins | dict(home=(home, vmem()), wproj=wproj, w1=w1, w2=w2), outs, second, "mlp",
        vmem_limit_bytes=60 * MIB,
    )
    two.gfield = lend_xla(two.gfield[:TOK], n_row, n_col)
    two.qkv_out, two.probs_out, two.wqkv_out, two.wproj_out = one.qkv, one.probs, *weights[:2]
    two.act_out, two.gu_out = two.act, two.gu
    return two


def back_prepare(r, n_row, n_col):
    r.table[...] = table_kernel_value(r.places[...], joint_table(r.rel_rows, r.rel_cols))
    r.small[...] = jnp.zeros_like(r.small)
    r.small[0:16, :] = r.small_in[...]
    r.gtab[...] = jnp.zeros_like(r.gtab)
    r.dqkv[...] = jnp.zeros_like(r.dqkv)
    for w in range(4):
        cut_windows(r.gfield, r.gw, n_row, n_col, w)


def back_mix(r):
    def mix(n, _):
        at = pl.multiple_of(n * 256, 256)
        r.gmix[:, pl.ds(at, 256)] = nn(r.gw[...], r.wproj[:, pl.ds(at, 256)]).astype(BF)
        return 0

    lax.fori_loop(0, 3, mix, 0)


def back_windows(r, n_row, n_col, hooks):
    def body(w, pair, n):
        attend_back_pair(w, pair, n, r.qkv, r.gmix, r.probs, r.table, r.marks, r.masks, r.dqkv, r.gtab)

    over_windows(body, hooks, n_row, n_col)


def back_weights(r, n_row, n_col, sent):
    for n in range(9):
        r.gqkv[pl.ds(256 * n, 256), :] = tn(r.dqkv[:, pl.ds(256 * n, 256)], r.xw[...]).astype(BF)
        sent(n)
    ones = jnp.ones((16, 4 * SLOT), BF)
    r.small[2:3, :] = nn(ones, r.dqkv[:, 0:D])[0:1, :]
    r.small[3:4, :] = nn(ones, r.dqkv[:, 2 * D : 3 * D])[0:1, :]
    lane = lax.broadcasted_iota(jnp.int32, (128, 128), 1)
    left = jnp.where(lane < 64, r.gtab[0], 0.0)
    right = jnp.where(lane >= 64, r.gtab[1], 0.0)
    tab = lax.dot_general(
        r.places[...].astype(F32),
        jnp.concatenate([left, right], 0),
        (((0,), (0,)), ((), ())),
        precision=lax.Precision.HIGHEST,
        preferred_element_type=F32,
    )
    for t in range(4):
        r.small[16:32, 128 * t : 128 * t + 128] = tab[16 * t : 16 * t + 16, :]


def back_return(r, n_row, n_col):
    _, row, col = grid_place()

    def chunk(w, _):
        rows = pl.ds(pl.multiple_of(w * SLOT, SLOT), SLOT)
        r.gw[rows, :] = nn(r.dqkv[rows, :], r.wqkv[...]).astype(BF)
        return 0

    lax.fori_loop(0, 4, chunk, 0)
    hot = one_hot(field_slots(row, col, n_row, n_col), 4 * SLOT)
    r.ret[...] = nn(hot, r.gw[...]).astype(BF)


def back_last(r, n_row, n_col):
    _, row, col = grid_place()
    hot = one_hot(home_index(row, col, n_row, n_col), FIELD)
    grad = nn(hot, r.home[...])
    gain = vector(r.ln1_gain)
    _, xhat, inverse = norm(r.tokens[...].astype(F32), gain, vector(r.ln1_bias))
    r.input_grad[...] = (r.grad_middle[...] + norm_back(grad, xhat, inverse, gain)).astype(BF)
    r.late[0] = jnp.zeros((8, D), F32)
    r.late[0, 0:1, :] = jnp.sum(grad * xhat, 0, keepdims=True)
    r.late[0, 1:2, :] = jnp.sum(grad, 0, keepdims=True)


class Small:
    def __init__(self, value, come, send, recv, keep):
        dp, row, col = grid_place()
        self.value, self.come, self.send, self.recv, self.keep = value, come, send, recv, keep
        self.partners = [
            (dp, jnp.bitwise_xor(row, 1), col),
            (dp, jnp.bitwise_xor(row, 2), col),
            (dp, row, jnp.bitwise_xor(col, 1)),
            (dp, row, jnp.bitwise_xor(col, 2)),
            (1 - dp, row, col),
        ]

    def copy(self, s):
        return pltpu.make_async_remote_copy(
            self.value, self.come.at[s], self.send.at[s], self.recv.at[s],
            device_id=self.partners[s], device_id_type=MESH,
        )

    def start(self):
        self.copy(0).start()

    def step(self, s):
        self.copy(s).wait()
        value = self.come[s]
        if s == 4 and self.keep is not None:
            line = lax.broadcasted_iota(jnp.int32, value.shape, 0)
            value = jnp.where(line == self.keep, 0.0, value)
        self.value[...] = self.value[...] + value
        if s < 4:
            self.copy(s + 1).start()


class Late:
    def __init__(self, value, come, send, recv):
        self.dp, self.row, self.col = grid_place()
        self.value, self.come, self.send, self.recv = value, come, send, recv

    def copies(self, s):
        dp, row, col = self.dp, self.row, self.col
        plan = (
            [(dp, row, lax.rem(col + d, 4)) for d in (1, 2, 3)],
            [(dp, lax.rem(row + d, 4), col) for d in (1, 2, 3)],
            [(1 - dp, row, col)],
        )[s]
        return [
            pltpu.make_async_remote_copy(
                self.value.at[s], self.come.at[3 * s + i], self.send.at[3 * s + i], self.recv.at[3 * s + i],
                device_id=other, device_id_type=MESH,
            )
            for i, other in enumerate(plan)
        ]

    def start(self, s):
        for copy in self.copies(s):
            copy.start()

    def step(self, s):
        total = self.value[s]
        for i, copy in enumerate(self.copies(s)):
            copy.wait_recv()
            total = total + self.come[3 * s + i]
        self.value[s + 1] = total
        if s < 2:
            self.start(s + 1)

    def finish(self):
        for s in range(3):
            for copy in self.copies(s):
                copy.wait_send()


def back_body(n_row, n_col, shapes, r):
    dp, row, col = grid_place()
    blocks = blocks_of(shapes)
    rest = FIELD - TOK
    r.home[pl.ds(TOK, rest), :] = jnp.zeros((rest, D), BF)
    hidden = shapes[2][0]
    loads = [
        (r.gu_in, r.gu),
        (r.act_in, r.act),
        (r.wproj_in, r.wproj),
        (r.qkv_in, r.qkv),
        (r.probs_in, r.probs),
        (r.wqkv_in, r.wqkv),
        (r.xw_in, r.xw),
    ]
    loads = [pltpu.make_async_copy(src, dst, r.load_sem.at[i]) for i, (src, dst) in enumerate(loads)]
    for load in loads:
        load.start()
    greet(n_row, n_col)
    ways = [
        Reduce(g, g, dp * blocks[i][1], c, *blocks[i], pieces, parts, p, q)
        for i, (g, c, pieces, parts, p, q) in enumerate(
            [
                (r.gqkv, r.c0, 9, 3, r.p0, r.r0),
                (r.gproj, r.c1, 1, 1, r.p1, r.r1),
                (r.g1, r.c2, UP_PIECES, 1, r.p2, r.r2),
                (r.g2, r.c3, DOWN_PIECES, 1, r.p3, r.r3),
            ]
        )
    ]
    qkv_way, proj_way, up_way, down_way = ways
    loads[0].wait()
    loads[1].wait()
    mlp_weights(r, hidden, lambda j: up_way.start(0, j), lambda j: down_way.start(0, j))
    up_way.step(0)
    down_way.step(0)
    proj_weight_grad(r)
    proj_way.start(0)
    back_prepare(r, n_row, n_col)
    loads[2].wait()
    back_mix(r)
    loads[3].wait()
    loads[4].wait()
    hooks = (
        (0, lambda: proj_way.step(0)),
        (2, lambda: up_way.step(1)),
        (5, lambda: down_way.step(1)),
        (6, lambda: proj_way.step(1)),
        (19, lambda: up_way.step(2)),
    )
    back_windows(r, n_row, n_col, hooks)
    loads[6].wait()
    back_weights(r, n_row, n_col, lambda n: qkv_way.start(0, n))
    small = Small(r.small, r.small_come, r.small_sem.at[0], r.small_sem.at[1], 12)
    late = Late(r.late, r.late_come, r.late_sem.at[0], r.late_sem.at[1])
    small.start()
    qkv_way.step(0)
    down_way.step(2)
    loads[5].wait()
    back_return(r, n_row, n_col)
    give = Halo(r.ret, None, r.home, True, r.give_sem.at[0], r.give_sem.at[1], n_row, n_col)
    give.start()
    small.step(0)
    r.home[pl.ds(0, TOK), :] = r.ret[pl.ds(0, TOK), :]
    proj_way.step(2)
    qkv_way.step(1, 0)
    give.wait()
    back_last(r, n_row, n_col)
    late.start(0)
    small.step(1)
    qkv_way.step(1, 1)
    qkv_way.step(1, 2)
    up_way.result(r.o2)
    small.step(2)
    late.step(0)
    qkv_way.step(2, 0)
    down_way.result(r.o3)
    small.step(3)
    late.step(1)
    proj_way.result(r.o1)
    qkv_way.step(2, 1)
    small.step(4)
    late.step(2)
    qkv_way.step(2, 2)
    r.small[0:2, :] = r.late[3, 0:2, :]
    for part in range(3):
        qkv_way.result(r.o0, part)
    for way in ways:
        way.finish()
    late.finish()


def backward_buffers(shapes):
    v = pltpu.VMEM
    return dict(
        gw=v((4 * SLOT, D), BF),
        gmix=v((4 * SLOT, D), BF),
        dqkv=v((4 * SLOT, 3 * D), BF),
        table=v((256, 128), BF),
        gtab=v((2, 128, 128), F32),
    )


def back_call(n_row, n_col, shapes, tensors, first):
    sd, v = jax.ShapeDtypeStruct, pltpu.VMEM
    blocks = blocks_of(shapes)
    ins = {k: (t, vmem()) for k, t in tensors.items()}
    ins |= dict(
        gfield=(first.gfield, vmem()),
        grad_middle=(first.grad_middle, vmem()),
        small_in=(first.small, vmem()),
        n2=(first.n2, vmem()),
        mixed_own=(first.mixed_own, vmem()),
        qkv_in=(first.qkv_out, hbm()),
        probs_in=(first.probs_out, hbm()),
        wqkv_in=(first.wqkv_out, hbm()),
        wproj_in=(first.wproj_out, hbm()),
        xw_in=(first.xw_out, hbm()),
        act_in=(first.act_out, hbm()),
        gu_in=(first.gu_out, hbm()),
    )
    outs = dict(input_grad=(sd((TOK, D), BF), vmem()), small=(sd((32, D), F32), vmem()))
    outs |= {"o" + str(i): (sd(b, F32), vmem()) for i, b in enumerate(blocks)}
    come = [v((31 * b, h), BF) for b, h in blocks]
    scratch = backward_buffers(shapes) | dict(
        qkv=v((4 * SLOT, 3 * D), BF),
        probs=v((4 * HEADS, 16 * WIN, SLOT), BF),
        xw=v((4 * SLOT, D), BF),
        wqkv=v(shapes[0], BF),
        wproj=v(shapes[1], BF),
        gqkv=v(shapes[0], BF),
        gproj=v(shapes[1], BF),
        g1=v(shapes[2], BF),
        g2=v(shapes[3], BF),
        act=v((TOK, shapes[2][0]), BF),
        gu=v((TOK, shapes[2][0]), BF),
        cot_t=v((D, TOK), BF),
        c0=come[0],
        c1=come[1],
        c2=come[2],
        c3=come[3],
        ret=v((FIELD, D), BF),
        home=v((FIELD, D), BF),
        late=v((4, 8, D), F32),
        small_come=v((5, 32, D), F32),
        late_come=v((7, 8, D), F32),
        load_sem=dma(7),
        give_sem=dma(2, 3),
        small_sem=dma(2, 5),
        late_sem=dma(2, 7),
    )
    for i in range(4):
        scratch |= {"p" + str(i): dma(Reduce.SEMS), "r" + str(i): dma(Reduce.SEMS)}
    return named_call(
        functools.partial(back_body, n_row, n_col, shapes), ins, outs, scratch, "back",
        vmem_limit_bytes=63 * MIB, collective_id=1, has_side_effects=True,
    )


def back_plain(n_row, n_col, shapes, tensors, first, field):
    sd, v = jax.ShapeDtypeStruct, pltpu.VMEM
    hidden = shapes[2][0]
    ins = dict(
        act=(first.act_out, vmem()),
        gu=(first.gu_out, vmem()),
        n2=(first.n2, vmem()),
        gfield=(first.gfield, vmem()),
        mixed_own=(first.mixed_own, vmem()),
    ) | split_ins(tensors, "cot")

    def weights_body(r):
        mlp_weights(r, hidden, lambda j: None, lambda j: None)
        proj_weight_grad(r)

    outs = {k: (sd(s, BF), vmem()) for k, s in zip(("gproj", "g1", "g2"), shapes[1:])}
    three = named_call(
        weights_body, ins, outs, dict(cot_t=v((D, TOK), BF)), "weights", vmem_limit_bytes=60 * MIB
    )
    ins = split_ins(tensors, "rel_rows", "rel_cols", "masks", "places", "marks") | dict(
        gfield=(first.gfield, vmem()),
        small_in=(first.small, vmem()),
        qkv=(first.qkv_out, vmem()),
        probs=(first.probs_out, vmem()),
        wqkv=(first.wqkv_out, vmem()),
        wproj=(first.wproj_out, vmem()),
        field=(field, vmem()),
    )
    outs = dict(
        gqkv=(sd(shapes[0], BF), vmem()),
        ret=(sd((FIELD, D), BF), vmem()),
        small=(sd((32, D), F32), vmem()),
    )

    def windows_body(r):
        back_prepare(r, n_row, n_col)
        for w in range(4):
            cut_windows(r.field, r.xw, n_row, n_col, w)
        back_mix(r)
        back_windows(r, n_row, n_col, ())
        back_weights(r, n_row, n_col, lambda n: None)
        back_return(r, n_row, n_col)

    scratch = backward_buffers(shapes) | dict(xw=v((4 * SLOT, D), BF))
    one = named_call(windows_body, ins, outs, scratch, "windows", vmem_limit_bytes=60 * MIB)
    home = return_xla(one.ret, n_row, n_col)
    ins = split_ins(tensors, "tokens", "ln1_gain", "ln1_bias") | dict(
        home=(home, vmem()), grad_middle=(first.grad_middle, vmem())
    )
    outs = dict(input_grad=(sd((TOK, D), BF), vmem()), late=(sd((4, 8, D), F32), vmem()))
    two = named_call(lambda r: back_last(r, n_row, n_col), ins, outs, {}, "ends", vmem_limit_bytes=60 * MIB)
    one.input_grad = two.input_grad
    one.gproj, one.g1, one.g2 = three.gproj, three.g1, three.g2
    one.small = jnp.concatenate([two.late[0, :2], one.small[2:]], 0)
    return one


def last_body(count, r):
    for i in range(4):
        r.__dict__["t" + str(i)][...] = r.__dict__["s" + str(i)][...].astype(F32)
    r.output_out[...] = r.output[...]
    r.input_grad_out[...] = r.input_grad[...]
    for i in range(8):
        r.__dict__["v" + str(i)][...] = r.small[i : i + 1, :].reshape(D)
    r.up[...] = jnp.concatenate([r.small[8 + i : 9 + i, :] for i in range(r.up.shape[0] // D)], 1).reshape(-1)
    tables = jnp.concatenate([r.small[16:32, 128 * t : 128 * t + 128] for t in range(4)], 0)
    tables = tables[:, :HEAD] + pltpu.roll(tables, HEAD, 1)[:, :HEAD]
    r.rows[...] = tables[0 : 2 * WIN - 1, :]
    r.cols[...] = tables[32 : 32 + 2 * WIN - 1, :]
    r.stats[...] = jnp.sqrt(r.small[12:13, :5] / count)


def last_call(count, hidden, sums, output, input_grad, small):
    sd = jax.ShapeDtypeStruct
    ins = {"s" + str(i): (s, vmem()) for i, s in enumerate(sums)}
    ins |= dict(output=(output, vmem()), input_grad=(input_grad, vmem()), small=(small, vmem()))
    outs = {"t" + str(i): (sd(s.shape, F32), vmem()) for i, s in enumerate(sums)}
    outs |= dict(output_out=(sd((TOK, D), BF), vmem()), input_grad_out=(sd((TOK, D), BF), vmem()))
    outs |= {"v" + str(i): (sd((D,), F32), vmem()) for i in range(8)}
    outs |= dict(
        up=(sd((hidden,), F32), vmem()),
        rows=(sd((2 * WIN - 1, HEAD), F32), vmem()),
        cols=(sd((2 * WIN - 1, HEAD), F32), vmem()),
        stats=(sd((1, 5), F32), vmem()),
    )
    return named_call(functools.partial(last_body, count), ins, outs, {}, "last", vmem_limit_bytes=20 * MIB)


def on_device(
    n_dp, n_row, n_col,
    tokens, ln1_gain, ln1_bias, qkv_weight, query_bias, value_bias, rel_rows, rel_cols,
    proj_weight, proj_bias, ln2_gain, ln2_bias, fc1_weight, fc1_bias, fc2_weight, fc2_bias, cotangent,
):
    direct = (n_dp, n_row, n_col) == (2, 4, 4)
    tok = tokens.reshape(TOK, D)
    mask_values = np.zeros((16, 128), np.float32)
    mask_values[0, :64] = 1.0
    mask_values[1, 64:] = 1.0
    shared = dict(
        tokens=tok,
        cot=cotangent.reshape(TOK, D),
        ln1_gain=ln1_gain,
        ln1_bias=ln1_bias,
        rel_rows=rel_rows,
        rel_cols=rel_cols,
        masks=jnp.asarray(mask_values, BF),
    )
    forward = shared | dict(
        query_bias=query_bias,
        value_bias=value_bias,
        proj_bias=proj_bias,
        ln2_gain=ln2_gain,
        ln2_bias=ln2_bias,
        fc1_bias=fc1_bias,
        fc2_bias=fc2_bias,
        places=jnp.asarray(table_places(False), BF),
        marks=jnp.asarray(key_marks(False), BF),
    )
    backward = shared | dict(
        places=jnp.asarray(table_places(True), BF),
        marks=jnp.asarray(key_marks(True), BF),
    )
    shards = (qkv_weight, proj_weight, fc1_weight, fc2_weight)
    shapes = [(s.shape[1] * n_row * n_col, s.shape[0] * n_dp) for s in shards]
    if direct:
        forward |= dict(pick=jnp.asarray(pick_rows(), BF))
        weights, field = [s.T for s in shards], None
    else:
        weights = []
        for s in shards:
            s = lax.all_gather(s, AXES, axis=1, tiled=True)
            weights.append(lax.all_gather(s, "dp", axis=0, tiled=True).T)
        normed = norm(tok.astype(F32), ln1_gain.astype(F32), ln1_bias.astype(F32))[0].astype(BF)
        field = lend_xla(normed, n_row, n_col)
    if direct:
        first = front_call(n_row, n_col, shapes, forward, weights)
        second = back_call(n_row, n_col, shapes, backward, first)
        small = second.small
        sums = (second.o0, second.o1, second.o2, second.o3)
    else:
        first = front_plain(n_row, n_col, shapes, forward, weights, field)
        second = back_plain(n_row, n_col, shapes, backward, first, field)
        sums = []
        for g in (second.gqkv, second.gproj, second.g1, second.g2):
            g = lax.psum_scatter(g, AXES, scatter_dimension=0, tiled=True)
            sums.append(lax.psum_scatter(g, "dp", scatter_dimension=1, tiled=True))
        local = lax.psum(second.small, AXES)
        line = jnp.arange(32)[:, None] == 12
        small = jnp.where(line, local, lax.psum(jnp.where(line, 0.0, local), "dp"))
    out = last_call(TOK * n_row * n_col * D, shapes[2][0], sums, first.output, second.input_grad, small)
    return (
        out.output_out.reshape(tokens.shape),
        out.input_grad_out.reshape(tokens.shape),
        out.v0,
        out.v1,
        out.t0.T,
        out.v2,
        out.v3,
        out.rows,
        out.cols,
        out.t1.T,
        out.v4,
        out.v5,
        out.v6,
        out.t2.T,
        out.up,
        out.t3.T,
        out.v7,
        out.stats,
    )


def solution(mesh):
    tile = P("dp", "row", "col", None)
    weight = P("dp", AXES)
    sizes = [mesh.shape[a] for a in ("dp", "row", "col")]
    ins = [tile] + [P()] * 16
    for i in (3, 8, 12, 14):
        ins[i] = weight
    ins[16] = tile
    outs = [tile, tile] + [P()] * 16
    for i in (4, 9, 13, 15):
        outs[i] = weight
    outs[17] = P("dp", None)
    return jax.shard_map(
        functools.partial(on_device, *sizes),
        mesh=mesh,
        in_specs=tuple(ins),
        out_specs=tuple(outs),
        check_vma=False,
    )
```

time: 1650 us -> 214 us (0.13)
  local copies, waits for them, and re-layouts: 659 us -> 5.63 us
  waiting for transfers between devices: 510 us -> 0 us
  Pallas kernels: 0 us -> 207 us
  matrix products: 171 us -> 0 us
  blocking collectives: 129 us -> 0 us
  other arithmetic: 114 us -> 0 us
  between operations: 23.2 us -> 0.86 us
  starting transfers between devices: 21.2 us -> 0 us
    add x36 -> x0, local copies, waits for them, and re-layouts: 363 us -> none  [the longest x32 357 us: window_scores(): base.reshape(head_count, WIN, WIN, WIN, WIN) + rows_term[:, :, :, :, None]]
    reduce_scatter x5 -> x0, waiting for transfers between devices: 348 us -> none  [the longest x1 135 us: reduce_tiles(): lax.psum_scatter(parts[3].astype(jnp.bfloat16), ('row', 'col'), scatter_d...]
    pallas_call x0 -> x3, Pallas kernels: none -> 207 us  [named_call(): pl.pallas_call(kernel, name=name, out_shape=[shape for shape, _ in outs.v...]
    dot_general x76 -> x0, matrix products: 171 us -> none  [the longest x8 22.7 us: window_scores(): jnp.einsum('ihc,jhc->hij', queries, keys_w, preferred_element_type=jnp.fl...]
    all_gather x7 -> x0, waiting for transfers between devices: 105 us -> none  [the longest x1 63 us: on_device(): lax.all_gather(qkv_weight, ('row', 'col'), axis=1, tiled=True)]
    psum x2 -> x0, blocking collectives: 79.2 us -> none  [the longest x1 40.1 us: on_device(): square_totals = lax.psum(squares, ('row', 'col'))]
    ppermute x8 -> x0, waiting for transfers between devices: 54.6 us -> none  [the longest x4 36.9 us: extended(): lax.ppermute(lax.slice_in_dim(block, block.shape[dim] - width, None, axis...]
    convert_element_type x5 -> x0, local copies, waits for them, and re-layouts: 50.8 us -> none  [the longest x4 50.7 us: attend_back(): rows_sum = jnp.sum(grad_five, axis=4, dtype=jnp.float32)]
  transfers between devices with their start and end apart: 23 -> 0, of which waited for: 14 -> 0; matrix products, arithmetic and copies ran while one was open for 55% -> 0% of each run, Pallas kernels for 0% -> 0%
where the time goes in v2:
time: 214 us; the launch traced here: 213 us
  Pallas kernels  207 us (97%)
  local copies, waits for them, and re-layouts  5.63 us (3%)
    pallas_call x3, Pallas kernels, named_call(): pl.pallas_call(kernel, name=name, out_shape=[shape for shape, _ in outs.v...  207 us
    unnamed x14, local copies, waits for them, and re-layouts  5.63 us

profile of v2, /device:TPU:0, one launch (start us, length us, event | category | flops | bytes accessed | tf_op | source)
XLA Modules:
  0.0 213.2 jit_solution(11158532828608475937)
XLA Ops:
  0.7 99.9 %front.1 = (bf16[1024,2304]{1,0:T(8,128)(2,1)}, bf16[48,224,256]{2,1,0:T(8,128)(2,1)}, bf16[2304,768]{1,0:T(8,128)(2,1)}, bf16[768,768]{1,0:T(8,128)(2,1)}, bf16...) custom-call(bf16[256,768]{1,0:T(8,128)(2,1)} %bitcast.12, ...), custom_call_target="tpu_custom_call" | custom-call | tf_op jit(solution)/shard_map/front/pallas_call | solution.py:550
  100.6 0.0 copy-start
  100.6 105.6 %back.1 = (bf16[256,768]{1,0:T(8,128)(2,1)}, f32[32,768]{1,0:T(8,128)}, f32[144,384]{1,0:T(8,128)}, f32[48,384]{1,0:T(8,128)}, f32[192,384]{1,0:T(8,128)}, /*index=5*/f32[48,1536]{1,0:T(8,128)}) custom-call(bf16[256,768]{1,0:T(8,128)(2,1)} %bitcast.13, bf16[256,768]{1,0:T(8,128)(2,1)} %bitcast.15, bf16[768]{0:T(1024)(128)(2,1)} %refs_2_.3, ...), custom_call_target="tpu_custom_call" | custom-call | tf_op jit(solution)/shard_map/back/pallas_call | solution.py:550
  206.2 0.0 copy-done
  206.2 0.0 copy-start.1
  206.2 1.0 copy-done.1
  207.2 0.0 copy-start.2
  207.2 1.0 copy-done.2
  208.2 0.0 copy-start.3
  208.2 1.0 copy-done.3
  209.1 0.0 copy-start.4
  209.1 0.9 copy-done.4
  210.1 0.0 copy-start.5
  210.1 0.9 copy-done.5
  211.0 0.0 copy-start.6
  211.0 0.9 copy-done.6
  211.8 1.2 last.1
Async XLA Ops:
  100.6 105.6 %copy-start = (bf16[256,768]{1,0:T(8,128)(2,1)S(1)}, bf16[256,768]{1,0:T(8,128)(2,1)}, u32[]{:S(2)}) copy-start(bf16[256,768]{1,0:T(8,128)(2,1)} %get-tuple-element.71.refs_4_) | copy-start | bytes 1179652
  206.2 1.0 copy-start.1
  207.2 1.0 copy-start.2
  208.2 1.0 copy-start.3
  209.1 0.9 copy-start.4
  210.1 0.9 copy-start.5
  211.0 0.9 copy-start.6

commit v3 on v2

v3 whole, which is shorter than its diff:
```python
import functools
import types

import jax
import jax.numpy as jnp
import numpy as np
from jax import lax
from jax.experimental import pallas as pl
from jax.experimental.pallas import tpu as pltpu
from jax.sharding import PartitionSpec as P

HEADS = 12
HEAD = 64
WIN = 14
EPS = 1e-06
MESH = pl.DeviceIdType.MESH
AXES = ("row", "col")
F32 = jnp.float32
BF = jnp.bfloat16

D = HEADS * HEAD
TILE = 16
TOK = TILE * TILE
LO = 6
SLOT = 256
PAIRS = HEADS // 2
FIELD = 496
PICKED = 144
MIB = 2**20

LINKS = {
    (1, 0): (True, 160, 96, 256),
    (0, 1): (False, 0, 96, 352),
    (1, 1): (False, 96, 48, 448),
}


def nt(a, b):
    return lax.dot_general(a, b, (((1,), (1,)), ((), ())), preferred_element_type=F32)


def nn(a, b):
    return lax.dot_general(a, b, (((1,), (0,)), ((), ())), preferred_element_type=F32)


def tn(a, b):
    return lax.dot_general(a, b, (((0,), (0,)), ((), ())), preferred_element_type=F32)


def pick_rows():
    table = np.zeros((PICKED, TOK), np.float32)
    for base, first in ((0, 0), (96, TILE - LO)):
        for i in range((TILE - first) * LO):
            y, x = divmod(i, LO)
            table[base + i, (first + y) * TILE + TILE - LO + x] = 1.0
    return table


def table_places(back):
    place = np.zeros((256, 64), np.float32)
    for head in range(2):
        for r in range(2 * WIN - 1):
            for copy in range(2):
                row_lane = (64 + 28 * copy + r + 64 * head) % 128
                col_lane = (28 * copy + r + 64 * head) % 128
                place[128 * head + row_lane, 26 - r] = 1.0
                place[128 * head + col_lane, 32 + (r if back else 26 - r)] = 1.0
    return place


def key_marks(back):
    marks = np.zeros((2, SLOT, 128), np.float32)
    for head in range(2):
        for j in range(SLOT):
            k, l = divmod(j, 16)
            if k < WIN and l < WIN:
                for copy in range(2):
                    marks[head, j, (64 + 28 * copy + k + 64 * head) % 128] = 1.0
                    marks[head, j, (78 + 28 * copy + (13 - l if back else l) + 64 * head) % 128] = 1.0
            else:
                marks[head, j, (120 + 64 * head) % 128] = -1e30
    return marks


def lane_kinds(rows):
    lane = lax.broadcasted_iota(jnp.int32, (rows, 128), 1)
    kinds = []
    for head in range(2):
        at = (lane + 64 * head) % 128 if head else lane
        own = at < 64
        first = (at >= 64) & (at < 92)
        second = (at >= 92) & (at < 120)
        is_row = ((at >= 64) & (at < 78)) | ((at >= 92) & (at < 106))
        kinds.append((own, first, second, is_row, at == 120))
    return kinds


def window_index(w, row, col, n_row, n_col):
    place = lax.broadcasted_iota(jnp.int32, (SLOT, 1), 0)
    y = place // 16
    x = place - 16 * y
    a, b = w // 2, w % 2
    ry = WIN * (row + a) + y - TILE * row
    rx = WIN * (col + b) + x - TILE * col
    good = (y < WIN) & (x < WIN) & (ry < TILE) & (rx < TILE)
    if a:
        good = good & (row == n_row - 1)
    if b:
        good = good & (col == n_col - 1)
    up, left = ry < 0, rx < 0
    base = jnp.where(up, jnp.where(left, 448, 256), jnp.where(left, 352, 0))
    width = jnp.where(left, LO, TILE)
    index = base + jnp.where(up, ry + LO, ry) * width + jnp.where(left, rx + LO, rx)
    return jnp.where(good, index, -1)


def field_slots(row, col, n_row, n_col):
    at = lax.broadcasted_iota(jnp.int32, (FIELD, 1), 0)
    above = (at >= 256) & (at < 352)
    left = (at >= 352) & (at < 448)
    corner = at >= 448
    narrow = left | corner
    rest = jnp.where(corner, at - 448, jnp.where(left, at - 352, jnp.where(above, at - 256, at)))
    sixth = sum((rest >= LO * k).astype(jnp.int32) for k in range(1, TILE))
    ty = jnp.where(narrow, sixth, rest // TILE)
    tx = rest - ty * jnp.where(narrow, LO, TILE)
    ty = jnp.where(above | corner, ty - LO, ty)
    tx = jnp.where(narrow, tx - LO, tx)
    good = at < 484
    where = 0
    for t, place, n, stride, unit in ((ty, row, n_row, 2, 16), (tx, col, n_col, 1, 1)):
        y = TILE * place + t - WIN * place
        late = y >= WIN
        good = good & (y >= 0) & (jnp.logical_not(late) | (place == n - 1))
        where = where + jnp.where(late, stride * SLOT + unit * (y - WIN), unit * y)
    return jnp.where(good, where, -1)


def home_index(row, col, n_row, n_col):
    place = lax.broadcasted_iota(jnp.int32, (TOK, 1), 0)
    ty = place // TILE
    tx = place - TILE * ty
    down = (TILE * row + ty - WIN * row >= WIN) & (row < n_row - 1)
    right = (TILE * col + tx - WIN * col >= WIN) & (col < n_col - 1)
    near = TILE - LO
    return jnp.where(
        down,
        jnp.where(right, 448 + (ty - near) * LO + tx - near, 256 + (ty - near) * TILE + tx),
        jnp.where(right, 352 + ty * LO + tx - near, place),
    )


def one_hot(index, size):
    lane = lax.broadcasted_iota(jnp.int32, (index.shape[0], size), 1)
    return jnp.where(lane == index, 1.0, 0.0).astype(BF)


STEP = 64


def by_rows(body, sums):
    def step(i, kept):
        parts = body(pl.ds(pl.multiple_of(i * STEP, STEP), STEP))
        return tuple(k + sum(p[8 * q : 8 * q + 8] for q in range(STEP // 8)) for k, p in zip(kept, parts))

    return lax.fori_loop(0, TOK // STEP, step, (jnp.zeros((8, D), F32),) * sums)


def column_sum(v):
    return jnp.sum(v, 0, keepdims=True)


def norm(v, gain, bias):
    mean = jnp.mean(v, -1, keepdims=True)
    center = v - mean
    inverse = lax.rsqrt(jnp.mean(center * center, -1, keepdims=True) + EPS)
    xhat = center * inverse
    return xhat * gain + bias, xhat, inverse


def norm_back(grad, xhat, inverse, gain):
    d = grad * gain
    return inverse * (
        d - jnp.mean(d, -1, keepdims=True) - xhat * jnp.mean(d * xhat, -1, keepdims=True)
    )


def grid_place():
    return lax.axis_index("dp"), lax.axis_index("row"), lax.axis_index("col")


def exists(step, row, col, n_row, n_col):
    r, c = row + step[0], col + step[1]
    return (r >= 0) & (r < n_row) & (c >= 0) & (c < n_col)


CORNERS = ((1, 1), (-1, -1))


def greet(n_row, n_col):
    dp, row, col = grid_place()
    barrier = pltpu.get_barrier_semaphore()
    others = [(dp, row, lax.rem(col + d, n_col)) for d in (1, 2, 3)]
    others += [(dp, lax.rem(row + d, n_row), col) for d in (1, 2, 3)]
    others.append((1 - dp, row, col))
    for other in others:
        pl.semaphore_signal(barrier, inc=1, device_id=other, device_id_type=MESH)
    count = len(others)
    for step in CORNERS:
        there = exists(step, row, col, n_row, n_col)

        @pl.when(there)
        def _():
            pl.semaphore_signal(
                barrier, inc=1, device_id=(dp, row + step[0], col + step[1]), device_id_type=MESH
            )

        count = count + jnp.where(there, 1, 0)
    pl.semaphore_wait(barrier, count)


class Halo:
    def __init__(self, source, picked, land, back, send, recv, n_row, n_col):
        self.source, self.picked, self.land, self.back = source, picked, land, back
        self.send, self.recv, self.size = send, recv, (n_row, n_col)

    def copies(self):
        dp, row, col = grid_place()
        sign = -1 if self.back else 1
        for i, ((dr, dc), (own, first, rows, there)) in enumerate(LINKS.items()):
            if self.back:
                src = self.source.at[pl.ds(there, rows)]
            else:
                src = (self.source if own else self.picked).at[pl.ds(first, rows)]
            copy = pltpu.make_async_remote_copy(
                src,
                self.land.at[pl.ds(there, rows)],
                self.send.at[i],
                self.recv.at[i],
                device_id=(dp, row + sign * dr, col + sign * dc),
                device_id_type=MESH,
            )
            goes = exists((sign * dr, sign * dc), row, col, *self.size)
            comes = exists((-sign * dr, -sign * dc), row, col, *self.size)
            yield copy, goes, comes

    def start(self):
        for copy, goes, _ in self.copies():
            pl.when(goes)(copy.start)

    def wait(self):
        for copy, goes, comes in self.copies():
            pl.when(goes)(copy.wait_send)
            pl.when(comes)(copy.wait_recv)


def pick_start(halo, pick):
    halo.picked[...] = nn(pick[...], halo.source[pl.ds(0, TOK), :]).astype(BF)
    halo.start()


def halo_xla(blocks, back, n_row, n_col):
    sign = -1 if back else 1
    pieces = [blocks[0]]
    for (dr, dc), block in zip(LINKS, blocks[1:]):
        dr, dc = sign * dr, sign * dc
        pairs = [
            (r * n_col + c, (r + dr) * n_col + c + dc)
            for r in range(n_row)
            for c in range(n_col)
            if 0 <= r + dr < n_row and 0 <= c + dc < n_col
        ]
        pieces.append(lax.ppermute(block, AXES, pairs))
    return jnp.concatenate(pieces, 0)


def lend_xla(own, n_row, n_col):
    grid = own.reshape(TILE, TILE, -1)
    corner = grid[TILE - LO :, TILE - LO :].reshape(LO * LO, -1)
    blocks = [
        own,
        own[TILE * (TILE - LO) :],
        grid[:, TILE - LO :].reshape(TILE * LO, -1),
        jnp.pad(corner, ((0, 48 - LO * LO), (0, 0))),
    ]
    return halo_xla(blocks, False, n_row, n_col)


def return_xla(field, n_row, n_col):
    return halo_xla([field[:256], field[256:352], field[352:448], field[448:]], True, n_row, n_col)


def blocks_of(shapes):
    return [(n // 16, k // 2) for n, k in shapes]


def rows_at(first, count):
    return pl.ds(pl.multiple_of(first, 16), count)


LINE, OWN, OWN_CORE, LINE_CORE, FAR, NEAR_CORE, FAR_CORE, CORE = range(10, 18)


class Gather:
    SEMS = 20

    def __init__(self, full, shard, block, half, send, recv, part=0, parts=1):
        self.dp, self.row, self.col = grid_place()
        width = half // parts
        self.full, self.shard, self.b = full, shard.at[:, pl.ds(part * width, width)], block
        self.send, self.recv = send, recv
        self.lanes = pl.ds(pl.multiple_of(self.dp * half + part * width, 128), width)
        self.other = pl.ds(pl.multiple_of((1 - self.dp) * half + part * width, 128), width)

    def block(self, flip, place):
        return (jnp.bitwise_xor(self.row, flip) * 4 + place) * self.b

    def came(self, d):
        return lax.rem(self.col + 4 - d, 4)

    def copy(self, i, first, count, land, target, shard=False):
        core = target == CORE
        if core:
            device = (1 - self.dp, self.row, self.col)
        elif isinstance(target, tuple):
            device = (self.dp, self.row, lax.rem(self.col + target[0], 4))
        else:
            device = (self.dp, jnp.bitwise_xor(self.row, target), self.col)

        def make(src, dst):
            return pltpu.make_async_remote_copy(
                src, dst, self.send.at[i], self.recv.at[i], device_id=device, device_id_type=MESH
            )

        def out():
            there = self.full.at[rows_at(first, count), self.lanes]
            return make(self.shard if shard else there, there)

        def come():
            here = self.full.at[rows_at(land, count), self.other if core else self.lanes]
            return make(here, here)

        return out, come

    def copies(self, k):
        b = self.b
        own = self.block(0, self.col)
        if k == LINE:
            return [
                self.copy(d - 1, own, b, self.block(0, self.came(d)), (d,), True) for d in (1, 2, 3)
            ]
        if k == OWN:
            return [self.copy(2 + f, own, b, self.block(f, self.col), f, True) for f in (1, 2)]
        if k == OWN_CORE:
            return [self.copy(5, own, b, own, CORE, True)]
        if k < LINE:
            at = self.came(k)
            return [
                self.copy(4 + 2 * k, self.block(0, at), b, self.block(1, at), 1),
                self.copy(5 + 2 * k, self.block(0, at), b, self.block(2, at), 2),
            ]
        if k == LINE_CORE:
            return [
                self.copy(11 + d, self.block(0, self.came(d)), b, self.block(0, self.came(d)), CORE)
                for d in (1, 2, 3)
            ]
        if k == FAR:
            return [
                self.copy(15, self.block(2, 0), 2 * b, self.block(3, 0), 1),
                self.copy(16, self.block(1, 2), 2 * b, self.block(3, 2), 2),
            ]
        if k == NEAR_CORE:
            return [self.copy(16 + f, self.block(f, 0), 4 * b, self.block(f, 0), CORE) for f in (1, 2)]
        return [self.copy(19, self.block(3, 0), 4 * b, self.block(3, 0), CORE)]

    def start(self, *kinds):
        for k in kinds:
            for out, _ in self.copies(k):
                out().start()

    def arrive(self, *kinds):
        for k in kinds:
            for _, come in self.copies(k):
                come().wait_recv()

    def step(self, n):
        if n == 0:
            for d in (1, 2, 3):
                self.copies(LINE)[d - 1][1]().wait_recv()
                self.start(d)
            self.start(LINE_CORE)
        elif n == 1:
            self.arrive(OWN, 1, 2, 3)
            self.start(FAR, NEAR_CORE)
        else:
            self.arrive(FAR)
            self.start(FAR_CORE)

    def whole(self):
        self.arrive(OWN_CORE, LINE_CORE, NEAR_CORE, FAR_CORE)

    def finish(self):
        for k in (LINE, OWN, OWN_CORE, 1, 2, 3, LINE_CORE, FAR, NEAR_CORE, FAR_CORE):
            for out, _ in self.copies(k):
                out().wait_send()


class Reduce:
    SEMS = 34

    def __init__(self, grad, total, base, land, come, block, half, pieces, parts, send, recv):
        self.dp, self.row, self.col = grid_place()
        self.grad, self.total, self.base, self.come = grad, total, base, come
        self.land, self.land_row, mirrored = land
        self.land_there = self.dp * half if mirrored else 0
        self.land_here = (1 - self.dp) * half if mirrored else 0
        self.b, self.h, self.send, self.recv = block, half, send, recv
        self.pieces, self.parts, self.width = pieces, parts, half // parts
        self.other = pl.ds(pl.multiple_of((1 - self.dp) * half, 128), half)

    def side(self, base, part, width):
        return pl.ds(pl.multiple_of(base + part * width, 128), width)

    def at(self, flip, place=0):
        return (jnp.bitwise_xor(self.row, flip) * 4 + place) * self.b

    def lanes(self, part):
        return pl.ds(pl.multiple_of(self.base + part * self.width, 128), self.width)

    def came(self, first, count, part):
        return self.come.at[rows_at(first, count), pl.ds(part * self.width, self.width)]

    def tot(self, first, count, part):
        return self.total.at[rows_at(first, count), self.lanes(part)]

    def sem(self, k, part):
        if k == 0:
            return part
        return self.pieces + 7 * part + {1: 0, 2: 2, 3: 4}[k]

    def copies(self, k, part):
        b = self.b
        if k == 0:
            n = 16 * b // self.pieces
            there = self.land.at[rows_at(self.land_row + part * n, n), self.side(self.land_there, 0, self.h)]
            plan = [(self.grad.at[rows_at(part * n, n), self.other], there, (1 - self.dp, self.row, self.col))]
        elif k == 1:
            plan = [
                (
                    self.tot(self.at(3, 2 * half), 2 * b, part),
                    self.came(2 * half * b, 2 * b, part),
                    (self.dp, jnp.bitwise_xor(self.row, 1 + half), self.col),
                )
                for half in (0, 1)
            ]
        elif k == 2:
            plan = [
                (
                    self.tot(self.at(flip), 4 * b, part),
                    self.came(4 * flip * b, 4 * b, part),
                    (self.dp, jnp.bitwise_xor(self.row, flip), self.col),
                )
                for flip in (1, 2)
            ]
        else:
            plan = []
            for d in (1, 2, 3):
                to = lax.rem(self.col + d, 4)
                plan.append(
                    (
                        self.tot(self.at(0, to), b, part),
                        self.came((11 + d) * b, b, part),
                        (self.dp, self.row, to),
                    )
                )
        base = self.sem(k, part)
        return [
            pltpu.make_async_remote_copy(
                src, dst, self.send.at[base + i], self.recv.at[base + i], device_id=dev, device_id_type=MESH
            )
            for i, (src, dst, dev) in enumerate(plan)
        ]

    def start(self, k, part=0):
        for copy in self.copies(k, part):
            copy.start()

    def arrive(self, k, part=0):
        for copy in self.copies(k, part):
            copy.wait_recv()

    def sum_rows(self, first, count, froms, part, source=None, base=0):
        most = (256 if len(froms) == 1 else 96) * 384
        step = next(n for n in range(count, 0, -16) if count % n == 0 and n * self.width <= most)
        lanes = self.lanes(part)
        side = self.side(base, part, self.width)
        source = self.come if source is None else source

        def body(i, _):
            at = rows_at(first + i * step, step)
            value = self.total[at, lanes]
            if len(froms) == 1:
                value = value + source[rows_at(froms[0] + i * step, step), side]
            else:
                value = value.astype(F32)
                for f in froms:
                    value = value + source[rows_at(f + i * step, step), side].astype(F32)
                value = value.astype(BF)
            self.total[at, lanes] = value
            return 0

        lax.fori_loop(0, count // step, body, 0)

    def add_piece(self, piece):
        n = 16 * self.b // self.pieces
        self.arrive(0, piece)
        for part in range(self.parts):
            self.sum_rows(piece * n, n, (self.land_row + piece * n,), part, self.land, self.land_here)

    def step(self, k, part=0):
        b = self.b
        if k == 0:
            for piece in range(self.pieces):
                self.add_piece(piece)
            for part in range(1, self.parts):
                self.start(1, part)
            part = 0
        else:
            self.arrive(k, part)
            if k == 1:
                self.sum_rows(self.at(2), 2 * b, (0,), part)
                self.sum_rows(self.at(1, 2), 2 * b, (2 * b,), part)
            else:
                self.sum_rows(self.at(0), 4 * b, (4 * b, 8 * b), part)
        self.start(k + 1, part)

    def result(self, out, part=0):
        b = self.b
        self.arrive(3, part)
        value = self.total[rows_at(self.at(0, self.col), b), self.lanes(part)].astype(F32)
        side = pl.ds(part * self.width, self.width)
        for d in (1, 2, 3):
            value = value + self.come[pl.ds((11 + d) * b, b), side].astype(F32)
        out[:, side] = value

    def gone(self):
        for piece in range(self.pieces):
            self.copies(0, piece)[0].wait_send()

    def finish(self):
        for part in range(self.parts):
            for k in (1, 2, 3):
                for copy in self.copies(k, part):
                    copy.wait_send()


def vmem():
    return pl.BlockSpec(memory_space=pltpu.VMEM)


def hbm():
    return pl.BlockSpec(memory_space=pl.ANY)


def dma(*n):
    return pltpu.SemaphoreType.DMA(n)


def named_call(body, ins, outs, scratch, name, **params):
    names = [*ins, *outs, *scratch]

    def kernel(*refs):
        body(types.SimpleNamespace(**dict(zip(names, refs))))

    result = pl.pallas_call(
        kernel,
        name=name,
        out_shape=[shape for shape, _ in outs.values()],
        in_specs=[spec for _, spec in ins.values()],
        out_specs=[spec for _, spec in outs.values()],
        scratch_shapes=list(scratch.values()),
        compiler_params=pltpu.CompilerParams(**params),
    )(*[array for array, _ in ins.values()])
    return types.SimpleNamespace(**dict(zip(outs, result)))


def vector(ref):
    return ref[...].astype(F32).reshape(1, -1)


def joint_table(rel_rows, rel_cols):
    parts = [rel_rows[...], jnp.zeros((5, HEAD), BF), rel_cols[...], jnp.zeros((5, HEAD), BF)]
    table = jnp.concatenate([p.astype(F32) for p in parts], 0)
    return jnp.concatenate([table, table], 1).astype(BF)


def table_kernel_value(places, table):
    value = nn(places, table)
    line = lax.broadcasted_iota(jnp.int32, value.shape, 0)
    lane = lax.broadcasted_iota(jnp.int32, value.shape, 1)
    return jnp.where((line < 128) == (lane < 64), value, 0.0).astype(BF)


def spread(a, back):
    rows, cols = [], []
    for y in range(a.shape[0] // 16):
        part = a[16 * y : 16 * y + 16, :]
        rows.append(pltpu.roll(part, 13 - y if back else (115 + y) % 128, 1))
        cols.append(pltpu.roll(part, 50 if back else 65, 1, stride=1, stride_axis=0))
    return jnp.concatenate(rows, 0), jnp.concatenate(cols, 0)


def pair_place(w, pair):
    return pl.multiple_of(w * SLOT, SLOT), pl.multiple_of(pair * 128, 128)


def attend_pair(w, place, pair, n, qkv, table, marks, masks, probs, mixed):
    r0, l0 = pair_place(w, pair)
    q2 = qkv[pl.ds(r0, n), pl.ds(l0, 128)]
    k2 = qkv[pl.ds(r0, SLOT), pl.ds(D + l0, 128)]
    v2 = qkv[pl.ds(r0, SLOT), pl.ds(2 * D + l0, 128)]
    a2 = nt(q2, table[...])
    qf = q2.astype(F32) * HEAD**-0.5
    kinds = lane_kinds(n)
    outs = []
    for head in range(2):
        own, first, second, is_row, one = kinds[head]
        rows, cols = spread(a2[:, 128 * head : 128 * head + 128], False)
        bias = jnp.where(is_row, rows, cols)
        high = bias.astype(BF).astype(F32)
        low = jnp.where(second, bias - high, jnp.where(one, 1.0, 0.0))
        aug = jnp.where(own, qf, jnp.where(first, high, low)).astype(BF)
        keys = k2 * masks[head : head + 1, :] + marks[head]
        scores = nt(aug, keys)
        top = jnp.max(scores, -1, keepdims=True)
        e = jnp.exp(scores - top)
        p = (e * (1.0 / jnp.sum(e, -1, keepdims=True))).astype(BF)
        probs[2 * place + head] = p
        outs.append(nn(p, v2))
    mixed[pl.ds(r0, n), pl.ds(l0, 128)] = jnp.where(kinds[0][0], outs[0], outs[1]).astype(BF)


def attend_back_pair(w, place, pair, n, qkv, gmix, probs, table, marks, masks, dqkv, gtab):
    r0, l0 = pair_place(w, pair)
    scale = HEAD**-0.5
    q2 = qkv[pl.ds(r0, n), pl.ds(l0, 128)]
    k2 = qkv[pl.ds(r0, SLOT), pl.ds(D + l0, 128)]
    v2 = qkv[pl.ds(r0, SLOT), pl.ds(2 * D + l0, 128)]
    g2 = gmix[pl.ds(r0, n), pl.ds(l0, 128)]
    kinds = lane_kinds(n)
    dq, dk, dv = [], [], []
    for head in range(2):
        own, first, second, is_row, one = kinds[head]
        mask = masks[head : head + 1, :]
        p = probs[2 * place + head]
        pf = p.astype(F32)
        dp = nt(g2, v2 * mask)
        ds = (pf * (dp - jnp.sum(pf * dp, -1, keepdims=True))).astype(BF)
        keys = k2 * (mask * jnp.asarray(scale, BF)) + marks[head]
        dqa = nn(ds, keys)
        marked = jnp.where(first | second, dqa, 0.0)
        rows, _ = spread(jnp.where(is_row, marked, 0.0), True)
        _, cols = spread(jnp.where(is_row, 0.0, marked), True)
        back = rows + cols
        at = lax.broadcasted_iota(jnp.int32, (n, 128), 1)
        if head:
            at = (at + 64) % 128
        high = back.astype(BF).astype(F32)
        split = jnp.where((at < 28) | ((at >= 64) & (at < 92)), high, back - high).astype(BF)
        extra = nn(split, table[128 * head : 128 * head + 128, :])
        dq.append(dqa + extra)
        gtab[head] += tn(split, q2)
        dk.append(tn(ds, q2))
        dv.append(tn(p, g2))
    wide = lane_kinds(SLOT)[0][0]
    dqkv[pl.ds(r0, n), pl.ds(l0, 128)] = jnp.where(kinds[0][0], dq[0], dq[1]).astype(BF)
    dqkv[pl.ds(4 * SLOT + r0, SLOT), pl.ds(l0, 128)] = (jnp.where(wide, dk[0], dk[1]) * scale).astype(BF)
    dqkv[pl.ds(8 * SLOT + r0, SLOT), pl.ds(l0, 128)] = jnp.where(wide, dv[0], dv[1]).astype(BF)


def over_windows(body, hooks, n_row, n_col):
    _, row, col = grid_place()
    for a, n in ((0, 16 * WIN), (1, 16 * (TILE * n_row - WIN * n_row))):

        def step(i, _):
            b = i // PAIRS
            good = (b == 0) | (col == n_col - 1)
            if a:
                good = good & (row == n_row - 1)

            @pl.when(good)
            def _():
                body(a, 2 * a + b, i, lax.rem(i, PAIRS), n)

            for when, hook in hooks:
                if when // (2 * PAIRS) == a:
                    pl.when(i == when % (2 * PAIRS))(hook)
            return 0

        lax.fori_loop(0, 2 * PAIRS, step, 0)


def attend_part(r, n_row, n_col, hooks, between):
    _, row, col = grid_place()
    biases = (vector(r.query_bias), None, vector(r.value_bias))
    for part, bias in enumerate(biases):
        for n in range(3):
            at = part * D + 256 * n
            value = nt(r.xw[...], r.wqkv[pl.ds(at, 256), :])
            if bias is not None:
                value = value + bias[:, 256 * n : 256 * n + 256]
            r.qkv[:, pl.ds(at, 256)] = value.astype(BF)
        between(part)

    def body(a, w, i, pair, n):
        attend_pair(w, i, pair, n, r.qkv, r.table, r.marks, r.masks, (r.probs0, r.probs1)[a], r.mixed)

    over_windows(body, hooks, n_row, n_col)
    hot = one_hot(field_slots(row, col, n_row, n_col), 4 * SLOT)
    r.ret[...] = nn(hot, r.mixed[...]).astype(BF)


def cut_windows(source, land, n_row, n_col, w):
    _, row, col = grid_place()
    hot = one_hot(window_index(w, row, col, n_row, n_col), FIELD)
    land[pl.ds(w * SLOT, SLOT), :] = nn(hot, source[...]).astype(BF)


def mlp_first(r, n_row, n_col, hidden, between, hooks):
    _, row, col = grid_place()
    hot = one_hot(home_index(row, col, n_row, n_col), FIELD)
    r.mixed_own[...] = nn(hot, r.home[...]).astype(BF)
    r.acc[...] = nt(r.mixed_own[...], r.wproj[...])
    shift, gain, bias = vector(r.proj_bias), vector(r.ln2_gain), vector(r.ln2_bias)

    def rows_body(rows):
        attended = (r.acc[rows, :] + shift).astype(BF)
        r.attended[rows, :] = attended
        middle = r.tokens[rows, :].astype(F32) + attended.astype(F32)
        r.n2[rows, :] = norm(middle, gain, bias)[0].astype(BF)
        return ()

    by_rows(rows_body, 0)
    between()
    up_bias = vector(r.fc1_bias)
    for line in range(hidden // D):
        r.up_bias[line : line + 1, :] = up_bias[:, line * D : line * D + D]

    def chunk(j, _):
        at = pl.multiple_of(j * 256, 256)
        lane = pl.multiple_of(lax.rem(j, 3) * 256, 256)
        u = nt(r.n2[...], r.w1[pl.ds(at, 256), :]) + r.up_bias[pl.ds(j // 3, 1), pl.ds(lane, 256)]
        cdf = 0.5 * (1.0 + lax.erf(u * 0.7071067811865476))
        r.act[:, pl.ds(at, 256)] = (u * cdf).astype(BF)
        r.slope[:, pl.ds(at, 256)] = (cdf + u * (jnp.exp(-0.5 * u * u) * 0.3989422804014327)).astype(BF)
        for when, hook in hooks:
            pl.when(j == when)(hook)
        return 0

    lax.fori_loop(0, hidden // 256, chunk, 0)


PARTS = 3


def mlp_second(r, hidden, ready):
    r.acc[...] = jnp.zeros_like(r.acc)
    r.small[...] = jnp.zeros_like(r.small)
    n = hidden // (2 * PARTS)
    for part in range(PARTS):
        ready(part)

        def chunk(i, _):
            at = pl.multiple_of((i * PARTS + part) * n, n)
            wide = pl.ds(at, n)
            gu = (nn(r.cot[...], r.w2[:, wide]) * r.slope[:, wide].astype(F32)).astype(BF)
            r.gu[:, wide] = gu
            r.acc[...] += nn(gu, r.w1[wide, :])
            r.up_sum[:, wide] = jnp.sum(gu.astype(F32), 0, keepdims=True)
            return 0

        lax.fori_loop(0, 2, chunk, 0)
    for line in range(hidden // D):
        r.small[8 + line : 9 + line, :] = r.up_sum[:, line * D : line * D + D]
    gain, bias = vector(r.ln2_gain), vector(r.ln2_bias)

    def rows_body(rows):
        middle = r.tokens[rows, :].astype(F32) + r.attended[rows, :].astype(F32)
        _, xhat, inverse = norm(middle, gain, bias)
        grad = r.acc[rows, :]
        cf = r.cot[rows, :].astype(F32)
        gm = cf + norm_back(grad, xhat, inverse, gain)
        r.grad_middle[rows, :] = gm
        low = gm.astype(BF)
        r.gfield[rows, :] = low
        return low.astype(F32), grad * xhat, grad, cf

    for line, value in enumerate(by_rows(rows_body, 4)):
        r.small[4 + line : 5 + line, :] = column_sum(value)


def mlp_branch(r, hidden):
    r.acc[...] = jnp.zeros_like(r.acc)

    def chunk(j, _):
        wide = pl.ds(pl.multiple_of(j * 512, 512), 512)
        r.acc[...] += nt(r.act[:, wide], r.w2[:, wide])
        return 0

    lax.fori_loop(0, hidden // 512, chunk, 0)


def mlp_out(r):
    bias = vector(r.fc2_bias)

    def rows_body(rows):
        att = r.attended[rows, :].astype(F32)
        tok = r.tokens[rows, :].astype(F32)
        middle = tok + att
        br = r.acc[rows, :] + bias
        result = middle + br
        r.output[rows, :] = result.astype(BF)
        return tuple(v * v for v in (tok, middle, result, att, br))

    lane = lax.broadcasted_iota(jnp.int32, (1, D), 1)
    stats = jnp.zeros((1, D), F32)
    for n, v in enumerate(by_rows(rows_body, 5)):
        stats = jnp.where(lane == n, jnp.sum(column_sum(v), 1, keepdims=True), stats)
    r.small[12:13, :] = stats


UP_PIECES, DOWN_PIECES = 12, 6


def up_weights(r, hidden, sent):
    def up(j, _):
        n = hidden // UP_PIECES
        at = pl.multiple_of(j * n, n)
        r.g1[pl.ds(at, n), :] = tn(r.gu[:, pl.ds(at, n)], r.n2[...]).astype(BF)
        sent(j)
        return 0

    lax.fori_loop(0, UP_PIECES, up, 0)


def down_weights(r, sent):
    r.cot_t[...] = r.cot[...].T

    def down(j, _):
        n = D // DOWN_PIECES
        at = pl.multiple_of(j * n, n)
        r.g2[pl.ds(at, n), :] = nn(r.cot_t[pl.ds(at, n), :], r.act[...]).astype(BF)
        sent(j)
        return 0

    lax.fori_loop(0, DOWN_PIECES, down, 0)


def proj_weight_grad(r):
    def chunk(n, _):
        at = pl.multiple_of(n * 256, 256)
        r.gproj[pl.ds(at, 256), :] = tn(r.gfield[pl.ds(0, TOK), pl.ds(at, 256)], r.mixed_own[...]).astype(BF)
        return 0

    lax.fori_loop(0, D // 256, chunk, 0)


def prepare(r):
    r.table[...] = table_kernel_value(r.places[...], joint_table(r.rel_rows, r.rel_cols))
    r.mixed[...] = jnp.zeros_like(r.mixed)


def back_prepare(r, n_row, n_col):
    r.table[...] = table_kernel_value(r.places_back[...], joint_table(r.rel_rows, r.rel_cols))
    r.gtab[...] = jnp.zeros_like(r.gtab)
    r.dqkv[...] = jnp.zeros_like(r.dqkv)
    for w in range(4):
        cut_windows(r.gfield, r.gw, n_row, n_col, w)


def back_mix(r):
    def mix(n, _):
        at = pl.multiple_of(n * 256, 256)
        r.gmix[:, pl.ds(at, 256)] = nn(r.gw[...], r.wproj[:, pl.ds(at, 256)]).astype(BF)
        return 0

    lax.fori_loop(0, 3, mix, 0)


def back_windows(r, n_row, n_col, hooks):
    def body(a, w, i, pair, n):
        attend_back_pair(w, i, pair, n, r.qkv, r.gmix, (r.probs0, r.probs1)[a], r.table, r.marks_back, r.masks, r.dqkv, r.gtab)

    over_windows(body, hooks, n_row, n_col)


def back_weights(r, n_row, n_col, sent):
    for n in range(9):
        rows, lanes = pl.ds(n // 3 * 4 * SLOT, 4 * SLOT), pl.ds(n % 3 * 256, 256)
        r.gqkv[pl.ds(256 * n, 256), :] = tn(r.dqkv[rows, lanes], r.xw[...]).astype(BF)
        sent(n)
    ones = jnp.ones((16, 4 * SLOT), BF)
    r.mid[...] = jnp.zeros_like(r.mid)
    r.mid[16:17, :] = nn(ones, r.dqkv[pl.ds(0, 4 * SLOT), :])[0:1, :]
    r.mid[17:18, :] = nn(ones, r.dqkv[pl.ds(8 * SLOT, 4 * SLOT), :])[0:1, :]
    lane = lax.broadcasted_iota(jnp.int32, (128, 128), 1)
    left = jnp.where(lane < 64, r.gtab[0], 0.0)
    right = jnp.where(lane >= 64, r.gtab[1], 0.0)
    tab = lax.dot_general(
        r.places_back[...].astype(F32),
        jnp.concatenate([left, right], 0),
        (((0,), (0,)), ((), ())),
        precision=lax.Precision.HIGHEST,
        preferred_element_type=F32,
    )
    for t in range(4):
        r.mid[0:16, 128 * t : 128 * t + 128] = tab[16 * t : 16 * t + 16, :]


def back_return(r, n_row, n_col, between):
    _, row, col = grid_place()
    for n in range(3):
        value = 0
        for part in range(3):
            rows = pl.ds(4 * part * SLOT, 4 * SLOT)
            value = value + nn(r.dqkv[rows, :], r.wqkv[pl.ds(part * D, D), pl.ds(256 * n, 256)])
        r.gw[:, pl.ds(256 * n, 256)] = value.astype(BF)
        between(n)
    hot = one_hot(field_slots(row, col, n_row, n_col), 4 * SLOT)
    r.ret[...] = nn(hot, r.gw[...]).astype(BF)


def back_last(r, n_row, n_col):
    _, row, col = grid_place()
    hot = one_hot(home_index(row, col, n_row, n_col), FIELD)
    r.acc[...] = nn(hot, r.home2[...])
    gain, bias = vector(r.ln1_gain), vector(r.ln1_bias)

    def rows_body(rows):
        grad = r.acc[rows, :]
        _, xhat, inverse = norm(r.tokens[rows, :].astype(F32), gain, bias)
        r.input_grad[rows, :] = (r.grad_middle[rows, :] + norm_back(grad, xhat, inverse, gain)).astype(BF)
        return grad * xhat, grad

    r.late[...] = jnp.zeros_like(r.late)
    for line, value in enumerate(by_rows(rows_body, 2)):
        r.late[line : line + 1, :] = column_sum(value)


class Small:
    def __init__(self, value, come, send, recv, keep=None):
        self.dp, self.row, self.col = grid_place()
        self.value, self.come, self.send, self.recv, self.keep = value, come, send, recv, keep

    def copies(self, s):
        dp, row, col = self.dp, self.row, self.col
        plan = (
            [(dp, row, lax.rem(col + d, 4)) for d in (1, 2, 3)],
            [(dp, lax.rem(row + d, 4), col) for d in (1, 2, 3)],
            [(1 - dp, row, col)],
        )[s]
        return [
            pltpu.make_async_remote_copy(
                self.value, self.come.at[3 * s + i], self.send.at[3 * s + i], self.recv.at[3 * s + i],
                device_id=other, device_id_type=MESH,
            )
            for i, other in enumerate(plan)
        ]

    def start(self, s=0):
        for copy in self.copies(s):
            copy.start()

    def step(self, s):
        total = self.value[...]
        for i, copy in enumerate(self.copies(s)):
            copy.wait()
            value = self.come[3 * s + i]
            if s == 2 and self.keep is not None:
                line = lax.broadcasted_iota(jnp.int32, value.shape, 0)
                value = jnp.where(line == self.keep, 0.0, value)
            total = total + value
        self.value[...] = total
        if s < 2:
            self.start(s + 1)


GATHERS = ((0, 0, 1), (1, 0, 1), (2, 0, 1), *((3, part, PARTS) for part in range(PARTS)))


def block_body(n_row, n_col, shapes, hidden, r):
    dp, row, col = grid_place()
    rest = FIELD - TOK
    r.gfield, r.home2 = r.field, r.home
    for ref in (r.field, r.home):
        ref[pl.ds(TOK, rest), :] = jnp.zeros((rest, D), BF)
    greet(n_row, n_col)
    blocks = blocks_of(shapes)
    fulls, shards = (r.wqkv, r.wproj, r.w1, r.w2), (r.s0, r.s1, r.s2, r.s3)
    gathers = [
        Gather(fulls[i], shards[i], *blocks[i], r.gather_sem.at[0, n], r.gather_sem.at[1, n], part, parts)
        for n, (i, part, parts) in enumerate(GATHERS)
    ]
    qkv_way, proj_way, up_way, *down_ways = gathers
    qkv_way.start(LINE, OWN, OWN_CORE)
    gain, bias = vector(r.ln1_gain), vector(r.ln1_bias)

    def rows_body(rows):
        r.field[rows, :] = norm(r.tokens[rows, :].astype(F32), gain, bias)[0].astype(BF)
        return ()

    by_rows(rows_body, 0)
    size = (n_row, n_col)
    lend = Halo(r.field, r.picked, r.field, False, r.lend_sem.at[0], r.lend_sem.at[1], *size)
    give = Halo(r.ret, None, r.home, True, r.give_sem.at[0], r.give_sem.at[1], *size)
    lend2 = Halo(r.gfield, r.picked, r.gfield, False, r.lend_sem.at[2], r.lend_sem.at[3], *size)
    give2 = Halo(r.ret, None, r.home2, True, r.give_sem.at[2], r.give_sem.at[3], *size)
    pick_start(lend, r.pick)
    local = []
    for way in gathers[1:]:
        way.start(OWN, OWN_CORE)
    for i, way in enumerate(gathers):
        own = way.full.at[rows_at(way.block(0, way.col), way.b), way.lanes]
        mine = pltpu.make_async_copy(way.shard, own, r.local_sem.at[i])
        mine.start()
        local.append(mine)
    prepare(r)
    for mine in local:
        mine.wait()
    qkv_way.step(0)
    proj_way.start(LINE)
    up_way.start(LINE)
    lend.wait()
    for w in range(4):
        cut_windows(r.field, r.xw, n_row, n_col, w)
    qkv_way.step(1)
    for way in down_ways:
        way.start(LINE)
    qkv_way.step(2)
    qkv_way.whole()

    def between(part):
        if part == 0:
            proj_way.step(0)

    hooks = (
        (3, lambda: up_way.step(0)),
        (4, lambda: proj_way.step(1)),
        (8, lambda: down_ways[0].step(0)),
        (11, lambda: down_ways[1].step(0)),
        (14, lambda: up_way.step(1)),
        (16, lambda: proj_way.step(2)),
        (18, lambda: down_ways[2].step(0)),
        (20, lambda: down_ways[0].step(1)),
    )
    attend_part(r, n_row, n_col, hooks, between)
    give.start()
    r.home[pl.ds(0, TOK), :] = r.ret[pl.ds(0, TOK), :]
    proj_way.whole()
    up_way.step(2)
    down_ways[1].step(1)
    give.wait()

    qkv_sum, proj_sum, up_sum, down_sum = sums = [
        Reduce(g, g, dp * blocks[i][1], land, c, *blocks[i], pieces, parts, p, q)
        for i, (g, land, c, pieces, parts, p, q) in enumerate(
            [
                (r.gqkv, (r.g1, 0, True), r.c0, 9, PARTS, r.t0, r.u0),
                (r.gproj, (r.g1, shapes[0][0], True), r.c1, 1, 1, r.t1, r.u1),
                (r.g1, (r.w1, 0, False), r.c2, UP_PIECES, PARTS, r.t2, r.u2),
                (r.g2, (r.w2, 0, False), r.c3, DOWN_PIECES, PARTS, r.t3, r.u3),
            ]
        )
    ]

    def free(k):
        pl.semaphore_signal(r.free_sem.at[k], inc=1, device_id=(1 - dp, row, col), device_id_type=MESH)

    early = Small(r.small, r.small_come, r.small_sem.at[0], r.small_sem.at[1], 12)
    mid = Small(r.mid, r.mid_come, r.mid_sem.at[0], r.mid_sem.at[1])
    late = Small(r.late, r.late_come, r.late_sem.at[0], r.late_sem.at[1])

    def middle(act, slope, gu, cot_t):
        m = types.SimpleNamespace(**r.__dict__, act=act, slope=slope, gu=gu, cot_t=cot_t)

        def arrived():
            down_ways[2].step(1)
            up_way.whole()

        hooks = (
            (2, lambda: down_ways[0].step(2)),
            (6, lambda: down_ways[1].step(2)),
            (11, lambda: down_ways[2].step(2)),
        )
        mlp_first(m, n_row, n_col, hidden, arrived, hooks)
        mlp_second(m, hidden, lambda part: down_ways[part].whole())
        for way in gathers:
            way.finish()
        free(0)
        pick_start(lend2, r.pick)
        pl.semaphore_wait(r.free_sem.at[0], 1)
        up_weights(m, hidden, lambda j: up_sum.start(0, j))
        up_sum.step(0)
        up_sum.gone()
        mlp_branch(m, hidden)
        free(1)
        pl.semaphore_wait(r.free_sem.at[1], 1)
        down_weights(m, lambda j: down_sum.start(0, j))
        mlp_out(m)
        early.start()
        down_sum.step(0)

    v = pltpu.VMEM
    wide = (TOK, hidden)
    pl.run_scoped(middle, v(wide, BF), v(wide, BF), v(wide, BF), v((D, TOK), BF))
    proj_weight_grad(r)
    proj_sum.start(0)
    lend2.wait()

    def all_parts(way, k):
        for part in range(way.parts):
            way.step(k, part)

    def ends(gw):
        e = types.SimpleNamespace(**r.__dict__, gw=gw, gmix=r.mixed, dqkv=r.w1)
        all_parts(up_sum, 1)
        back_prepare(e, n_row, n_col)
        proj_sum.step(0)
        back_mix(e)
        early.step(0)
        hooks = (
            (2, lambda: all_parts(down_sum, 1)),
            (9, lambda: all_parts(up_sum, 2)),
            (10, lambda: proj_sum.step(1)),
            (20, lambda: all_parts(down_sum, 2)),
        )
        back_windows(e, n_row, n_col, hooks)
        back_return(e, n_row, n_col, lambda n: None)
        give2.start()
        r.home2[pl.ds(0, TOK), :] = r.ret[pl.ds(0, TOK), :]
        early.step(1)
        back_weights(e, n_row, n_col, lambda n: qkv_sum.start(0, n))
        mid.start()
        proj_sum.step(2)
        give2.wait()
        back_last(e, n_row, n_col)
        late.start()
        qkv_sum.step(0)
        early.step(2)
        mid.step(0)
        late.step(0)
        for part in range(PARTS):
            up_sum.result(r.o2, part)
        qkv_sum.step(1, 0)
        qkv_sum.step(1, 1)
        mid.step(1)
        late.step(1)
        qkv_sum.step(1, 2)
        for part in range(PARTS):
            down_sum.result(r.o3, part)
        proj_sum.result(r.o1)
        qkv_sum.step(2, 0)
        mid.step(2)
        late.step(2)
        qkv_sum.step(2, 1)
        qkv_sum.step(2, 2)
        for part in range(PARTS):
            qkv_sum.result(r.o0, part)
        for way in (qkv_sum, proj_sum, down_sum):
            way.gone()
        for way in sums:
            way.finish()

    pl.run_scoped(ends, v((4 * SLOT, D), BF))


def split_ins(tensors, *names):
    return {k: (tensors[k], vmem()) for k in names}


def as_out(buffer):
    return (jax.ShapeDtypeStruct(buffer.shape, buffer.dtype), vmem())


def window_buffers(n_row):
    v = pltpu.VMEM
    late = 16 * (TILE * n_row - WIN * n_row)
    return dict(
        xw=v((4 * SLOT, D), BF),
        qkv=v((4 * SLOT, 3 * D), BF),
        probs0=v((2 * HEADS, 16 * WIN, SLOT), BF),
        probs1=v((2 * HEADS, late, SLOT), BF),
        mixed=v((4 * SLOT, D), BF),
        table=v((256, 128), BF),
        ret=v((FIELD, D), BF),
    )


def mlp_buffers(hidden):
    v = pltpu.VMEM
    return dict(
        mixed_own=v((TOK, D), BF),
        attended=v((TOK, D), BF),
        n2=v((TOK, D), BF),
        acc=v((TOK, D), F32),
        up_bias=v((hidden // D, D), F32),
        up_sum=v((1, hidden), F32),
        grad_middle=v((TOK, D), F32),
    )


def block_call(n_row, n_col, shapes, tensors, shards):
    hidden = shapes[2][0]
    sd, v = jax.ShapeDtypeStruct, pltpu.VMEM
    blocks = blocks_of(shapes)
    ins = {k: (t, vmem()) for k, t in tensors.items()}
    ins |= {"s" + str(i): (w, vmem()) for i, w in enumerate(shards)}
    outs = dict(
        output=(sd((TOK, D), BF), vmem()),
        input_grad=(sd((TOK, D), BF), vmem()),
        small=(sd((16, D), F32), vmem()),
        mid=(sd((24, D), F32), vmem()),
        late=(sd((8, D), F32), vmem()),
    )
    outs |= {"o" + str(i): (sd(b, F32), vmem()) for i, b in enumerate(blocks)}
    wqkv, wproj, w1, w2 = [v(s, BF) for s in shapes]
    come = [v((15 * b, h), BF) for b, h in blocks]
    field = v((FIELD, D), BF)
    scratch = dict(
        **window_buffers(n_row),
        **mlp_buffers(hidden),
        wqkv=wqkv,
        wproj=wproj,
        w1=w1,
        w2=w2,
        gqkv=wqkv,
        gproj=wproj,
        g1=w1,
        g2=w2,
        c0=come[0],
        c1=come[1],
        c2=come[2],
        c3=come[3],
        field=field,
        home=field,
        picked=v((PICKED, D), BF),
        gtab=v((2, 128, 128), F32),
        small_come=v((7, 16, D), F32),
        mid_come=v((7, 24, D), F32),
        late_come=v((7, 8, D), F32),
        local_sem=dma(len(GATHERS)),
        gather_sem=dma(2, len(GATHERS), Gather.SEMS),
        lend_sem=dma(4, 3),
        give_sem=dma(4, 3),
        small_sem=dma(2, 7),
        mid_sem=dma(2, 7),
        late_sem=dma(2, 7),
        free_sem=pltpu.SemaphoreType.REGULAR((2,)),
    )
    for i in range(4):
        scratch |= {"t" + str(i): dma(Reduce.SEMS), "u" + str(i): dma(Reduce.SEMS)}
    return named_call(
        functools.partial(block_body, n_row, n_col, shapes, hidden), ins, outs, scratch, "block",
        vmem_limit_bytes=63 * MIB, collective_id=0, has_side_effects=True,
    )


def plain_block(n_row, n_col, shapes, tensors, weights, field):
    hidden = shapes[2][0]
    sd, v = jax.ShapeDtypeStruct, pltpu.VMEM
    wqkv, wproj, w1, w2 = [(w, vmem()) for w in weights]
    limit = dict(vmem_limit_bytes=60 * MIB)

    def given(value, *names):
        return {k: (getattr(value, k), vmem()) for k in names}

    names = ("query_bias", "value_bias", "rel_rows", "rel_cols", "masks", "places", "marks")
    windows = window_buffers(n_row)
    outs = {k: as_out(windows.pop(k)) for k in ("qkv", "xw", "probs0", "probs1", "ret")}

    def attend_body(r):
        prepare(r)
        for w in range(4):
            cut_windows(r.field, r.xw, n_row, n_col, w)
        attend_part(r, n_row, n_col, (), lambda part: None)

    ins = split_ins(tensors, *names) | dict(field=(field, vmem()), wqkv=wqkv)
    one = named_call(attend_body, ins, outs, windows, "attend", **limit)
    home = (return_xla(one.ret, n_row, n_col), vmem())
    names = ("tokens", "cot", "proj_bias", "ln2_gain", "ln2_bias", "fc1_bias", "fc2_bias")
    buffers = mlp_buffers(hidden)
    outs = dict(grad_middle=as_out(buffers.pop("grad_middle")), gfield=(sd((FIELD, D), BF), vmem()))
    outs |= {k: (sd(s, BF), vmem()) for k, s in zip(("gproj", "g1", "g2"), shapes[1:])}
    outs |= dict(output=(sd((TOK, D), BF), vmem()), small=(sd((16, D), F32), vmem()))
    wide = (TOK, hidden)
    buffers |= dict(act=v(wide, BF), slope=v(wide, BF), gu=v(wide, BF), cot_t=v((D, TOK), BF))

    def mlp_body(r):
        r.gfield[...] = jnp.zeros_like(r.gfield)
        mlp_first(r, n_row, n_col, hidden, lambda: None, ())
        mlp_second(r, hidden, lambda part: None)
        up_weights(r, hidden, lambda j: None)
        mlp_branch(r, hidden)
        down_weights(r, lambda j: None)
        mlp_out(r)
        proj_weight_grad(r)

    ins = split_ins(tensors, *names) | dict(home=home, wproj=wproj, w1=w1, w2=w2)
    two = named_call(mlp_body, ins, outs, buffers, "mlp", **limit)
    gfield = (lend_xla(two.gfield[:TOK], n_row, n_col), vmem())
    ins = split_ins(tensors, "rel_rows", "rel_cols", "masks", "places_back", "marks_back")
    ins |= given(one, "qkv", "xw", "probs0", "probs1") | dict(wqkv=wqkv, wproj=wproj, gfield=gfield)
    outs = dict(
        gqkv=(sd(shapes[0], BF), vmem()),
        ret=(sd((FIELD, D), BF), vmem()),
        mid=(sd((24, D), F32), vmem()),
    )
    rows = v((4 * SLOT, D), BF)
    scratch = dict(gw=rows, gmix=rows, dqkv=v((12 * SLOT, D), BF))
    scratch |= dict(table=v((256, 128), BF), gtab=v((2, 128, 128), F32))

    def windows_body(r):
        back_prepare(r, n_row, n_col)
        back_mix(r)
        back_windows(r, n_row, n_col, ())
        back_weights(r, n_row, n_col, lambda n: None)
        back_return(r, n_row, n_col, lambda w: None)

    three = named_call(windows_body, ins, outs, scratch, "windows", **limit)
    home = (return_xla(three.ret, n_row, n_col), vmem())
    ins = split_ins(tensors, "tokens", "ln1_gain", "ln1_bias") | dict(home2=home) | given(two, "grad_middle")
    outs = dict(input_grad=(sd((TOK, D), BF), vmem()), late=(sd((8, D), F32), vmem()))
    four = named_call(lambda r: back_last(r, n_row, n_col), ins, outs, dict(acc=v((TOK, D), F32)), "ends", **limit)
    grads = []
    for g in (three.gqkv, two.gproj, two.g1, two.g2):
        g = lax.psum_scatter(g, AXES, scatter_dimension=0, tiled=True)
        grads.append(lax.psum_scatter(g, "dp", scatter_dimension=1, tiled=True))
    line = jnp.arange(16)[:, None] == 12
    local = lax.psum(two.small, AXES)
    small = jnp.where(line, local, lax.psum(jnp.where(line, 0.0, local), "dp"))
    mid, late = (lax.psum(v, ("dp", *AXES)) for v in (three.mid, four.late))
    return grads, two.output, four.input_grad, small, mid, late


def last_body(count, r):
    for i in range(4):
        r.__dict__["t" + str(i)][...] = r.__dict__["s" + str(i)][...].astype(F32)
    r.output_out[...] = r.output[...]
    r.input_grad_out[...] = r.input_grad[...]
    lines = ((r.late, 0), (r.late, 1), (r.mid, 16), (r.mid, 17), (r.small, 4), (r.small, 5), (r.small, 6), (r.small, 7))
    for i, (ref, line) in enumerate(lines):
        r.__dict__["v" + str(i)][...] = ref[line : line + 1, :].reshape(D)
    r.up[...] = jnp.concatenate([r.small[8 + i : 9 + i, :] for i in range(r.up.shape[0] // D)], 1).reshape(-1)
    tables = jnp.concatenate([r.mid[0:16, 128 * t : 128 * t + 128] for t in range(4)], 0)
    tables = tables[:, :HEAD] + pltpu.roll(tables, HEAD, 1)[:, :HEAD]
    r.rows[...] = tables[0 : 2 * WIN - 1, :]
    r.cols[...] = tables[32 : 32 + 2 * WIN - 1, :]
    r.stats[...] = jnp.sqrt(r.small[12:13, :5] / count)


def last_call(count, hidden, sums, output, input_grad, small, mid, late):
    sd = jax.ShapeDtypeStruct
    ins = {"s" + str(i): (s, vmem()) for i, s in enumerate(sums)}
    ins |= dict(output=(output, vmem()), input_grad=(input_grad, vmem()), small=(small, vmem()))
    ins |= dict(mid=(mid, vmem()), late=(late, vmem()))
    outs = {"t" + str(i): (sd(s.shape, F32), vmem()) for i, s in enumerate(sums)}
    outs |= dict(output_out=(sd((TOK, D), BF), vmem()), input_grad_out=(sd((TOK, D), BF), vmem()))
    outs |= {"v" + str(i): (sd((D,), F32), vmem()) for i in range(8)}
    outs |= dict(
        up=(sd((hidden,), F32), vmem()),
        rows=(sd((2 * WIN - 1, HEAD), F32), vmem()),
        cols=(sd((2 * WIN - 1, HEAD), F32), vmem()),
        stats=(sd((1, 5), F32), vmem()),
    )
    return named_call(functools.partial(last_body, count), ins, outs, {}, "last", vmem_limit_bytes=63 * MIB)


def on_device(
    n_dp, n_row, n_col,
    tokens, ln1_gain, ln1_bias, qkv_weight, query_bias, value_bias, rel_rows, rel_cols,
    proj_weight, proj_bias, ln2_gain, ln2_bias, fc1_weight, fc1_bias, fc2_weight, fc2_bias, cotangent,
):
    direct = (n_dp, n_row, n_col) == (2, 4, 4)
    tok = tokens.reshape(TOK, D)
    mask_values = np.zeros((16, 128), np.float32)
    mask_values[0, :64] = 1.0
    mask_values[1, 64:] = 1.0
    shared = dict(
        tokens=tok,
        cot=cotangent.reshape(TOK, D),
        ln1_gain=ln1_gain,
        ln1_bias=ln1_bias,
        rel_rows=rel_rows,
        rel_cols=rel_cols,
        masks=jnp.asarray(mask_values, BF),
    )
    tensors = shared | dict(
        query_bias=query_bias,
        value_bias=value_bias,
        proj_bias=proj_bias,
        ln2_gain=ln2_gain,
        ln2_bias=ln2_bias,
        fc1_bias=fc1_bias,
        fc2_bias=fc2_bias,
        places=jnp.asarray(table_places(False), BF),
        marks=jnp.asarray(key_marks(False), BF),
        places_back=jnp.asarray(table_places(True), BF),
        marks_back=jnp.asarray(key_marks(True), BF),
    )
    shards = (qkv_weight, proj_weight, fc1_weight, fc2_weight)
    shapes = [(s.shape[1] * n_row * n_col, s.shape[0] * n_dp) for s in shards]
    if direct:
        tensors |= dict(pick=jnp.asarray(pick_rows(), BF))
        done = block_call(n_row, n_col, shapes, tensors, [s.T for s in shards])
        sums = (done.o0, done.o1, done.o2, done.o3)
        rest = (done.output, done.input_grad, done.small, done.mid, done.late)
    else:
        weights = []
        for s in shards:
            s = lax.all_gather(s, AXES, axis=1, tiled=True)
            weights.append(lax.all_gather(s, "dp", axis=0, tiled=True).T)
        normed = norm(tok.astype(F32), ln1_gain.astype(F32), ln1_bias.astype(F32))[0].astype(BF)
        field = lend_xla(normed, n_row, n_col)
        sums, *rest = plain_block(n_row, n_col, shapes, tensors, weights, field)
    out = last_call(TOK * n_row * n_col * D, shapes[2][0], sums, *rest)
    return (
        out.output_out.reshape(tokens.shape),
        out.input_grad_out.reshape(tokens.shape),
        out.v0,
        out.v1,
        out.t0.T,
        out.v2,
        out.v3,
        out.rows,
        out.cols,
        out.t1.T,
        out.v4,
        out.v5,
        out.v6,
        out.t2.T,
        out.up,
        out.t3.T,
        out.v7,
        out.stats,
    )


def solution(mesh):
    tile = P("dp", "row", "col", None)
    weight = P("dp", AXES)
    sizes = [mesh.shape[a] for a in ("dp", "row", "col")]
    ins = [tile] + [P()] * 16
    for i in (3, 8, 12, 14):
        ins[i] = weight
    ins[16] = tile
    outs = [tile, tile] + [P()] * 16
    for i in (4, 9, 13, 15):
        outs[i] = weight
    outs[17] = P("dp", None)
    return jax.shard_map(
        functools.partial(on_device, *sizes),
        mesh=mesh,
        in_specs=tuple(ins),
        out_specs=tuple(outs),
        check_vma=False,
    )
```

time: 214 us -> 197 us (0.921)
  Pallas kernels: 207 us -> 196 us
  local copies, waits for them, and re-layouts: 5.63 us -> 0 us
    pallas_call x3 -> x2, Pallas kernels: 207 us -> 196 us  [named_call(): pl.pallas_call(kernel, name=name, out_shape=[shape for shape, _ in outs.v...]
    unnamed x14 -> x0, local copies, waits for them, and re-layouts: 5.63 us -> none
where the time goes in v3:
time: 197 us
  Pallas kernels  196 us (99%)
    pallas_call x2, Pallas kernels, named_call(): pl.pallas_call(kernel, name=name, out_shape=[shape for shape, _ in outs.v...  196 us

profile of v3, /device:TPU:0, one launch (start us, length us, event | category | flops | bytes accessed | tf_op | source)
XLA Modules:
  0.0 197.2 jit_solution(15456330811205737412)
XLA Ops:
  0.7 193.7 %block.1 = (bf16[256,768]{1,0:T(8,128)(2,1)}, bf16[256,768]{1,0:T(8,128)(2,1)}, f32[16,768]{1,0:T(8,128)}, f32[24,768]{1,0:T(8,128)}, f32[8,768]{1,0:T(8,128)}, ...) custom-call(bf16[256,768]{1,0:T(8,128)(2,1)} %bitcast.12, ...), custom_call_target="tpu_custom_call" | custom-call | tf_op jit(solution)/shard_map/block/pallas_call | solution.py:575
  194.4 2.7 %last.1 = (f32[144,384]{1,0:T(8,128)}, f32[48,384]{1,0:T(8,128)}, f32[192,384]{1,0:T(8,128)}, f32[48,1536]{1,0:T(8,128)}, bf16[256,768]{1,0:T(8,128)(2,1)}, /*in...) custom-call(f32[144,384]{1,0:T(8,128)} %get-tuple-element.45.refs_0_, ...), custom_call_target="tpu_custom_call" | custom-call | tf_op jit(solution)/shard_map/last/pallas_call | solution.py:575

commit v4 on v3

--- a/solution.py
+++ b/solution.py
@@ -248,10 +248,17 @@
         for copy, goes, _ in self.copies():
             pl.when(goes)(copy.start)
 
+    def arrive(self):
+        for copy, _, comes in self.copies():
+            pl.when(comes)(copy.wait_recv)
+
+    def gone(self):
+        for copy, goes, _ in self.copies():
+            pl.when(goes)(copy.wait_send)
+
     def wait(self):
-        for copy, goes, comes in self.copies():
-            pl.when(goes)(copy.wait_send)
-            pl.when(comes)(copy.wait_recv)
+        self.arrive()
+        self.gone()
 
 
 def pick_start(halo, pick):
@@ -901,8 +908,8 @@
         sent(n)
     ones = jnp.ones((16, 4 * SLOT), BF)
     r.mid[...] = jnp.zeros_like(r.mid)
-    r.mid[16:17, :] = nn(ones, r.dqkv[pl.ds(0, 4 * SLOT), :])[0:1, :]
-    r.mid[17:18, :] = nn(ones, r.dqkv[pl.ds(8 * SLOT, 4 * SLOT), :])[0:1, :]
+    r.mid[8:9, :] = nn(ones, r.dqkv[pl.ds(0, 4 * SLOT), :])[0:1, :]
+    r.mid[9:10, :] = nn(ones, r.dqkv[pl.ds(8 * SLOT, 4 * SLOT), :])[0:1, :]
     lane = lax.broadcasted_iota(jnp.int32, (128, 128), 1)
     left = jnp.where(lane < 64, r.gtab[0], 0.0)
     right = jnp.where(lane >= 64, r.gtab[1], 0.0)
@@ -913,8 +920,11 @@
         precision=lax.Precision.HIGHEST,
         preferred_element_type=F32,
     )
+    tab = tab + pltpu.roll(tab, HEAD, 1)
+    low = lax.broadcasted_iota(jnp.int32, (32, 128), 1) < HEAD
+    tab = jnp.where(low, tab[:32], tab[32:])
     for t in range(4):
-        r.mid[0:16, 128 * t : 128 * t + 128] = tab[16 * t : 16 * t + 16, :]
+        r.mid[0:8, 128 * t : 128 * t + 128] = tab[8 * t : 8 * t + 8, :]
 
 
 def back_return(r, n_row, n_col, between):
@@ -985,7 +995,7 @@
             self.start(s + 1)
 
 
-GATHERS = ((0, 0, 1), (1, 0, 1), (2, 0, 1), *((3, part, PARTS) for part in range(PARTS)))
+GATHERS = ((0, 0, 1), (1, 0, 1), *((i, part, PARTS) for i in (2, 3) for part in range(PARTS)))
 
 
 def block_body(n_row, n_col, shapes, hidden, r):
@@ -1001,7 +1011,8 @@
         Gather(fulls[i], shards[i], *blocks[i], r.gather_sem.at[0, n], r.gather_sem.at[1, n], part, parts)
         for n, (i, part, parts) in enumerate(GATHERS)
     ]
-    qkv_way, proj_way, up_way, *down_ways = gathers
+    qkv_way, proj_way = gathers[:2]
+    up_ways, down_ways = gathers[2 : 2 + PARTS], gathers[2 + PARTS :]
     qkv_way.start(LINE, OWN, OWN_CORE)
     gain, bias = vector(r.ln1_gain), vector(r.ln1_bias)
 
@@ -1029,7 +1040,8 @@
         mine.wait()
     qkv_way.step(0)
     proj_way.start(LINE)
-    up_way.start(LINE)
+    for way in up_ways:
+        way.start(LINE)
     lend.wait()
     for w in range(4):
         cut_windows(r.field, r.xw, n_row, n_col, w)
@@ -1041,25 +1053,33 @@
 
     def between(part):
         if part == 0:
+            up_ways[0].step(0)
+        elif part == 1:
             proj_way.step(0)
+        else:
+            up_ways[1].step(0)
 
     hooks = (
-        (3, lambda: up_way.step(0)),
-        (4, lambda: proj_way.step(1)),
+        (2, lambda: up_ways[2].step(0)),
+        (4, lambda: up_ways[0].step(1)),
+        (5, lambda: proj_way.step(1)),
         (8, lambda: down_ways[0].step(0)),
-        (11, lambda: down_ways[1].step(0)),
-        (14, lambda: up_way.step(1)),
+        (10, lambda: up_ways[1].step(1)),
+        (12, lambda: down_ways[1].step(0)),
+        (14, lambda: up_ways[2].step(1)),
         (16, lambda: proj_way.step(2)),
+        (17, lambda: up_ways[0].step(2)),
         (18, lambda: down_ways[2].step(0)),
         (20, lambda: down_ways[0].step(1)),
+        (22, lambda: up_ways[1].step(2)),
     )
     attend_part(r, n_row, n_col, hooks, between)
     give.start()
     r.home[pl.ds(0, TOK), :] = r.ret[pl.ds(0, TOK), :]
     proj_way.whole()
-    up_way.step(2)
     down_ways[1].step(1)
-    give.wait()
+    up_ways[2].step(2)
+    give.arrive()
 
     qkv_sum, proj_sum, up_sum, down_sum = sums = [
         Reduce(g, g, dp * blocks[i][1], land, c, *blocks[i], pieces, parts, p, q)
@@ -1084,10 +1104,12 @@
         m = types.SimpleNamespace(**r.__dict__, act=act, slope=slope, gu=gu, cot_t=cot_t)
 
         def arrived():
-            down_ways[2].step(1)
-            up_way.whole()
+            for way in up_ways:
+                way.whole()
+            give.gone()
 
         hooks = (
+            (1, lambda: down_ways[2].step(1)),
             (2, lambda: down_ways[0].step(2)),
             (6, lambda: down_ways[1].step(2)),
             (11, lambda: down_ways[2].step(2)),
@@ -1130,14 +1152,14 @@
         early.step(0)
         hooks = (
             (2, lambda: all_parts(down_sum, 1)),
-            (9, lambda: all_parts(up_sum, 2)),
-            (10, lambda: proj_sum.step(1)),
-            (20, lambda: all_parts(down_sum, 2)),
+            (12, lambda: all_parts(up_sum, 2)),
+            (13, lambda: proj_sum.step(1)),
         )
         back_windows(e, n_row, n_col, hooks)
         back_return(e, n_row, n_col, lambda n: None)
         give2.start()
         r.home2[pl.ds(0, TOK), :] = r.ret[pl.ds(0, TOK), :]
+        all_parts(down_sum, 2)
         early.step(1)
         back_weights(e, n_row, n_col, lambda n: qkv_sum.start(0, n))
         mid.start()
@@ -1147,23 +1169,19 @@
         late.start()
         qkv_sum.step(0)
         early.step(2)
+        for part in range(PARTS):
+            up_sum.result(r.o2, part)
+        all_parts(qkv_sum, 1)
         mid.step(0)
         late.step(0)
         for part in range(PARTS):
-            up_sum.result(r.o2, part)
-        qkv_sum.step(1, 0)
-        qkv_sum.step(1, 1)
+            down_sum.result(r.o3, part)
+        proj_sum.result(r.o1)
+        all_parts(qkv_sum, 2)
         mid.step(1)
         late.step(1)
-        qkv_sum.step(1, 2)
-        for part in range(PARTS):
-            down_sum.result(r.o3, part)
-        proj_sum.result(r.o1)
-        qkv_sum.step(2, 0)
         mid.step(2)
         late.step(2)
-        qkv_sum.step(2, 1)
-        qkv_sum.step(2, 2)
         for part in range(PARTS):
             qkv_sum.result(r.o0, part)
         for way in (qkv_sum, proj_sum, down_sum):
@@ -1219,7 +1237,7 @@
         output=(sd((TOK, D), BF), vmem()),
         input_grad=(sd((TOK, D), BF), vmem()),
         small=(sd((16, D), F32), vmem()),
-        mid=(sd((24, D), F32), vmem()),
+        mid=(sd((16, D), F32), vmem()),
         late=(sd((8, D), F32), vmem()),
     )
     outs |= {"o" + str(i): (sd(b, F32), vmem()) for i, b in enumerate(blocks)}
@@ -1246,7 +1264,7 @@
         picked=v((PICKED, D), BF),
         gtab=v((2, 128, 128), F32),
         small_come=v((7, 16, D), F32),
-        mid_come=v((7, 24, D), F32),
+        mid_come=v((7, 16, D), F32),
         late_come=v((7, 8, D), F32),
         local_sem=dma(len(GATHERS)),
         gather_sem=dma(2, len(GATHERS), Gather.SEMS),
@@ -1313,7 +1331,7 @@
     outs = dict(
         gqkv=(sd(shapes[0], BF), vmem()),
         ret=(sd((FIELD, D), BF), vmem()),
-        mid=(sd((24, D), F32), vmem()),
+        mid=(sd((16, D), F32), vmem()),
     )
     rows = v((4 * SLOT, D), BF)
     scratch = dict(gw=rows, gmix=rows, dqkv=v((12 * SLOT, D), BF))
@@ -1347,14 +1365,13 @@
         r.__dict__["t" + str(i)][...] = r.__dict__["s" + str(i)][...].astype(F32)
     r.output_out[...] = r.output[...]
     r.input_grad_out[...] = r.input_grad[...]
-    lines = ((r.late, 0), (r.late, 1), (r.mid, 16), (r.mid, 17), (r.small, 4), (r.small, 5), (r.small, 6), (r.small, 7))
+    lines = ((r.late, 0), (r.late, 1), (r.mid, 8), (r.mid, 9), (r.small, 4), (r.small, 5), (r.small, 6), (r.small, 7))
     for i, (ref, line) in enumerate(lines):
         r.__dict__["v" + str(i)][...] = ref[line : line + 1, :].reshape(D)
     r.up[...] = jnp.concatenate([r.small[8 + i : 9 + i, :] for i in range(r.up.shape[0] // D)], 1).reshape(-1)
-    tables = jnp.concatenate([r.mid[0:16, 128 * t : 128 * t + 128] for t in range(4)], 0)
-    tables = tables[:, :HEAD] + pltpu.roll(tables, HEAD, 1)[:, :HEAD]
-    r.rows[...] = tables[0 : 2 * WIN - 1, :]
-    r.cols[...] = tables[32 : 32 + 2 * WIN - 1, :]
+    tables = jnp.concatenate([r.mid[0:8, 128 * t : 128 * t + 128] for t in range(4)], 0)
+    r.rows[...] = tables[0 : 2 * WIN - 1, :HEAD]
+    r.cols[...] = pltpu.roll(tables, HEAD, 1)[0 : 2 * WIN - 1, :HEAD]
     r.stats[...] = jnp.sqrt(r.small[12:13, :5] / count)
 
 

time: 197 us -> 187 us (0.949)
  Pallas kernels: 196 us -> 186 us
    pallas_call x2, Pallas kernels: 196 us -> 186 us  [named_call(): pl.pallas_call(kernel, name=name, out_shape=[shape for shape, _ in outs.v...]
where the time goes in v4:
time: 187 us
  Pallas kernels  186 us (99%)
    pallas_call x2, Pallas kernels, named_call(): pl.pallas_call(kernel, name=name, out_shape=[shape for shape, _ in outs.v...  186 us

profile of v4, /device:TPU:0, one launch (start us, length us, event | category | flops | bytes accessed | tf_op | source)
XLA Modules:
  0.0 186.9 jit_solution(6109601740388904903)
XLA Ops:
  0.7 183.4 %block.1 = (bf16[256,768]{1,0:T(8,128)(2,1)}, bf16[256,768]{1,0:T(8,128)(2,1)}, f32[16,768]{1,0:T(8,128)}, f32[16,768]{1,0:T(8,128)}, f32[8,768]{1,0:T(8,128)}, ...) custom-call(bf16[256,768]{1,0:T(8,128)(2,1)} %bitcast.12, ...), custom_call_target="tpu_custom_call" | custom-call | tf_op jit(solution)/shard_map/block/pallas_call | solution.py:582
  184.1 2.7 %last.1 = (f32[144,384]{1,0:T(8,128)}, f32[48,384]{1,0:T(8,128)}, f32[192,384]{1,0:T(8,128)}, f32[48,1536]{1,0:T(8,128)}, bf16[256,768]{1,0:T(8,128)(2,1)}, /*in...) custom-call(f32[144,384]{1,0:T(8,128)} %get-tuple-element.45.refs_0_, ...), custom_call_target="tpu_custom_call" | custom-call | tf_op jit(solution)/shard_map/last/pallas_call | solution.py:582
